TPU v7x, 1024 devices: a whole 4x8x16 slice. The times are simulated.
1024 devices in a mesh: segment: 16 (over z), dp: 64 (over x, y, core).
Axes of the slice: x: 4, y: 8, z: 16, core: 2. Of those that a mesh axis runs over, the one named last changes fastest.
Arguments:
- activations: bfloat16 [16, 2, 4, 256, 32, 128], P('segment', None, None, 'dp'), may hold values from -6 to 6
- pre_norm: bfloat16 [16, 2, 4, 256, 32, 128], P('segment', None, None, 'dp'), may hold values from -6 to 6
- cot_first: bfloat16 [16, 4, 256, 32, 128], P('segment', None, 'dp'), may hold values from -6 to 6
- loss_grad: bfloat16 [1, 4, 256, 32, 128], P(None, None, 'dp'), may hold values from -6 to 6
- frame_clip: int32 [16, 2, 64, 4], P('segment', None, 'dp'), may hold values from 0 to 4, as said below
- weight: bfloat16 [16, 3456, 128], P('segment'), may hold values from -0.109375 to 0.109375
- norm_gain: float32 [16, 128], P('segment'), may hold values from 0.5 to 2
- norm_shift: float32 [16, 128], P('segment'), may hold values from -3 to 3
Outputs:
- grad_inputs: bfloat16 [16, 2, 4, 256, 32, 128], P('segment', None, None, 'dp')
- grad_weight: float32 [16, 3456, 128], P('segment', 'dp')
- grad_gain: float32 [16, 128], P('segment', 'dp')
- grad_shift: float32 [16, 128], P('segment', 'dp')
Inputs may be any that keep to these rules, and one draw needn't show every extreme that they name: `frame_clip`: for every section and turn the lists of all dp indices are equal. Each list starts with 0, live slots come first, their clip numbers never fall and rise by at most one from slot to slot, padding slots at the end carry 4; at least 2 slots are live.
All inputs are finite; a program needn't handle non-finite values.
Results may differ from a plain program's by a relative error of at most 0.0053.
Values may be sent and summed in bfloat16 or wider, within the bound.
No kernel may reach another device: no remote copies, remote signals or barrier semaphores. Data moves between devices by JAX's collectives and lax.ppermute only.
A program may use at most 32 MiB of HBM per device.

v0:
```python
import jax
import jax.numpy as jnp
from jax import lax
from jax.sharding import PartitionSpec as P

NORM_GROUPS = 32
TAPS = 27
TURNS = 2


epsilon = 1e-05


def shifted(x, axis, by):
    count = lax.axis_size(axis)
    pairs = [(i, i + by) for i in range(count) if 0 <= i + by < count]
    return lax.ppermute(x, axis, pairs)


def extended(cells, sides, width):
    for axis, dim in sides:
        count = lax.axis_size(axis)
        ends = count - 1
        head = lax.slice_in_dim(cells, 0, width, axis=dim)
        tail = lax.slice_in_dim(cells, cells.shape[dim] - width, cells.shape[dim], axis=dim)
        cells = jnp.concatenate(
            [
                lax.ppermute(tail, axis, [(i, (i + 1) % count) for i in range(ends)]),
                cells,
                lax.ppermute(head, axis, [((i + 1) % count, i) for i in range(ends)]),
            ],
            axis=dim,
        )
    return cells


def local(activations, pre_norm, cot_first, loss_grad, frame_clip, weight, norm_gain, norm_shift):
    segment_index = lax.axis_index("segment")
    segment_last = lax.axis_size("segment") - 1
    dp_index = lax.axis_index("dp")
    strips = lax.axis_size("dp")
    strip_index = dp_index % strips
    group_index = dp_index // strips
    group_count = lax.axis_size("dp") // strips
    frames = activations.shape[2]
    strip_rows = activations.shape[3]
    frame_cols = activations.shape[4]
    channels = activations.shape[5]
    per_group = channels // NORM_GROUPS
    taps_weight = weight[0].reshape(TAPS, channels, channels)
    gain = norm_gain[0]
    shift_vec = norm_shift[0]
    clip_range = jnp.arange(frames, dtype=jnp.int32)
    group_pick = (jnp.arange(group_count, dtype=jnp.int32) == group_index).astype(jnp.float32)
    cells = float(strips * strip_rows * frame_cols * per_group)
    row_mark = jnp.arange(strip_rows + 2, dtype=jnp.int32)
    keep_rows = jnp.logical_not(
        (row_mark == 0) & (strip_index == 0)
        | (row_mark == strip_rows + 1) & (strip_index == strips - 1)
    )
    zero_value = jnp.zeros((), jnp.bfloat16)
    results = []
    sums = None
    previous = None
    for turn_index in range(TURNS):
        if turn_index == 0:
            incoming = cot_first[0]
        else:
            handed = shifted(previous, "segment", -1)
            incoming = jnp.where(segment_index == segment_last, loss_grad[turn_index - 1], handed)
        clips = frame_clip[0, turn_index, 0]
        live = clips < frames
        onehot = (clips[:, None] == clip_range[None, :]).astype(jnp.float32)
        count = jnp.maximum(jnp.sum(onehot, axis=0) * cells, 1.0)[:, None]

        def to_clips(values):
            return jnp.einsum("fc,fk->ck", onehot, values, precision=lax.Precision.HIGHEST)

        def spread(table):
            return group_pick[:, None, None] * table[None]

        def own_rows(table):
            return lax.dynamic_index_in_dim(table, group_index, 0, keepdims=False)

        def per_frame(values):
            framed = jnp.einsum("fc,ck->fk", onehot, values, precision=lax.Precision.HIGHEST)
            return framed[:, None, :, None]

        pre = (
            pre_norm[0, turn_index]
            .astype(jnp.float32)
            .reshape(frames, strip_rows * frame_cols, NORM_GROUPS, per_group)
        )
        first = to_clips(jnp.sum(pre, axis=(1, 3)))
        second = to_clips(jnp.sum(pre * pre, axis=(1, 3)))
        stat_tables = lax.psum((spread(first), spread(second)), "dp")
        first_total = own_rows(stat_tables[0])
        second_total = own_rows(stat_tables[1])
        mean_clip = first_total / count
        var_clip = second_total / count - mean_clip * mean_clip
        rstd_clip = 1.0 / jnp.sqrt(var_clip + epsilon)
        rstd_frame = per_frame(rstd_clip)
        normed = (pre - per_frame(mean_clip)) * rstd_frame
        gain_grid = gain.reshape(NORM_GROUPS, per_group)
        shift_grid = shift_vec.reshape(NORM_GROUPS, per_group)
        act = normed * gain_grid + shift_grid
        sigm = jax.nn.sigmoid(act)
        live_mask = live[:, None, None, None]
        upstream = incoming.astype(jnp.float32).reshape(pre.shape)
        grad_act = jnp.where(live_mask, upstream * sigm * (1.0 + act * (1.0 - sigm)), 0.0)
        gain_part = jnp.sum(grad_act * normed, axis=(0, 1)).reshape(channels)
        shift_part = jnp.sum(grad_act, axis=(0, 1)).reshape(channels)
        scaled = grad_act * gain_grid
        third = to_clips(jnp.sum(scaled, axis=(1, 3)))
        fourth = to_clips(jnp.sum(scaled * normed, axis=(1, 3)))
        grad_tables = lax.psum((spread(third), spread(fourth)), "dp")
        third_total = own_rows(grad_tables[0])
        fourth_total = own_rows(grad_tables[1])
        avg_a = per_frame(third_total / count)
        avg_b = per_frame(fourth_total / count)
        grad_pre = jnp.where(live_mask, rstd_frame * (scaled - avg_a - normed * avg_b), 0.0)
        grad_pre = grad_pre.astype(jnp.bfloat16).reshape(frames, strip_rows, frame_cols, channels)
        rimmed = extended(grad_pre, (("dp", 1),), 1)
        rimmed = jnp.where(keep_rows[None, :, None, None], rimmed, zero_value)
        padded = jnp.pad(rimmed, ((0, 2), (0, 0), (1, 1), (0, 0)))
        earlier = jnp.concatenate([jnp.full((2,), -1, jnp.int32), clips], axis=0)
        pieces = []
        for time_tap in range(3):
            pair_ok = live & (earlier[2 - time_tap : 2 - time_tap + frames] == clips)
            pair_pad = jnp.concatenate([pair_ok, jnp.zeros((2,), bool)], axis=0)
            masked = jnp.where(pair_pad[:, None, None, None], padded, zero_value)
            for row_tap in (-1, 0, 1):
                for col_tap in (-1, 0, 1):
                    pieces.append(
                        masked[
                            time_tap : time_tap + frames,
                            1 - row_tap : 1 - row_tap + strip_rows,
                            1 - col_tap : 1 - col_tap + frame_cols,
                        ]
                    )
        columns = jnp.stack(pieces, axis=3).reshape(-1, TAPS, channels)
        grad_in = jnp.einsum(
            "rko,kio->ri", columns, taps_weight, preferred_element_type=jnp.float32
        )
        previous = grad_in.astype(jnp.bfloat16).reshape(frames, strip_rows, frame_cols, channels)
        results.append(previous)
        rows_in = activations[0, turn_index].reshape(-1, channels)
        weight_part = jnp.einsum(
            "ri,rko->kio", rows_in, columns, preferred_element_type=jnp.float32
        ).reshape(TAPS * channels, channels)
        local_terms = (weight_part, gain_part, shift_part)
        sums = local_terms if sums is None else jax.tree.map(jnp.add, sums, local_terms)
    sums = (
        lax.psum_scatter(sums[0], "dp", scatter_dimension=0, tiled=True),
        lax.psum_scatter(sums[1], "dp", scatter_dimension=0, tiled=True),
        lax.psum_scatter(sums[2], "dp", scatter_dimension=0, tiled=True),
    )
    scale = 1.0 / lax.axis_size("dp")
    grad_inputs = jnp.stack(results, axis=0)[None]
    return (grad_inputs, (sums[0] * scale)[None], (sums[1] * scale)[None], (sums[2] * scale)[None])


def solution(mesh):
    in_specs = (
        P("segment", None, None, "dp", None, None),
        P("segment", None, None, "dp", None, None),
        P("segment", None, "dp", None, None),
        P(None, None, "dp", None, None),
        P("segment", None, "dp", None),
        P("segment", None, None),
        P("segment", None),
        P("segment", None),
    )
    out_specs = (
        P("segment", None, None, "dp", None, None),
        P("segment", "dp", None),
        P("segment", "dp"),
        P("segment", "dp"),
    )
    return jax.shard_map(local, mesh=mesh, in_specs=in_specs, out_specs=out_specs, check_vma=False)
```

profile of v0, /device:TPU:2, one launch (start us, length us, event | category | flops | bytes accessed | tf_op | source)
XLA Modules:
  0.0 607.9 jit_solution(11742169022652018414)
XLA Ops:
  0.7 0.8 broadcast_compare_fusion
  1.4 0.7 slice_bitcast_fusion.1
  2.2 1.1 fusion.14
  3.9 0.3 convolution_multiply_fusion.6
  4.1 0.3 convolution_multiply_fusion.3
  4.4 0.3 convolution_multiply_fusion.2
  5.1 107.6 %all-reduce.16 = (f32[4,32]{1,0:T(4,128)S(1)}, f32[4,32]{1,0:T(4,128)S(1)}) all-reduce(f32[4,32]{1,0:T(4,128)S(1)} %convolution_multiply_fusion.7, f32[4,32]{1,0:T(4,128)S(1)} %convolution_multiply_fusion.6), channel_id=1, replica_groups=mesh['segment'=16,'dp'=64] {'dp'}, use_global_device_ids=true, to_apply=%region_2.3 | all-reduce | flops 256 | bytes 2048 | tf_op jit(solution)/shard_map/psum | solution.py:96
  113.5 1.2 fusion.61
  114.9 0.3 convolution_multiply_fusion.4
  115.4 0.3 convolution_multiply_fusion.5
  115.7 119.5 %all-reduce.15 = (f32[4,32]{1,0:T(4,128)S(1)}, f32[4,32]{1,0:T(4,128)S(1)}, f32[4,32]{1,0:T(4,128)S(1)}, f32[4,32]{1,0:T(4,128)S(1)}) all-reduce(f32[4,32]{1,0:T(4,128)S(1)} %convolution_multiply_fusion.4, f32[4,32]{1,0:T(4,128)S(1)} %convolution_multiply_fusion.5, ...), channel_id=1, replica_groups=mesh['segment'=16,'dp'=64] {'dp'}, use_global_device_ids=true, to_apply=%region_12.13 | all-reduce | flops 512 | bytes 4096 | tf_op jit(solution)/shard_map/psum | solution.py:116
  236.0 1.2 fusion.11
  237.2 1.9 collective-permute-start
  239.2 7.0 %collective-permute-start.1 = (bf16[4,1,32,128]{3,2,1,0:T(8,128)(2,1)S(1)}, bf16[4,1,32,128]{3,2,1,0:T(8,128)(2,1)S(1)}, u32[]{:S(2)}, u32[]{:S(2)}) collective-permute-start(bf16[4,1,32,128]{3,2,1,0:T(8,128)(2,1)S(1)} %get-tuple-element.100), channel_id=1, source_target_pairs={{1,0},{2,1},{3,2},{4,3},{5,4},{6,5},{7,6},{8,7},{9,8},{10,9},{11,1... | collective-permute-start | bytes 98312 | tf_op jit(solution)/shard_map/ppermute | solution.py:30
  247.3 1.4 fusion.117
  250.5 0.4 fusion.111
  251.7 1.1 fusion.1
  252.9 1.4 collective-permute-start.2
  254.3 1.9 fusion.118
  256.2 3.6 collective-permute-done.2
  260.3 0.3 convolution_multiply_fusion
  260.8 0.3 convolution_multiply_fusion.1
  261.1 121.6 %all-reduce.14 = (f32[4,32]{1,0:T(4,128)S(1)}, f32[4,32]{1,0:T(4,128)S(1)}, f32[128]{0:T(128)S(1)}, f32[128]{0:T(128)S(1)}) all-reduce(f32[4,32]{1,0:T(4,128)S(1)} %convolution_multiply_fusion, f32[4,32]{1,0:T(4,128)S(1)} %convolution_multiply_fusion.1, f32[128]{0:T(128)S(1)} %add.173, ...), channel_id=1, replica_groups=mesh['segment'=16,'dp'=64] {'dp'}, use_global_device_ids=true, to_apply=%region_25.26 | all-reduce | flops 512 | bytes 4096 | tf_op jit(solution)/shard_map/psum | solution.py:116
  383.6 1.9 collective-permute-start.3
  385.5 6.8 %collective-permute-start.4 = (bf16[4,1,32,128]{3,2,1,0:T(8,128)(2,1)S(1)}, bf16[4,1,32,128]{3,2,1,0:T(8,128)(2,1)S(1)}, u32[]{:S(2)}, u32[]{:S(2)}) collective-permute-start(bf16[4,1,32,128]{3,2,1,0:T(8,128)(2,1)S(1)} %get-tuple-element.98), channel_id=1, source_target_pairs={{1,0},{2,1},{3,2},{4,3},{5,4},{6,5},{7,6},{8,7},{9,8},{10,9},{11,1... | collective-permute-start | bytes 98312 | tf_op jit(solution)/shard_map/ppermute | solution.py:30
  392.4 0.6 fusion.104
  392.9 0.6 fusion.103
  393.5 0.4 collective-permute-done.4
  395.5 0.7 copy-done.1
  396.3 0.7 convolution_add_fusion
  397.0 0.3 copy-done.2
  397.3 130.2 %fusion = f32[64,128]{1,0:T(8,128)S(1)} fusion(f32[3456,128]{1,0:T(8,128)S(1)} %bitcast.250), kind=kCustom, calls=%all-reduce-scatter | all-reduce-scatter fusion | flops 524289 | bytes 1806336
  527.5 1.9 collective-permute-start.13
  529.4 1.9 collective-permute-start.12
  531.4 1.9 collective-permute-start.11
  533.3 7.0 %collective-permute-start.10 = (f32[64,128]{1,0:T(8,128)S(1)}, f32[64,128]{1,0:T(8,128)S(1)}, u32[]{:S(2)}, u32[]{:S(2)}) collective-permute-start(f32[64,128]{1,0:T(8,128)S(1)} %fusion), channel_id=1, source_target_pairs={{0,6},{1,7},{2,8},{3,9},{4,10},{5,11},{6,12},{7,13},{8,14},{9,15},... | collective-permute-start | bytes 98312
  540.3 26.7 %collective-permute-start.14 = (f32[54,128]{1,0:T(8,128)S(1)}, f32[54,128]{1,0:T(8,128)S(1)}, u32[]{:S(2)}, u32[]{:S(2)}) collective-permute-start(f32[54,128]{1,0:T(8,128)S(1)} %slice.330), channel_id=1, source_target_pairs={{0,10},{1,11},{2,12},{3,13},{4,14},{5,15},{6,16},{7,17},{8,18},{9,... | collective-permute-start | bytes 82952
  567.1 3.1 fusion.2
  570.2 16.4 %collective-permute-start.9 = (f32[64,128]{1,0:T(8,128)S(1)}, f32[64,128]{1,0:T(8,128)S(1)}, u32[]{:S(2)}, u32[]{:S(2)}) collective-permute-start(f32[64,128]{1,0:T(8,128)S(1)} %fusion), channel_id=1, source_target_pairs={{0,5},{1,6},{2,7},{3,8},{4,9},{5,10},{6,11},{7,12},{8,13},{9,14},{... | collective-permute-start | bytes 98312
  586.6 1.9 collective-permute-start.8
  588.5 6.3 %collective-permute-start.7 = (f32[64,128]{1,0:T(8,128)S(1)}, f32[64,128]{1,0:T(8,128)S(1)}, u32[]{:S(2)}, u32[]{:S(2)}) collective-permute-start(f32[64,128]{1,0:T(8,128)S(1)} %fusion), channel_id=1, source_target_pairs={{0,3},{1,4},{2,5},{3,6},{4,7},{5,8},{6,9},{7,10},{8,11},{9,12},{10... | collective-permute-start | bytes 98312
  594.8 3.0 collective-permute-start.6
  597.9 2.7 collective-permute-start.5
  600.5 0.7 maximum_bitcast_fusion
  601.3 1.4 collective-permute-done.6
  602.7 2.9 collective-permute-done.5
  605.6 1.6 concatenate.42
  607.2 0.6 copy.21
  (150 shorter events, 8.3 us)
Async XLA Ops:
  0.6 251.1 %copy-start = (bf16[1,3456,128]{2,1,0:T(8,128)(2,1)S(1)}, bf16[1,3456,128]{2,1,0:T(8,128)(2,1)}, u32[]{:S(2)}) copy-start(bf16[1,3456,128]{2,1,0:T(8,128)(2,1)} %param.13) | copy-start | bytes 2654212
  0.6 246.1 %copy-start.4 = (bf16[1,2,4,4,32,128]{5,4,3,2,1,0:T(8,128)(2,1)S(1)}, bf16[1,2,4,4,32,128]{5,4,3,2,1,0:T(8,128)(2,1)}, u32[]{:S(2)}) copy-start(bf16[1,2,4,4,32,128]{5,4,3,2,1,0:T(8,128)(2,1)} %param.8) | copy-start | bytes 786436
  237.2 12.8 %collective-permute-start = (bf16[4,1,32,128]{3,2,1,0:T(8,128)(2,1)S(1)}, bf16[4,1,32,128]{3,2,1,0:T(8,128)(2,1)S(1)}, u32[]{:S(2)}, u32[]{:S(2)}) collective-permute-start(bf16[4,1,32,128]{3,2,1,0:T(8,128)(2,1)S(1)} %get-tuple-element.99), channel_id=1, source_target_pairs={{0,1},{1,2},{2,3},{3,4},{4,5},{5,6},{6,7},{7,8},{8,9},{9,10},{10,1... | collective-permute-start | bytes 98312 | tf_op jit(solution)/shard_map/ppermute | solution.py:28
  239.2 10.9 %collective-permute-start.1 = (bf16[4,1,32,128]{3,2,1,0:T(8,128)(2,1)S(1)}, bf16[4,1,32,128]{3,2,1,0:T(8,128)(2,1)S(1)}, u32[]{:S(2)}, u32[]{:S(2)}) collective-permute-start(bf16[4,1,32,128]{3,2,1,0:T(8,128)(2,1)S(1)} %get-tuple-element.100), channel_id=1, source_target_pairs={{1,0},{2,1},{3,2},{4,3},{5,4},{6,5},{7,6},{8,7},{9,8},{10,9},{11,1... | collective-permute-start | bytes 98312 | tf_op jit(solution)/shard_map/ppermute | solution.py:30
  252.8 7.0 %copy-start.3 = (bf16[1,2,4,4,32,128]{5,4,3,2,1,0:T(8,128)(2,1)S(1)}, bf16[1,2,4,4,32,128]{5,4,3,2,1,0:T(8,128)(2,1)}, u32[]{:S(2)}) copy-start(bf16[1,2,4,4,32,128]{5,4,3,2,1,0:T(8,128)(2,1)} %param.9) | copy-start | bytes 786436
  252.8 7.0 %copy-start.5 = (bf16[1,4,4,32,128]{4,3,2,1,0:T(8,128)(2,1)S(1)}, bf16[1,4,4,32,128]{4,3,2,1,0:T(8,128)(2,1)}, u32[]{:S(2)}) copy-start(bf16[1,4,4,32,128]{4,3,2,1,0:T(8,128)(2,1)} %param.11) | copy-start | bytes 393220
  252.8 7.0 %copy-start.6 = (f32[1,128]{1,0:T(1,128)S(1)}, f32[1,128]{1,0:T(1,128)}, u32[]{:S(2)}) copy-start(f32[1,128]{1,0:T(1,128)} %param.14) | copy-start | bytes 1540
  252.8 7.0 %copy-start.7 = (f32[1,128]{1,0:T(1,128)S(1)}, f32[1,128]{1,0:T(1,128)}, u32[]{:S(2)}) copy-start(f32[1,128]{1,0:T(1,128)} %param.15) | copy-start | bytes 1540
  252.9 7.0 %collective-permute-start.2 = (bf16[4,4,32,128]{3,2,1,0:T(8,128)(2,1)S(1)}, bf16[4,4,32,128]{3,2,1,0:T(8,128)(2,1)S(1)}, u32[]{:S(2)}, u32[]{:S(2)}) collective-permute-start(bf16[4,4,32,128]{3,2,1,0:T(8,128)(2,1)S(1)} %bitcast.307), channel_id=1, source_target_pairs={{64,0},{128,64},{192,128},{256,192},{320,256},{384,320},{448,384},... | collective-permute-start | bytes 393224 | tf_op jit(solution)/shard_map/ppermute | solution.py:17
  383.6 10.0 %collective-permute-start.3 = (bf16[4,1,32,128]{3,2,1,0:T(8,128)(2,1)S(1)}, bf16[4,1,32,128]{3,2,1,0:T(8,128)(2,1)S(1)}, u32[]{:S(2)}, u32[]{:S(2)}) collective-permute-start(bf16[4,1,32,128]{3,2,1,0:T(8,128)(2,1)S(1)} %get-tuple-element.97), channel_id=1, source_target_pairs={{0,1},{1,2},{2,3},{3,4},{4,5},{5,6},{6,7},{7,8},{8,9},{9,10},{10,1... | collective-permute-start | bytes 98312 | tf_op jit(solution)/shard_map/ppermute | solution.py:28
  385.5 8.4 %collective-permute-start.4 = (bf16[4,1,32,128]{3,2,1,0:T(8,128)(2,1)S(1)}, bf16[4,1,32,128]{3,2,1,0:T(8,128)(2,1)S(1)}, u32[]{:S(2)}, u32[]{:S(2)}) collective-permute-start(bf16[4,1,32,128]{3,2,1,0:T(8,128)(2,1)S(1)} %get-tuple-element.98), channel_id=1, source_target_pairs={{1,0},{2,1},{3,2},{4,3},{5,4},{6,5},{7,6},{8,7},{9,8},{10,9},{11,1... | collective-permute-start | bytes 98312 | tf_op jit(solution)/shard_map/ppermute | solution.py:30
  394.8 1.5 copy-start.1
  395.5 1.8 copy-start.2
  527.5 59.1 %collective-permute-start.13 = (f32[64,128]{1,0:T(8,128)S(1)}, f32[64,128]{1,0:T(8,128)S(1)}, u32[]{:S(2)}, u32[]{:S(2)}) collective-permute-start(f32[64,128]{1,0:T(8,128)S(1)} %fusion), channel_id=1, source_target_pairs={{0,9},{1,10},{2,11},{3,12},{4,13},{5,14},{6,15},{7,16},{8,17},{9,1... | collective-permute-start | bytes 98312
  529.4 59.1 %collective-permute-start.12 = (f32[64,128]{1,0:T(8,128)S(1)}, f32[64,128]{1,0:T(8,128)S(1)}, u32[]{:S(2)}, u32[]{:S(2)}) collective-permute-start(f32[64,128]{1,0:T(8,128)S(1)} %fusion), channel_id=1, source_target_pairs={{0,8},{1,9},{2,10},{3,11},{4,12},{5,13},{6,14},{7,15},{8,16},{9,17... | collective-permute-start | bytes 98312
  531.4 63.4 %collective-permute-start.11 = (f32[64,128]{1,0:T(8,128)S(1)}, f32[64,128]{1,0:T(8,128)S(1)}, u32[]{:S(2)}, u32[]{:S(2)}) collective-permute-start(f32[64,128]{1,0:T(8,128)S(1)} %fusion), channel_id=1, source_target_pairs={{0,7},{1,8},{2,9},{3,10},{4,11},{5,12},{6,13},{7,14},{8,15},{9,16}... | collective-permute-start | bytes 98312
  533.3 64.5 %collective-permute-start.10 = (f32[64,128]{1,0:T(8,128)S(1)}, f32[64,128]{1,0:T(8,128)S(1)}, u32[]{:S(2)}, u32[]{:S(2)}) collective-permute-start(f32[64,128]{1,0:T(8,128)S(1)} %fusion), channel_id=1, source_target_pairs={{0,6},{1,7},{2,8},{3,9},{4,10},{5,11},{6,12},{7,13},{8,14},{9,15},... | collective-permute-start | bytes 98312
  540.3 29.8 %collective-permute-start.14 = (f32[54,128]{1,0:T(8,128)S(1)}, f32[54,128]{1,0:T(8,128)S(1)}, u32[]{:S(2)}, u32[]{:S(2)}) collective-permute-start(f32[54,128]{1,0:T(8,128)S(1)} %slice.330), channel_id=1, source_target_pairs={{0,10},{1,11},{2,12},{3,13},{4,14},{5,15},{6,16},{7,17},{8,18},{9,... | collective-permute-start | bytes 82952
  570.2 31.1 %collective-permute-start.9 = (f32[64,128]{1,0:T(8,128)S(1)}, f32[64,128]{1,0:T(8,128)S(1)}, u32[]{:S(2)}, u32[]{:S(2)}) collective-permute-start(f32[64,128]{1,0:T(8,128)S(1)} %fusion), channel_id=1, source_target_pairs={{0,5},{1,6},{2,7},{3,8},{4,9},{5,10},{6,11},{7,12},{8,13},{9,14},{... | collective-permute-start | bytes 98312
  586.6 14.7 %collective-permute-start.8 = (f32[64,128]{1,0:T(8,128)S(1)}, f32[64,128]{1,0:T(8,128)S(1)}, u32[]{:S(2)}, u32[]{:S(2)}) collective-permute-start(f32[64,128]{1,0:T(8,128)S(1)} %fusion), channel_id=1, source_target_pairs={{0,4},{1,5},{2,6},{3,7},{4,8},{5,9},{6,10},{7,11},{8,12},{9,13},{1... | collective-permute-start | bytes 98312
  588.5 12.8 %collective-permute-start.7 = (f32[64,128]{1,0:T(8,128)S(1)}, f32[64,128]{1,0:T(8,128)S(1)}, u32[]{:S(2)}, u32[]{:S(2)}) collective-permute-start(f32[64,128]{1,0:T(8,128)S(1)} %fusion), channel_id=1, source_target_pairs={{0,3},{1,4},{2,5},{3,6},{4,7},{5,8},{6,9},{7,10},{8,11},{9,12},{10... | collective-permute-start | bytes 98312
  594.8 7.9 %collective-permute-start.6 = (f32[64,128]{1,0:T(8,128)S(1)}, f32[64,128]{1,0:T(8,128)S(1)}, u32[]{:S(2)}, u32[]{:S(2)}) collective-permute-start(f32[64,128]{1,0:T(8,128)S(1)} %fusion), channel_id=1, source_target_pairs={{0,2},{1,3},{2,4},{3,5},{4,6},{5,7},{6,8},{7,9},{8,10},{9,11},{10,... | collective-permute-start | bytes 98312
  597.9 7.7 %collective-permute-start.5 = (f32[64,128]{1,0:T(8,128)S(1)}, f32[64,128]{1,0:T(8,128)S(1)}, u32[]{:S(2)}, u32[]{:S(2)}) collective-permute-start(f32[64,128]{1,0:T(8,128)S(1)} %fusion), channel_id=1, source_target_pairs={{0,1},{1,2},{2,3},{3,4},{4,5},{5,6},{6,7},{7,8},{8,9},{9,10},{10,1... | collective-permute-start | bytes 98312
where the time goes:
time: 609 us; the launch traced here: 608 us
  blocking collectives  479 us (79%)
  starting transfers between devices  88.9 us (15%)
  matrix products  10.4 us (2%)
  local copies, waits for them, and re-layouts  10.2 us (2%)
  waiting for transfers between devices  8.35 us (1%)
  other arithmetic  8.19 us (1%)
    psum x2, blocking collectives, local(): grad_tables = lax.psum((spread(third), spread(fourth)), 'dp')  241 us
    unnamed x1, blocking collectives  130 us
    psum x1, blocking collectives, local(): stat_tables = lax.psum((spread(first), spread(second)), 'dp')  108 us
    unnamed x10, starting transfers between devices  69.8 us
    ppermute x2, starting transfers between devices, extended(): lax.ppermute(head, axis, [((i + 1) % count, i) for i in range(ends)])  13.8 us
  transfers between devices with their start and end apart: 15, of which 4 were waited for; matrix products, arithmetic and copies ran while one was open for 2% of the time, Pallas kernels for 0%

commit v1 on v0

v1 whole, which is shorter than its diff:
```python
import functools
import jax
import jax.numpy as jnp
from jax import lax
from jax.experimental import pallas as pl
from jax.experimental.pallas import tpu as pltpu
from jax.sharding import PartitionSpec as P

F32, BF16 = jnp.float32, jnp.bfloat16
FRAMES, ROWS, COLS, CH = 4, 4, 32, 128
GROUPS, PER = 32, 4
TAPS = 27
EPS = 1e-05
VMEM = pl.BlockSpec(memory_space=pltpu.VMEM)
SMEM = pl.BlockSpec(memory_space=pltpu.SMEM)


def exact_dot(a, b):
    return jnp.dot(a, b, precision=lax.Precision.HIGHEST, preferred_element_type=F32)


def iota(dim, shape=(CH, CH)):
    return lax.broadcasted_iota(jnp.int32, shape, dim)


def pack_rows(per_frame):
    total = None
    for f in range(FRAMES):
        place = (iota(1) == f * GROUPS + (iota(0) >> 2)).astype(F32)
        term = exact_dot(per_frame[f], place)
        total = term if total is None else total + term
    return total


def unpack_rows(table, clips):
    slot = iota(0) >> 5
    clip_of_row = jnp.where(
        slot == 0, clips[0], jnp.where(slot == 1, clips[1], jnp.where(slot == 2, clips[2], clips[3]))
    )
    same_group = (iota(0) & (GROUPS - 1)) == (iota(1) >> 2)
    return [
        exact_dot(table, (same_group & (clip_of_row == clips[f])).astype(F32)) for f in range(FRAMES)
    ]


def counts(clips, cells):
    out = []
    for f in range(FRAMES):
        n = jnp.int32(0)
        for other in range(FRAMES):
            n = n + (clips[other] == clips[f]).astype(jnp.int32)
        out.append(n.astype(F32) * cells)
    return out


def clips_of(info_ref, turn):
    return [info_ref[turn * FRAMES + f] for f in range(FRAMES)]


def paired(clips, f, kt):
    ok = clips[f] < FRAMES
    if kt:
        ok = ok & (clips[f - kt] == clips[f])
    return ok


def colsum(x):
    return jnp.sum(x, axis=0, keepdims=True)


def flat(x):
    return x.reshape(-1, CH)


def statistics(table, clips, cells):
    total = unpack_rows(table, clips)
    count = counts(clips, cells)
    out = []
    for f in range(FRAMES):
        mean = total[f][0:1] / count[f]
        var = total[f][1:2] / count[f] - mean * mean
        out.append((mean, 1.0 / jnp.sqrt(var + EPS)))
    return out


def act_slope(normed, gain, shift):
    act = normed * gain + shift
    sigm = jax.nn.sigmoid(act)
    return sigm * (1.0 + act * (1.0 - sigm))


def sums_kernel(pre_ref, cot_ref, loss_ref, out_ref, head_ref, tail_ref):
    per_frame = []
    for f in range(FRAMES):
        rows = []
        for t in range(2):
            x = flat(pre_ref[t, f].astype(F32))
            rows += [colsum(x), colsum(x * x)]
        per_frame.append(jnp.concatenate(rows, axis=0))
    out_ref[...] = jnp.broadcast_to(pack_rows(per_frame)[None], out_ref.shape)
    for ref, two, one in ((head_ref, 0, 0), (tail_ref, ROWS - 2, ROWS - 1)):
        ref[:, 0:2] = pre_ref[0, :, two : two + 2]
        ref[:, 2:4] = cot_ref[:, two : two + 2]
        ref[:, 4:5] = pre_ref[1, :, one : one + 1]
        ref[:, 5:6] = loss_ref[:, one : one + 1]


def act_first_kernel(
    cells, info_ref, table_ref, pre_ref, cot_ref, up_ref, down_ref, gain_ref, shift_ref,
    out_ref, scaled_ref, normed_ref, stats_ref, parts_ref,
):
    table = jnp.sum(table_ref[...], axis=0)
    gain, shift = gain_ref[...], shift_ref[...]
    clips = clips_of(info_ref, 0)
    stats = statistics(table[0:2], clips, cells)
    later = statistics(table[2:4], clips_of(info_ref, 1), cells)
    per_frame = []
    gain_part = jnp.zeros((1, CH), F32)
    shift_part = jnp.zeros((1, CH), F32)
    for f in range(FRAMES):
        mean, rstd = stats[f]
        live = clips[f] < FRAMES
        sums = None
        for row, count, pre, cot in (
            (0, 2, up_ref[f, 0:2], up_ref[f, 2:4]),
            (2, ROWS, pre_ref[0, f], cot_ref[f]),
            (2 + ROWS, 2, down_ref[f, 0:2], down_ref[f, 2:4]),
        ):
            normed = (flat(pre.astype(F32)) - mean) * rstd
            grad_act = flat(cot.astype(F32)) * act_slope(normed, gain, shift)
            grad_act = jnp.where(live, grad_act, 0.0)
            if count == ROWS:
                sums = (colsum(grad_act), colsum(grad_act * normed))
            scaled_ref[f, row : row + count] = ((rstd * gain) * grad_act).reshape(count, COLS, CH)
            normed_ref[f, row : row + count] = (normed * rstd).reshape(count, COLS, CH)
        shift_part = shift_part + sums[0]
        gain_part = gain_part + sums[1]
        per_frame.append(jnp.concatenate([sums[0] * gain, sums[1] * gain], axis=0))
        stats_ref[f : f + 1] = rstd
        stats_ref[FRAMES + f : FRAMES + f + 1] = later[f][0]
        stats_ref[2 * FRAMES + f : 2 * FRAMES + f + 1] = later[f][1]
    parts_ref[0:1] = gain_part
    parts_ref[1:2] = shift_part
    out_ref[...] = jnp.broadcast_to(pack_rows(per_frame)[None], out_ref.shape)


def write_columns(columns_ref, info_ref, halo, clips, table, cells, scaled_ref, normed_ref, rstd_of):
    total = unpack_rows(table, clips)
    count = counts(clips, cells)
    rows = ROWS + 2 * halo
    place = iota(0, (rows * COLS, CH))
    column = place & (COLS - 1)
    row = place >> 5
    first = jnp.where(info_ref[2 * FRAMES] == 1, halo, 0)
    last = jnp.where(info_ref[2 * FRAMES + 1] == 1, halo + ROWS, rows)
    inside = (row >= first) & (row < last)
    for f in range(FRAMES):
        avg_a = total[f][0:1] / count[f]
        avg_b = total[f][1:2] / count[f]
        keep = inside & (clips[f] < FRAMES)
        value = flat(scaled_ref[f]) - rstd_of(f) * avg_a - flat(normed_ref[f]) * avg_b
        value = jnp.where(keep, value, 0.0)
        left = jnp.where(column == COLS - 1, 0.0, pltpu.roll(value, rows * COLS - 1, 0))
        right = jnp.where(column == 0, 0.0, pltpu.roll(value, 1, 0))
        columns_ref[f, :, 0:CH] = left.astype(BF16)
        columns_ref[f, :, CH : 2 * CH] = value.astype(BF16)
        columns_ref[f, :, 2 * CH : 3 * CH] = right.astype(BF16)


def conv_frame(columns_ref, weight_ref, clips, f, rows):
    total = None
    for kt in range(min(3, FRAMES - f)):
        part = None
        for dy in (-1, 0, 1):
            start = (1 - dy) * COLS
            term = jnp.dot(
                columns_ref[f + kt, start : start + rows * COLS],
                weight_ref[3 * kt + dy + 1],
                preferred_element_type=F32,
            )
            part = term if part is None else part + term
        part = jnp.where(paired(clips, f + kt, kt), part, 0.0)
        total = part if total is None else total + part
    return total.astype(BF16).reshape(rows, COLS, CH)


def kernel_terms(columns_ref, act_ref, clips, halo, kt, dy):
    count = FRAMES - kt
    start = (halo - dy) * COLS
    blocks = [
        jnp.where(paired(clips, f + kt, kt), act_ref[:, f * CH : (f + 1) * CH], jnp.zeros((), BF16))
        for f in range(count)
    ]
    columns = columns_ref[kt:FRAMES, start : start + ROWS * COLS, :].reshape(count * CH, 3 * CH)
    return jnp.dot(jnp.concatenate(blocks, axis=1), columns, preferred_element_type=F32)


def conv_first_kernel(
    cells, info_ref, table_ref, scaled_ref, normed_ref, stats_ref, weight_ref, grad_ref, columns_ref
):
    clips = clips_of(info_ref, 0)
    table = jnp.sum(table_ref[...], axis=0)
    write_columns(
        columns_ref, info_ref, 2, clips, table, cells, scaled_ref, normed_ref,
        lambda f: stats_ref[f : f + 1],
    )
    for f in range(FRAMES):
        grad_ref[f] = conv_frame(columns_ref, weight_ref, clips, f, ROWS + 2)


def weight_first_kernel(info_ref, columns_ref, act_ref, out_ref):
    clips = clips_of(info_ref, 0)
    for kt in range(3):
        for dy in (-1, 0, 1):
            terms = kernel_terms(columns_ref, act_ref, clips, 2, kt, dy)
            tap = 9 * kt + 3 * (dy + 1)
            for dx in range(3):
                out_ref[tap + dx] = terms[:, dx * CH : (dx + 1) * CH]


def act_second_kernel(
    info_ref, hand_ref, loss_ref, pre_ref, up_ref, down_ref, stats_ref, parts_ref, gain_ref, shift_ref,
    out_ref, scaled_ref, normed_ref,
):
    gain, shift = gain_ref[...], shift_ref[...]
    clips = clips_of(info_ref, 1)
    is_last = info_ref[2 * FRAMES + 2] == 1
    per_frame = []
    gain_part = parts_ref[0:1]
    shift_part = parts_ref[1:2]
    for f in range(FRAMES):
        mean = stats_ref[FRAMES + f : FRAMES + f + 1]
        rstd = stats_ref[2 * FRAMES + f : 2 * FRAMES + f + 1]
        live = clips[f] < FRAMES
        sums = None
        for row, count, pre, loss in (
            (0, 1, up_ref[f, 4:5], up_ref[f, 5:6]),
            (1, ROWS, pre_ref[1, f], loss_ref[f]),
            (1 + ROWS, 1, down_ref[f, 4:5], down_ref[f, 5:6]),
        ):
            normed = (flat(pre.astype(F32)) - mean) * rstd
            incoming = jnp.where(
                is_last, flat(loss.astype(F32)), flat(hand_ref[f, row : row + count].astype(F32))
            )
            grad_act = jnp.where(live, incoming * act_slope(normed, gain, shift), 0.0)
            if count == ROWS:
                sums = (colsum(grad_act), colsum(grad_act * normed))
            scaled_ref[f, row : row + count] = ((rstd * gain) * grad_act).reshape(count, COLS, CH)
            normed_ref[f, row : row + count] = (normed * rstd).reshape(count, COLS, CH)
        shift_part = shift_part + sums[0]
        gain_part = gain_part + sums[1]
        per_frame.append(jnp.concatenate([sums[0] * gain, sums[1] * gain], axis=0))
    rows = jnp.concatenate([pack_rows(per_frame), gain_part, shift_part], axis=0)
    out_ref[...] = jnp.broadcast_to(rows[None], out_ref.shape)


def weight_second_kernel(
    cells, scale, info_ref, table_ref, scaled_ref, normed_ref, stats_ref, act_ref, first_ref,
    out_ref, columns_ref, parts_ref, sum_ref,
):
    clips = clips_of(info_ref, 1)
    table = jnp.sum(table_ref[...], axis=0)
    parts_ref[...] = table[2:4] * scale
    write_columns(
        columns_ref, info_ref, 1, clips, table[0:2], cells, scaled_ref, normed_ref,
        lambda f: stats_ref[2 * FRAMES + f : 2 * FRAMES + f + 1],
    )
    for kt in range(3):
        for dy in (-1, 0, 1):
            terms = kernel_terms(columns_ref, act_ref, clips, 1, kt, dy)
            tap = 9 * kt + 3 * (dy + 1)
            for dx in range(3):
                at = (tap + dx) * CH
                sum_ref[at : at + CH] = first_ref[tap + dx] + terms[:, dx * CH : (dx + 1) * CH]
    cores, chips, chunk, _ = out_ref.shape
    for chip in range(chips):
        for core in range(cores):
            at = (chip * cores + core) * chunk
            out_ref[core, chip] = sum_ref[at : at + chunk].astype(BF16)


def conv_second_kernel(info_ref, columns_ref, weight_ref, first_ref, out_ref):
    clips = clips_of(info_ref, 1)
    for f in range(FRAMES):
        out_ref[0, f] = first_ref[f, 1 : 1 + ROWS]
        out_ref[1, f] = conv_frame(columns_ref, weight_ref, clips, f, ROWS)


def call(kernel, name, args, outs, scratch=(), flops=10_000_000):
    smem = [SMEM] if args[0].dtype == jnp.int32 else []
    size = sum(a.size * a.dtype.itemsize for a in list(args) + list(outs))
    return pl.pallas_call(
        kernel,
        out_shape=tuple(outs),
        in_specs=smem + [VMEM] * (len(args) - len(smem)),
        out_specs=tuple([VMEM] * len(outs)),
        scratch_shapes=list(scratch),
        compiler_params=pltpu.CompilerParams(vmem_limit_bytes=40 * 1024 * 1024),
        cost_estimate=pl.CostEstimate(flops=flops, bytes_accessed=size, transcendentals=0),
        name=name,
    )(*args)


def shape(dims, dtype=F32):
    return jax.ShapeDtypeStruct(dims, dtype)


def local(activations, pre_norm, cot_first, loss_grad, frame_clip, weight, norm_gain, norm_shift):
    dp = lax.axis_size("dp")
    me = lax.axis_index("dp")
    cells = float(dp * ROWS * COLS * PER)
    chips, chunk = dp // 2, TAPS * CH // dp
    flags = [me == 0, me == dp - 1, lax.axis_index("segment") == lax.axis_size("segment") - 1]
    info = jnp.concatenate([frame_clip.reshape(2 * FRAMES), jnp.stack(flags).astype(jnp.int32)])
    pre = pre_norm[0]
    cot, loss = cot_first[0], loss_grad[0]
    taps = weight[0].reshape(9, 3, CH, CH).transpose(0, 1, 3, 2).reshape(9, 3 * CH, CH)
    act = activations[0].reshape(2, FRAMES * ROWS * COLS, CH).transpose(0, 2, 1)

    def exchange(table):
        return lax.all_to_all(table, "dp", 0, 0, tiled=True)

    edge = (FRAMES, 6, COLS, CH)
    table, head, tail = call(
        sums_kernel, "sums", (pre, cot, loss),
        (shape((dp, 4, CH)), shape(edge, BF16), shape(edge, BF16)),
    )
    down = lax.ppermute(head, "dp", [(i + 1, i) for i in range(dp - 1)])
    up = lax.ppermute(tail, "dp", [(i, i + 1) for i in range(dp - 1)])
    table = exchange(table)

    wide = (FRAMES, ROWS + 4, COLS, CH)
    table, scaled, normed, stats, parts = call(
        functools.partial(act_first_kernel, cells), "act_first",
        (info, table, pre, cot, up, down, norm_gain, norm_shift),
        (shape((dp, 2, CH)), shape(wide), shape(wide), shape((3 * FRAMES, CH)), shape((2, CH))),
    )
    table = exchange(table)

    grad_first, columns = call(
        functools.partial(conv_first_kernel, cells), "conv_first",
        (info, table, scaled, normed, stats, taps),
        (shape((FRAMES, ROWS + 2, COLS, CH), BF16), shape((FRAMES, (ROWS + 4) * COLS, 3 * CH), BF16)),
        flops=700_000_000,
    )
    count = lax.axis_size("segment")
    hand = lax.ppermute(grad_first, "segment", [(i + 1, i) for i in range(count - 1)])
    (weight_first,) = call(
        weight_first_kernel, "weight_first", (info, columns, act[0]),
        (shape((TAPS, CH, CH)),), flops=450_000_000,
    )

    wide = (FRAMES, ROWS + 2, COLS, CH)
    table, scaled, normed = call(
        act_second_kernel, "act_second",
        (info, hand, loss, pre, up, down, stats, parts, norm_gain, norm_shift),
        (shape((dp, 4, CH)), shape(wide), shape(wide)),
    )
    table = exchange(table)

    terms, columns, parts = call(
        functools.partial(weight_second_kernel, cells, 1.0 / dp), "weight_second",
        (info, table, scaled, normed, stats, act[1], weight_first),
        (
            shape((2, chips, chunk, CH), BF16),
            shape((FRAMES, (ROWS + 2) * COLS, 3 * CH), BF16),
            shape((2, CH)),
        ),
        scratch=[pltpu.VMEM((TAPS * CH, CH), F32)],
        flops=450_000_000,
    )
    pairs = [[2 * i, 2 * i + 1] for i in range(chips)]
    terms = lax.all_to_all(terms, "dp", 0, 0, axis_index_groups=pairs, tiled=True)
    terms = jnp.sum(terms.astype(F32), axis=0).astype(BF16)
    sides = [[2 * i + core for i in range(chips)] for core in range(2)]
    terms = lax.all_to_all(terms, "dp", 0, 0, axis_index_groups=sides, tiled=True)
    grad_weight = jnp.sum(terms.astype(F32), axis=0) * (1.0 / dp)

    (grad_inputs,) = call(
        conv_second_kernel, "conv_second", (info, columns, taps, grad_first),
        (shape((2, FRAMES, ROWS, COLS, CH), BF16),), flops=450_000_000,
    )
    width = CH // dp
    own = lax.dynamic_slice_in_dim(parts, me * width, width, axis=1)
    return (grad_inputs[None], grad_weight[None], own[0:1], own[1:2])


def solution(mesh):
    in_specs = (
        P("segment", None, None, "dp", None, None),
        P("segment", None, None, "dp", None, None),
        P("segment", None, "dp", None, None),
        P(None, None, "dp", None, None),
        P("segment", None, "dp", None),
        P("segment", None, None),
        P("segment", None),
        P("segment", None),
    )
    out_specs = (
        P("segment", None, None, "dp", None, None),
        P("segment", "dp", None),
        P("segment", "dp"),
        P("segment", "dp"),
    )
    return jax.shard_map(local, mesh=mesh, in_specs=in_specs, out_specs=out_specs, check_vma=False)
```

time: 609 us -> 123 us (0.20)
  the two profiles are of different devices: /device:TPU:2 before, /device:TPU:8 now
where the time goes in v1:
time: 123 us; the launch traced here: 122 us
  starting transfers between devices  45.6 us (37%)
  waiting for transfers between devices  38 us (31%)
  local copies, waits for them, and re-layouts  18.7 us (15%)
  Pallas kernels  12.8 us (10%)
  blocking collectives  4.43 us (4%)
  other arithmetic  1.98 us (2%)
    all_to_all x3, starting transfers between devices, exchange(): return lax.all_to_all(table, 'dp', 0, 0, tiled=True)  33.9 us
    all_to_all x3, waiting for transfers between devices, exchange(): return lax.all_to_all(table, 'dp', 0, 0, tiled=True)  16.5 us
    all_to_all x1, waiting for transfers between devices, local(): lax.all_to_all(terms, 'dp', 0, 0, axis_index_groups=sides, tiled=True)  13.9 us
    pallas_call x7, Pallas kernels, call(): pl.pallas_call(kernel, out_shape=tuple(outs), in_specs=smem + [VMEM] * (l...  12.8 us
    unnamed x41, local copies, waits for them, and re-layouts  12.7 us
    ppermute x1, waiting for transfers between devices, local(): lax.ppermute(grad_first, 'segment', [(i + 1, i) for i in range(count - 1)])  6.42 us
    all_to_all x1, starting transfers between devices, local(): lax.all_to_all(terms, 'dp', 0, 0, axis_index_groups=sides, tiled=True)  4.81 us
    all_to_all x1, blocking collectives, local(): lax.all_to_all(terms, 'dp', 0, 0, axis_index_groups=pairs, tiled=True)  4.43 us
  transfers between devices with their start and end apart: 7, of which 6 were waited for; matrix products, arithmetic and copies ran while one was open for 5% of the time, Pallas kernels for 3%

profile of v1, /device:TPU:8, one launch (start us, length us, event | category | flops | bytes accessed | tf_op | source)
XLA Modules:
  0.0 122.4 jit_solution(4410308756516628456)
XLA Ops:
  0.6 0.9 copy-done
  1.6 0.9 copy-done.3
  2.5 0.9 copy-done.6
  3.4 1.1 sums.1
  4.5 17.2 %all-to-all-start = ((f32[64,4,128]{2,1,0:T(4,128)}), f32[64,4,128]{2,1,0:T(4,128)S(1)}, u32[]{:S(2)}, u32[]{:S(2)}) async-start(f32[64,4,128]{2,1,0:T(4,128)} %get-tuple-element.20), calls=%async_computation | async-start | bytes 262144 | tf_op jit(solution)/shard_map/all_to_all | solution.py:321
  21.6 2.1 %collective-permute-start = (bf16[4,6,32,128]{3,2,1,0:T(8,128)(2,1)S(1)}, bf16[4,6,32,128]{3,2,1,0:T(8,128)(2,1)S(1)}, u32[]{:S(2)}, u32[]{:S(2)}) collective-permute-start(bf16[4,6,32,128]{3,2,1,0:T(8,128)(2,1)S(1)} %get-tuple-element.21), channel_id=1, source_target_pairs={{0,1},{1,2},{2,3},{3,4},{4,5},{5,6},{6,7},{7,8},{8,9},{9,10},{10,1... | collective-permute-start | bytes 589832 | tf_op jit(solution)/shard_map/ppermute | solution.py:329
  23.7 3.5 %collective-permute-start.1 = (bf16[4,6,32,128]{3,2,1,0:T(8,128)(2,1)S(1)}, bf16[4,6,32,128]{3,2,1,0:T(8,128)(2,1)S(1)}, u32[]{:S(2)}, u32[]{:S(2)}) collective-permute-start(bf16[4,6,32,128]{3,2,1,0:T(8,128)(2,1)S(1)} %get-tuple-element.22), channel_id=1, source_target_pairs={{1,0},{2,1},{3,2},{4,3},{5,4},{6,5},{7,6},{8,7},{9,8},{10,9},{11,1... | collective-permute-start | bytes 589832 | tf_op jit(solution)/shard_map/ppermute | solution.py:328
  27.2 0.5 broadcast.12
  27.7 1.3 %reduce.4 = s32[2,4]{1,0:T(2,128)S(1)} reduce(s32[1,2,1,4]{3,2,1,0:T(1,128)} %param.12, s32[]{:T(128)} %broadcast.12), dimensions={0,2}, to_apply=%param.12.reduce_sub_computation.3 | reduce | bytes 68 | tf_op args[4]
  29.1 0.1 reshape.23
  29.2 0.1 pad_add_fusion.info_ref
  29.3 1.1 collective-permute-done.1.down_ref
  30.4 1.4 %all-to-all-done.table_ref = f32[64,4,128]{2,1,0:T(4,128)S(1)} async-done(((f32[64,4,128]{2,1,0:T(4,128)}), f32[64,4,128]{2,1,0:T(4,128)S(1)}, u32[]{:S(2)}, u32[]{:S(2)}) %all-to-all-start) | async-done | bytes 131104 | tf_op jit(solution)/shard_map/all_to_all | solution.py:321
  31.8 0.9 copy-done.1
  32.7 0.9 copy-done.7
  33.6 0.7 copy-done.14
  34.3 0.7 copy-done.16
  34.9 2.3 %act_first.1 = (f32[64,2,128]{2,1,0:T(2,128)}, f32[4,8,32,128]{3,2,1,0:T(8,128)S(1)}, f32[4,8,32,128]{3,2,1,0:T(8,128)S(1)}, f32[12,128]{1,0:T(8,128)S(1)}, f32[2,128]{1,0:T(2,128)S(1)}) custom-call(s32[11]{0:T(128)S(1)} %pad_add_fusion.info_ref, f32[64,4,128]{2,1,0:T(4,128)S(1)} %all-to-all-done.table_ref, bf16[2,4,4,32,128]{4,3,2,1,0:T(8,128)(2,1)S(1)} %bitcast.20, ...), custom_call_target="tpu_custom_call" | custom-call | flops 10000000 | bytes 2039852 | tf_op jit(solution)/shard_map/act_first/pallas_call | solution.py:292
  37.2 0.8 copy-done.18
  38.0 10.7 %all-to-all-start.1 = ((f32[64,2,128]{2,1,0:T(2,128)}), f32[64,2,128]{2,1,0:T(2,128)S(1)}, u32[]{:S(2)}, u32[]{:S(2)}) async-start(f32[64,2,128]{2,1,0:T(2,128)} %get-tuple-element.23), calls=%async_computation.1 | async-start | bytes 131072 | tf_op jit(solution)/shard_map/all_to_all | solution.py:321
  48.7 1.9 %copy.22 = bf16[9,3,128,128]{2,3,1,0:T(8,128)(2,1)S(1)} copy(bf16[9,3,128,128]{3,2,1,0:T(8,128)(2,1)} %bitcast.27) | data formatting | bytes 1769472 | tf_op jit(solution)/shard_map/reshape;squeeze | solution.py:317
  50.7 7.0 %all-to-all-done.1.table_ref = f32[64,2,128]{2,1,0:T(2,128)S(1)} async-done(((f32[64,2,128]{2,1,0:T(2,128)}), f32[64,2,128]{2,1,0:T(2,128)S(1)}, u32[]{:S(2)}, u32[]{:S(2)}) %all-to-all-start.1) | async-done | bytes 65568 | tf_op jit(solution)/shard_map/all_to_all | solution.py:321
  57.7 1.0 copy-done.19
  58.7 2.2 %conv_first.1 = (bf16[4,6,32,128]{3,2,1,0:T(8,128)(2,1)S(1)}, bf16[4,256,384]{2,1,0:T(8,128)(2,1)S(1)}) custom-call(s32[11]{0:T(128)S(1)} %pad_add_fusion.info_ref, f32[64,2,128]{2,1,0:T(2,128)S(1)} %all-to-all-done.1.table_ref, f32[4,8,32,128]{3,2,1,0:T(8,128)S(1)} %get-tuple-element.24.scaled_ref, f32[4,8,32,128]{3,2,1,0:T(8,128)S(1)} %copy-done.19, ...), custom_call_target="tpu_custom_call" | custom-call | flops 700000000 | bytes 2988076 | tf_op jit(solution)/shard_map/conv_first/pallas_call | solution.py:292
  60.9 1.3 %collective-permute-start.2 = (bf16[4,6,32,128]{3,2,1,0:T(8,128)(2,1)S(1)}, bf16[4,6,32,128]{3,2,1,0:T(8,128)(2,1)S(1)}, u32[]{:S(2)}, u32[]{:S(2)}) collective-permute-start(bf16[4,6,32,128]{3,2,1,0:T(8,128)(2,1)S(1)} %get-tuple-element.27.first_ref), channel_id=1, source_target_pairs={{64,0},{128,64},{192,128},{256,192},{320,256},{384,320},{448,384},... | collective-permute-start | bytes 589832 | tf_op jit(solution)/shard_map/ppermute | solution.py:347
  62.2 1.1 copy.23
  63.3 6.4 %collective-permute-done.2.hand_ref = bf16[4,6,32,128]{3,2,1,0:T(8,128)(2,1)S(1)} collective-permute-done((bf16[4,6,32,128]{3,2,1,0:T(8,128)(2,1)S(1)}, bf16[4,6,32,128]{3,2,1,0:T(8,128)(2,1)S(1)}, u32[]{:S(2)}, u32[]{:S(2)}) %collective-permute-start.2) | collective-permute-done | bytes 196640 | tf_op jit(solution)/shard_map/ppermute | solution.py:347
  69.7 1.8 %act_second.1 = (f32[64,4,128]{2,1,0:T(4,128)}, f32[4,6,32,128]{3,2,1,0:T(8,128)S(1)}, f32[4,6,32,128]{3,2,1,0:T(8,128)S(1)}) custom-call(s32[11]{0:T(128)S(1)} %pad_add_fusion.info_ref, bf16[4,6,32,128]{3,2,1,0:T(8,128)(2,1)S(1)} %collective-permute-done.2.hand_ref, bf16[4,4,32,128]{3,2,1,0:T(8,128)(2,1)S(1)} %bitcast.23, ...), custom_call_target="tpu_custom_call" | custom-call | flops 10000000 | bytes 1908780 | tf_op jit(solution)/shard_map/act_second/pallas_call | solution.py:292
  71.5 0.8 copy-done.8
  72.3 0.7 copy-done.10
  73.0 6.1 %all-to-all-start.2 = ((f32[64,4,128]{2,1,0:T(4,128)}), f32[64,4,128]{2,1,0:T(4,128)}, u32[]{:S(2)}, u32[]{:S(2)}) async-start(f32[64,4,128]{2,1,0:T(4,128)} %get-tuple-element.29), calls=%async_computation.2 | async-start | bytes 262144 | tf_op jit(solution)/shard_map/all_to_all | solution.py:321
  79.1 0.7 slice_bitcast_fusion
  79.8 1.2 weight_first.1.first_ref
  81.0 8.2 %all-to-all-done.2.table_ref = f32[64,4,128]{2,1,0:T(4,128)} async-done(((f32[64,4,128]{2,1,0:T(4,128)}), f32[64,4,128]{2,1,0:T(4,128)}, u32[]{:S(2)}, u32[]{:S(2)}) %all-to-all-start.2) | async-done | bytes 131104 | tf_op jit(solution)/shard_map/all_to_all | solution.py:321
  89.2 0.9 copy-done.5
  90.1 1.0 copy-done.9
  91.1 1.0 copy-done.11
  92.1 2.2 %weight_second.1 = (bf16[2,32,54,128]{3,2,1,0:T(8,128)(2,1)S(1)}, bf16[4,192,384]{2,1,0:T(8,128)(2,1)S(1)}, f32[2,128]{1,0:T(2,128)S(1)}) custom-call(s32[11]{0:T(128)S(1)} %pad_add_fusion.info_ref, f32[64,4,128]{2,1,0:T(4,128)} %all-to-all-done.2.table_ref, f32[4,6,32,128]{3,2,1,0:T(8,128)S(1)} %copy-done.9, f32[4,6,32,128]{3,2,1,0:T(8,128)S(1)} %copy-done.11, ...), custom_call_target="tpu_custom_call" | custom-call | flops 450000000 | bytes 4299820 | tf_op jit(solution)/shard_map/weight_second/pallas_call | solution.py:292
  94.3 0.1 copy.24
  94.4 4.4 %all_to_all.25 = bf16[2,32,54,128]{3,1,2,0:T(8,128)(2,1)S(1)} all-to-all(bf16[2,32,54,128]{3,1,2,0:T(8,128)(2,1)S(1)} %copy.24), channel_id=1, replica_groups={{0,1},{2,3},{4,5},{6,7},{8,9},{10,11},{12,13},{14,15},{16,17},{18,19},{..., dimensions={0} | all-to-all | bytes 1769472 | tf_op jit(solution)/shard_map/all_to_all | solution.py:373
  98.8 0.4 reduce_sum.21
  99.2 0.9 copy.25
  100.2 4.8 %all-to-all-start.4 = ((bf16[32,54,128]{2,1,0:T(8,128)(2,1)}), bf16[32,54,128]{2,1,0:T(8,128)(2,1)S(1)}, u32[]{:S(2)}, u32[]{:S(2)}) async-start(bf16[32,54,128]{2,1,0:T(8,128)(2,1)} %copy.25), calls=%async_computation.4 | async-start | bytes 917504 | tf_op jit(solution)/shard_map/all_to_all | solution.py:376
  105.0 2.1 %conv_second.1 = bf16[2,4,4,32,128]{4,3,2,1,0:T(8,128)(2,1)} custom-call(s32[11]{0:T(128)S(1)} %pad_add_fusion.info_ref, bf16[4,192,384]{2,1,0:T(8,128)(2,1)S(1)} %get-tuple-element.33.columns_ref, bf16[9,384,128]{2,1,0:T(8,128)(2,1)S(1)} %bitcast.18, bf16[4,6,32,128]{3,2,1,0:T(8,128)(2,1)S(1)} %copy-done.13), custom_call_target="tpu_custom_call" | custom-call | flops 450000000 | bytes 1933356 | tf_op jit(solution)/shard_map/conv_second/pallas_call | solution.py:292
  107.2 0.5 fusion
  107.7 13.9 %all-to-all-done.4 = bf16[32,54,128]{2,1,0:T(8,128)(2,1)S(1)} async-done(((bf16[32,54,128]{2,1,0:T(8,128)(2,1)}), bf16[32,54,128]{2,1,0:T(8,128)(2,1)S(1)}, u32[]{:S(2)}, u32[]{:S(2)}) %all-to-all-start.4) | async-done | bytes 442400 | tf_op jit(solution)/shard_map/all_to_all | solution.py:376
  121.7 0.1 convert_reduce_fusion
  121.7 0.6 mul.21
  (30 shorter events, 0.2 us)
Async XLA Ops:
  0.6 1.0 copy-start
  1.6 0.9 copy-start.3
  2.5 0.9 copy-start.6
  4.5 27.3 %all-to-all-start = ((f32[64,4,128]{2,1,0:T(4,128)}), f32[64,4,128]{2,1,0:T(4,128)S(1)}, u32[]{:S(2)}, u32[]{:S(2)}) async-start(f32[64,4,128]{2,1,0:T(4,128)} %get-tuple-element.20), calls=%async_computation | async-start | bytes 262144 | tf_op jit(solution)/shard_map/all_to_all | solution.py:321
  21.6 7.7 %collective-permute-start = (bf16[4,6,32,128]{3,2,1,0:T(8,128)(2,1)S(1)}, bf16[4,6,32,128]{3,2,1,0:T(8,128)(2,1)S(1)}, u32[]{:S(2)}, u32[]{:S(2)}) collective-permute-start(bf16[4,6,32,128]{3,2,1,0:T(8,128)(2,1)S(1)} %get-tuple-element.21), channel_id=1, source_target_pairs={{0,1},{1,2},{2,3},{3,4},{4,5},{5,6},{6,7},{7,8},{8,9},{9,10},{10,1... | collective-permute-start | bytes 589832 | tf_op jit(solution)/shard_map/ppermute | solution.py:329
  23.7 6.7 %collective-permute-start.1 = (bf16[4,6,32,128]{3,2,1,0:T(8,128)(2,1)S(1)}, bf16[4,6,32,128]{3,2,1,0:T(8,128)(2,1)S(1)}, u32[]{:S(2)}, u32[]{:S(2)}) collective-permute-start(bf16[4,6,32,128]{3,2,1,0:T(8,128)(2,1)S(1)} %get-tuple-element.22), channel_id=1, source_target_pairs={{1,0},{2,1},{3,2},{4,3},{5,4},{6,5},{7,6},{8,7},{9,8},{10,9},{11,1... | collective-permute-start | bytes 589832 | tf_op jit(solution)/shard_map/ppermute | solution.py:328
  31.8 1.0 copy-start.1
  32.7 0.9 copy-start.7
  33.6 0.7 copy-start.14
  34.3 0.7 copy-start.16
  37.2 0.8 copy-start.18
  38.0 19.6 %all-to-all-start.1 = ((f32[64,2,128]{2,1,0:T(2,128)}), f32[64,2,128]{2,1,0:T(2,128)S(1)}, u32[]{:S(2)}, u32[]{:S(2)}) async-start(f32[64,2,128]{2,1,0:T(2,128)} %get-tuple-element.23), calls=%async_computation.1 | async-start | bytes 131072 | tf_op jit(solution)/shard_map/all_to_all | solution.py:321
  50.6 19.1 %copy-start.2 = (bf16[1,2,4,4,32,128]{5,4,3,2,1,0:T(8,128)(2,1)S(1)}, bf16[1,2,4,4,32,128]{5,4,3,2,1,0:T(8,128)(2,1)}, u32[]{:S(2)}) copy-start(bf16[1,2,4,4,32,128]{5,4,3,2,1,0:T(8,128)(2,1)} %param.9) | copy-start | bytes 786436
  50.6 19.1 %copy-start.4 = (bf16[1,4,4,32,128]{4,3,2,1,0:T(8,128)(2,1)S(1)}, bf16[1,4,4,32,128]{4,3,2,1,0:T(8,128)(2,1)}, u32[]{:S(2)}) copy-start(bf16[1,4,4,32,128]{4,3,2,1,0:T(8,128)(2,1)} %param.11) | copy-start | bytes 393220
  50.6 19.1 %copy-start.15 = (f32[1,128]{1,0:T(1,128)S(1)}, f32[1,128]{1,0:T(1,128)}, u32[]{:S(2)}) copy-start(f32[1,128]{1,0:T(1,128)} %gain_ref.3) | copy-start | bytes 1540
  50.7 19.1 %copy-start.17 = (f32[1,128]{1,0:T(1,128)S(1)}, f32[1,128]{1,0:T(1,128)}, u32[]{:S(2)}) copy-start(f32[1,128]{1,0:T(1,128)} %shift_ref.3) | copy-start | bytes 1540
  57.7 1.0 copy-start.19
  60.9 18.9 %copy-start.12 = (bf16[4,6,32,128]{3,2,1,0:T(8,128)(2,1)}, bf16[4,6,32,128]{3,2,1,0:T(8,128)(2,1)S(1)}, u32[]{:S(2)}) copy-start(bf16[4,6,32,128]{3,2,1,0:T(8,128)(2,1)S(1)} %get-tuple-element.27.first_ref) | copy-start | bytes 589828
  60.9 8.8 %collective-permute-start.2 = (bf16[4,6,32,128]{3,2,1,0:T(8,128)(2,1)S(1)}, bf16[4,6,32,128]{3,2,1,0:T(8,128)(2,1)S(1)}, u32[]{:S(2)}, u32[]{:S(2)}) collective-permute-start(bf16[4,6,32,128]{3,2,1,0:T(8,128)(2,1)S(1)} %get-tuple-element.27.first_ref), channel_id=1, source_target_pairs={{64,0},{128,64},{192,128},{256,192},{320,256},{384,320},{448,384},... | collective-permute-start | bytes 589832 | tf_op jit(solution)/shard_map/ppermute | solution.py:347
  71.5 0.8 copy-start.8
  72.3 0.8 copy-start.10
  73.0 16.1 %all-to-all-start.2 = ((f32[64,4,128]{2,1,0:T(4,128)}), f32[64,4,128]{2,1,0:T(4,128)}, u32[]{:S(2)}, u32[]{:S(2)}) async-start(f32[64,4,128]{2,1,0:T(4,128)} %get-tuple-element.29), calls=%async_computation.2 | async-start | bytes 262144 | tf_op jit(solution)/shard_map/all_to_all | solution.py:321
  89.2 0.9 copy-start.5
  90.1 1.0 copy-start.9
  91.1 1.0 copy-start.11
  98.8 6.2 %copy-start.13 = (bf16[4,6,32,128]{3,2,1,0:T(8,128)(2,1)S(1)}, bf16[4,6,32,128]{3,2,1,0:T(8,128)(2,1)}, u32[]{:S(2)}) copy-start(bf16[4,6,32,128]{3,2,1,0:T(8,128)(2,1)} %copy-done.12) | copy-start | bytes 589828
  100.2 21.5 %all-to-all-start.4 = ((bf16[32,54,128]{2,1,0:T(8,128)(2,1)}), bf16[32,54,128]{2,1,0:T(8,128)(2,1)S(1)}, u32[]{:S(2)}, u32[]{:S(2)}) async-start(bf16[32,54,128]{2,1,0:T(8,128)(2,1)} %copy.25), calls=%async_computation.4 | async-start | bytes 917504 | tf_op jit(solution)/shard_map/all_to_all | solution.py:376

commit v2 on v1

v2 whole, which is shorter than its diff:
```python
import functools
import jax
import jax.numpy as jnp
from jax import lax
from jax.experimental import pallas as pl
from jax.experimental.pallas import tpu as pltpu
from jax.sharding import PartitionSpec as P

F32, BF16 = jnp.float32, jnp.bfloat16
FRAMES, ROWS, COLS, CH = 4, 4, 32, 128
GROUPS, PER = 32, 4
TAPS = 27
EPS = 1e-05
VMEM = pl.BlockSpec(memory_space=pltpu.VMEM)
SMEM = pl.BlockSpec(memory_space=pltpu.SMEM)
HBM = pl.BlockSpec(memory_space=pltpu.HBM)

GAIN, SHIFT, CORE, LAST = 0, 1, 2, 3
TURN = 24
INV, LIVE, TOP, BOTTOM, PAIR1, PAIR2 = (8 + 4 * n for n in range(6))
OTHER_TOP, OTHER_BOTTOM = 56, 60
CLIPS = 64
OTHER_TURN = 16
PARAM_ROWS = 80
MEAN0, RSTD0, MEAN1, RSTD1, GAIN_PART, SHIFT_PART = 0, 4, 8, 12, 16, 17
STAT_ROWS = 24


def iota(dim, dims=(CH, CH)):
    return lax.broadcasted_iota(jnp.int32, dims, dim)


def split_dot(rows, marks):
    count = rows.shape[0]
    high = rows.astype(BF16)
    rest = rows - high.astype(F32)
    middle = rest.astype(BF16)
    low = (rest - middle.astype(F32)).astype(BF16)
    out = jnp.dot(
        jnp.concatenate([high.astype(F32), middle.astype(F32), low.astype(F32)], axis=0).astype(BF16),
        marks,
        preferred_element_type=F32,
    )
    return out[0:count] + out[count : 2 * count] + out[2 * count : 3 * count]


def pack_rows(per_frame):
    rows = jnp.concatenate(per_frame, axis=1)
    dims = (FRAMES * CH, CH)
    marks = (iota(1, dims) == (iota(0, dims) >> 2)).astype(F32).astype(BF16)
    return split_dot(rows, marks)


def unpack_rows(table, marks):
    total = split_dot(table, marks)
    return [total[:, f * CH : (f + 1) * CH] for f in range(FRAMES)]


def row(ref, at):
    return ref[at : at + 1]


def colsum(x):
    return jnp.sum(x, axis=0, keepdims=True)


def flat(x):
    return x.reshape(-1, CH)


def act_slope(normed, gain, shift):
    act = normed * gain + shift
    sigm = jax.nn.sigmoid(act)
    return sigm * (1.0 + act * (1.0 - sigm))


def copy_in(pairs, sems):
    copies = [pltpu.make_async_copy(src, dst, sems.at[n]) for n, (src, dst) in enumerate(pairs)]
    for copy in copies:
        copy.start()
    return copies


def sums_kernel(pre_ref, cot_ref, loss_ref, out_ref, head_ref, tail_ref, held_ref, sems):
    pairs = [(pre_ref, held_ref)]
    for ref, two, one in ((head_ref, 0, 0), (tail_ref, ROWS - 2, ROWS - 1)):
        pairs += [
            (pre_ref.at[0, :, two : two + 2], ref.at[:, 0:2]),
            (cot_ref.at[:, two : two + 2], ref.at[:, 2:4]),
            (pre_ref.at[1, :, one : one + 1], ref.at[:, 4:5]),
            (loss_ref.at[:, one : one + 1], ref.at[:, 5:6]),
        ]
    copies = copy_in(pairs, sems)
    copies[0].wait()
    per_frame = []
    for f in range(FRAMES):
        rows = []
        for t in range(2):
            x = flat(held_ref[t, f].astype(F32))
            rows += [colsum(x), colsum(x * x)]
        per_frame.append(jnp.concatenate(rows, axis=0))
    out_ref[...] = jnp.broadcast_to(pack_rows(per_frame)[None], out_ref.shape)
    for copy in copies[1:]:
        copy.wait()


def clip_marks(params_ref, turn):
    slot = iota(0) >> 5
    clips = [row(params_ref, CLIPS + FRAMES * turn + f) for f in range(FRAMES)]
    clip_of_row = jnp.where(
        slot == 0, clips[0], jnp.where(slot == 1, clips[1], jnp.where(slot == 2, clips[2], clips[3]))
    )
    same_group = (iota(0) & (GROUPS - 1)) == (iota(1) >> 2)
    blocks = [(same_group & (clip_of_row == clips[f])).astype(F32).astype(BF16) for f in range(FRAMES)]
    return jnp.concatenate(blocks, axis=1)


def prepare_kernel(
    cells, flag_ref, clip_hbm, pre_ref, cot_ref, gain_ref, shift_ref,
    own_ref, params_ref, clip_ref, held_pre, held_cot, sems,
):
    copies = copy_in(
        [
            (clip_hbm, clip_ref), (pre_ref, held_pre), (cot_ref, held_cot),
            (gain_ref, params_ref.at[GAIN : GAIN + 1]), (shift_ref, params_ref.at[SHIFT : SHIFT + 1]),
        ],
        sems,
    )

    def put(at, scalar):
        params_ref[at : at + 1] = jnp.full((1, CH), scalar, F32)

    put(CORE, flag_ref[4].astype(F32))
    put(LAST, flag_ref[5].astype(F32))
    params_ref[LAST + 1 : INV] = jnp.zeros((INV - LAST - 1, CH), F32)
    flag = [flag_ref[n].astype(F32) for n in range(4)]
    copies[0].wait()
    for t in range(2):
        clips = [clip_ref[0, t, 0, f] for f in range(FRAMES)]
        for f in range(FRAMES):
            count = jnp.int32(0)
            for other in range(FRAMES):
                count = count + (clips[other] == clips[f]).astype(jnp.int32)
            live = (clips[f] < FRAMES).astype(F32)
            base = TURN * t + f
            params_ref[base + INV : base + INV + 1] = 1.0 / jnp.full((1, CH), count.astype(F32) * cells, F32)
            put(base + LIVE, live)
            put(base + TOP, live * flag[0])
            put(base + BOTTOM, live * flag[1])
            put(CLIPS + FRAMES * t + f, clips[f].astype(F32))
            for kt, at in ((1, PAIR1), (2, PAIR2)):
                pair = live * (clips[f - kt] == clips[f]).astype(F32) if f >= kt else live * 0.0
                put(base + at, pair)
            put(OTHER_TURN * t + OTHER_TOP + f, live * flag[2])
            put(OTHER_TURN * t + OTHER_BOTTOM + f, live * flag[3])
    for copy in copies[1:]:
        copy.wait()
    own_ref[0] = held_pre[0].astype(F32)
    own_ref[1] = held_cot[...].astype(F32)


def act_first_kernel(table_ref, own_ref, params_ref, out_ref, stats_ref):
    table = jnp.sum(table_ref[...], axis=0)
    gain, shift = row(params_ref, GAIN), row(params_ref, SHIFT)
    for t, mean_at, rstd_at in ((0, MEAN0, RSTD0), (1, MEAN1, RSTD1)):
        total = unpack_rows(table[2 * t : 2 * t + 2], clip_marks(params_ref, t))
        for f in range(FRAMES):
            inverse = row(params_ref, TURN * t + INV + f)
            mean = total[f][0:1] * inverse
            var = total[f][1:2] * inverse - mean * mean
            stats_ref[mean_at + f : mean_at + f + 1] = mean
            stats_ref[rstd_at + f : rstd_at + f + 1] = 1.0 / jnp.sqrt(var + EPS)
    per_frame = []
    gain_part = jnp.zeros((1, CH), F32)
    shift_part = jnp.zeros((1, CH), F32)
    for f in range(FRAMES):
        normed = (flat(own_ref[0, f]) - row(stats_ref, MEAN0 + f)) * row(stats_ref, RSTD0 + f)
        grad_act = flat(own_ref[1, f]) * act_slope(normed, gain, shift)
        live = row(params_ref, LIVE + f)
        plain = colsum(grad_act) * live
        times = colsum(grad_act * normed) * live
        shift_part = shift_part + plain
        gain_part = gain_part + times
        per_frame.append(jnp.concatenate([plain * gain, times * gain], axis=0))
    stats_ref[GAIN_PART : GAIN_PART + 1] = gain_part
    stats_ref[SHIFT_PART : SHIFT_PART + 1] = shift_part
    stats_ref[SHIFT_PART + 1 :] = jnp.zeros((STAT_ROWS - SHIFT_PART - 1, CH), F32)
    out_ref[...] = jnp.broadcast_to(pack_rows(per_frame)[None], out_ref.shape)


def fields(pre, incoming, mean, rstd, gain, shift, mask):
    normed = (flat(pre.astype(F32)) - mean) * rstd
    scaled = flat(incoming.astype(F32)) * act_slope(normed, gain, shift) * gain
    rstd = rstd * mask
    return scaled * rstd, normed * rstd


def fields_first_kernel(
    up_ref, down_ref, params_ref, stats_ref, pre_ref, cot_ref, loss_ref, act_ref,
    out_ref, bundle_ref, loss_out_ref, held_pre, held_cot, held_loss, sems,
):
    pairs = [
        (pre_ref.at[0], held_pre), (cot_ref, held_cot), (loss_ref, held_loss),
        (act_ref.at[0], bundle_ref.at[:, 6 : 6 + ROWS]), (act_ref.at[1], bundle_ref.at[:, 6 + ROWS : 6 + 2 * ROWS]),
    ]
    for at, edge, own in ((0, 4, pre_ref.at[1]), (14, 1, pre_ref.at[0]), (20, 3, cot_ref)):
        below = 0 if at == 14 else 2 if at == 20 else 4
        pairs += [
            (up_ref.at[:, edge : edge + 1], bundle_ref.at[:, at : at + 1]),
            (own, bundle_ref.at[:, at + 1 : at + 1 + ROWS]),
            (down_ref.at[:, below : below + 1], bundle_ref.at[:, at + 1 + ROWS : at + 2 + ROWS]),
        ]
    copies = copy_in(pairs, sems)
    for copy in copies[:3]:
        copy.wait()
    gain, shift = row(params_ref, GAIN), row(params_ref, SHIFT)
    last = row(params_ref, LAST).reshape(1, 1, 1, CH)
    loss_out_ref[:, 0:1] = (up_ref[:, 5:6].astype(F32) * last).astype(BF16)
    loss_out_ref[:, 1 : 1 + ROWS] = (held_loss[...].astype(F32) * last).astype(BF16)
    loss_out_ref[:, 1 + ROWS : 2 + ROWS] = (down_ref[:, 5:6].astype(F32) * last).astype(BF16)
    for f in range(FRAMES):
        mean, rstd = row(stats_ref, MEAN0 + f), row(stats_ref, RSTD0 + f)
        for at, count, pre, cot, mask in (
            (0, 2, up_ref[f, 0:2], up_ref[f, 2:4], TOP),
            (2, ROWS, held_pre[f], held_cot[f], LIVE),
            (2 + ROWS, 2, down_ref[f, 0:2], down_ref[f, 2:4], BOTTOM),
        ):
            pair = fields(pre, cot, mean, rstd, gain, shift, row(params_ref, mask + f))
            for n in range(2):
                out_ref[n, f, at : at + count] = pair[n].reshape(count, COLS, CH)
    for copy in copies[3:]:
        copy.wait()


def write_columns(store, table, fields_ref, at_fields, params_ref, stats_ref, rstd_at, turn, halo, masks):
    total = unpack_rows(table, clip_marks(params_ref, turn))
    rows = ROWS + 2 * halo
    column = iota(0, (rows * COLS, CH)) & (COLS - 1)
    for f in range(FRAMES):
        inverse = row(params_ref, TURN * turn + INV + f)
        avg_a = total[f][0:1] * inverse * row(stats_ref, rstd_at + f)
        avg_b = total[f][1:2] * inverse
        pieces = []
        for mask, at, count in ((masks[0], 0, halo), (masks[1], halo, ROWS), (masks[2], halo + ROWS, halo)):
            scaled = flat(fields_ref[at_fields + (0, f, slice(at, at + count))])
            normed = flat(fields_ref[at_fields + (1, f, slice(at, at + count))])
            pieces.append(scaled - avg_a * row(params_ref, mask + f) - normed * avg_b)
        value = jnp.concatenate(pieces, axis=0)
        left = jnp.where(column == COLS - 1, 0.0, pltpu.roll(value, rows * COLS - 1, 0))
        right = jnp.where(column == 0, 0.0, pltpu.roll(value, 1, 0))
        store(f, left.astype(BF16), value.astype(BF16), right.astype(BF16))


def store_columns(ref, prefix=()):
    def store(f, left, value, right):
        for n, x in enumerate((left, value, right)):
            ref[prefix + (f, slice(None), slice(n * CH, (n + 1) * CH))] = x

    return store


def conv_frame(columns, weight_ref, params_ref, turn, f, rows):
    total = None
    for kt in range(min(3, FRAMES - f)):
        part = None
        for dy in (-1, 0, 1):
            start = (1 - dy) * COLS
            term = jnp.dot(
                columns(f + kt, start, rows * COLS), weight_ref[3 * kt + dy + 1], preferred_element_type=F32
            )
            part = term if part is None else part + term
        if kt:
            part = part * row(params_ref, TURN * turn + (PAIR1 if kt == 1 else PAIR2) + f + kt)
        total = part if total is None else total + part
    return total.astype(BF16).reshape(rows, COLS, CH)


def conv_first_kernel(
    table_ref, fields_ref, params_ref, stats_ref, taps_ref, grad_ref, value_hbm, columns_ref, weight_ref, value_ref, sems
):
    (copy,) = copy_in([(taps_ref, weight_ref)], sems)
    table = jnp.sum(table_ref[...], axis=0)
    fill = store_columns(columns_ref)

    def store(f, left, value, right):
        fill(f, left, value, right)
        value_ref[f] = value[COLS : COLS * (ROWS + 3)].reshape(ROWS + 2, COLS, CH)

    write_columns(
        store, table, fields_ref, (), params_ref, stats_ref, RSTD0, 0, 2, (TOP, LIVE, BOTTOM)
    )
    value_out = pltpu.make_async_copy(value_ref, value_hbm, sems.at[1])
    value_out.start()
    copy.wait()
    for f in range(FRAMES):
        grad_ref[f] = conv_frame(
            lambda g, start, size: columns_ref[g, start : start + size], weight_ref, params_ref, 0, f, ROWS + 2
        )
    value_out.wait()


def put_acts(turn, bundle_ref, other_ref, params_ref, out_ref):
    for strip, ref in enumerate((bundle_ref, other_ref)):
        for f in range(FRAMES):
            x = flat(ref[f, 6 + ROWS * turn : 6 + ROWS * (turn + 1)].astype(F32)).T
            for kt in range(min(3, FRAMES - f)):
                at = CH * (2 * sum(FRAMES - n for n in range(kt)) + strip * (FRAMES - kt) + f)
                y = x if kt == 0 else x * row(params_ref, TURN * turn + (PAIR1 if kt == 1 else PAIR2) + f + kt)
                out_ref[:, at : at + CH] = y.astype(BF16)


def kernel_terms(columns_ref, act_ref, kt, dy):
    count = FRAMES - kt
    start = (1 - dy) * COLS
    columns = columns_ref[:, kt:FRAMES, start : start + ROWS * COLS, :].reshape(2 * count * CH, 3 * CH)
    at = 2 * CH * sum(FRAMES - n for n in range(kt))
    return jnp.dot(act_ref[:, at : at + 2 * count * CH], columns, preferred_element_type=F32)


def act_second_kernel(hand_ref, loss_ref, slope_ref, params_ref, stats_ref, out_ref, incoming_ref):
    gain = row(params_ref, GAIN)
    per_frame = []
    gain_part = row(stats_ref, GAIN_PART)
    shift_part = row(stats_ref, SHIFT_PART)
    for f in range(FRAMES):
        incoming = hand_ref[f].astype(F32) + loss_ref[f].astype(F32)
        incoming_ref[f] = incoming.astype(BF16)
        grad_act = flat(incoming[1 : 1 + ROWS]) * flat(slope_ref[0, f])
        live = row(params_ref, TURN + LIVE + f)
        plain = colsum(grad_act) * live
        times = colsum(grad_act * flat(slope_ref[1, f])) * live
        shift_part = shift_part + plain
        gain_part = gain_part + times
        per_frame.append(jnp.concatenate([plain * gain, times * gain], axis=0))
    rows = jnp.concatenate([pack_rows(per_frame), gain_part, shift_part], axis=0)
    out_ref[...] = jnp.broadcast_to(rows[None], out_ref.shape)


def weight_first_kernel(
    table_ref, params_ref, stats_ref, value_hbm, bundle_hbm, other_hbm,
    slope_ref, act_hbm, first_hbm,
    columns_ref, act_first_ref, act_ref, first_ref, value_ref, bundle_ref, other_ref, fields_ref, sems,
):
    copies = copy_in([(bundle_hbm, bundle_ref), (other_hbm, other_ref), (value_hbm, value_ref)], sems)
    table = jnp.sum(table_ref[...], axis=0)
    gain, shift = row(params_ref, GAIN), row(params_ref, SHIFT)
    copies[0].wait()
    for f in range(FRAMES):
        normed = flat(bundle_ref[f, 1 : 1 + ROWS].astype(F32)) - row(stats_ref, MEAN1 + f)
        normed = normed * row(stats_ref, RSTD1 + f)
        slope_ref[0, f] = act_slope(normed, gain, shift).reshape(ROWS, COLS, CH)
        slope_ref[1, f] = normed.reshape(ROWS, COLS, CH)
    copies[1].wait()
    put_acts(0, bundle_ref, other_ref, params_ref, act_first_ref)
    put_acts(1, bundle_ref, other_ref, params_ref, act_ref)
    acts_out = pltpu.make_async_copy(act_ref, act_hbm, sems.at[3])
    acts_out.start()
    for f in range(FRAMES):
        mean, rstd = row(stats_ref, MEAN0 + f), row(stats_ref, RSTD0 + f)
        for at, count, mask in ((0, 1, OTHER_TOP), (1, ROWS, LIVE), (1 + ROWS, 1, OTHER_BOTTOM)):
            pair = fields(
                other_ref[f, 14 + at : 14 + at + count], other_ref[f, 20 + at : 20 + at + count], mean, rstd,
                gain, shift, row(params_ref, mask + f),
            )
            for n in range(2):
                fields_ref[n, f, at : at + count] = pair[n].reshape(count, COLS, CH)
    write_columns(
        store_columns(columns_ref, (1,)), table, fields_ref, (), params_ref, stats_ref, RSTD0, 0, 1,
        (OTHER_TOP, LIVE, OTHER_BOTTOM),
    )
    copies[2].wait()
    rows = ROWS + 2
    column = iota(0, (rows * COLS, CH)) & (COLS - 1)
    fill = store_columns(columns_ref, (0,))
    for f in range(FRAMES):
        value = flat(value_ref[f].astype(F32))
        left = jnp.where(column == COLS - 1, 0.0, pltpu.roll(value, rows * COLS - 1, 0))
        right = jnp.where(column == 0, 0.0, pltpu.roll(value, 1, 0))
        fill(f, left.astype(BF16), value.astype(BF16), right.astype(BF16))
    for kt in range(3):
        for dy in (-1, 0, 1):
            terms = kernel_terms(columns_ref, act_first_ref, kt, dy)
            tap = 9 * kt + 3 * (dy + 1)
            for dx in range(3):
                first_ref[tap + dx] = terms[:, dx * CH : (dx + 1) * CH]
    first_out = pltpu.make_async_copy(first_ref, first_hbm, sems.at[4])
    first_out.start()
    acts_out.wait()
    first_out.wait()


def fields_second_kernel(
    incoming_ref, arrived_ref, bundle_hbm, other_hbm, params_ref, stats_ref, out_ref, bundle_ref, other_ref, sems,
):
    pre_part = slice(0, ROWS + 2)
    copies = copy_in(
        [(bundle_hbm.at[:, pre_part], bundle_ref), (other_hbm.at[:, pre_part], other_ref)], sems
    )
    for copy in copies:
        copy.wait()
    gain, shift = row(params_ref, GAIN), row(params_ref, SHIFT)
    for f in range(FRAMES):
        mean, rstd = row(stats_ref, MEAN1 + f), row(stats_ref, RSTD1 + f)
        for strip, pre_ref, come_ref, top, bottom in (
            (0, bundle_ref, incoming_ref, TURN + TOP, TURN + BOTTOM),
            (1, other_ref, arrived_ref, OTHER_TURN + OTHER_TOP, OTHER_TURN + OTHER_BOTTOM),
        ):
            for at, count, mask in ((0, 1, top), (1, ROWS, TURN + LIVE), (1 + ROWS, 1, bottom)):
                pair = fields(
                    pre_ref[f, at : at + count], come_ref[f, at : at + count], mean, rstd, gain, shift,
                    row(params_ref, mask + f),
                )
                for n in range(2):
                    out_ref[strip, n, f, at : at + count] = pair[n].reshape(count, COLS, CH)


def weight_second_kernel(
    scale, chunk, table_ref, fields_ref, params_ref, stats_ref, first_hbm, act_hbm,
    out_hbm, own_hbm, parts_ref, columns_ref, sum_ref, act_ref, first_ref, out_ref, sems,
):
    copies = copy_in([(act_hbm, act_ref), (first_hbm, first_ref)], sems)
    table = jnp.sum(table_ref[...], axis=0)
    parts_ref[...] = table[2:4] * scale
    for strip, top, bottom in ((0, TURN + TOP, TURN + BOTTOM), (1, OTHER_TURN + OTHER_TOP, OTHER_TURN + OTHER_BOTTOM)):
        write_columns(
            store_columns(columns_ref, (strip,)), table[0:2], fields_ref, (strip,), params_ref, stats_ref,
            RSTD1, 1, 1, (top, TURN + LIVE, bottom),
        )
    copy_own = pltpu.make_async_copy(columns_ref.at[0], own_hbm, sems.at[2])
    copy_own.start()
    for copy in copies:
        copy.wait()
    second = row(params_ref, CORE) > 0.5
    filler = jnp.zeros((out_ref.shape[1] - chunk, CH), F32)
    chips = out_ref.shape[0]
    done = 0
    copies = [copy_own]
    for kt in range(3):
        for dy in (-1, 0, 1):
            terms = kernel_terms(columns_ref, act_ref, kt, dy)
            tap = 9 * kt + 3 * (dy + 1)
            for dx in range(3):
                at = (tap + dx) * CH
                sum_ref[at : at + CH] = first_ref[tap + dx] + terms[:, dx * CH : (dx + 1) * CH]
        begin = done
        while done < chips and 2 * (done + 1) * chunk <= 9 * (kt + 1) * CH:
            at = 2 * done * chunk
            mine = jnp.where(second, sum_ref[at + chunk : at + 2 * chunk], sum_ref[at : at + chunk])
            if filler.shape[0]:
                mine = jnp.concatenate([mine, filler], axis=0)
            out_ref[done] = mine.astype(BF16)
            done += 1
        if done > begin:
            send = pltpu.make_async_copy(out_ref.at[begin:done], out_hbm.at[begin:done], sems.at[3 + kt])
            send.start()
            copies.append(send)
    for copy in copies:
        copy.wait()


def conv_second_kernel(params_ref, columns_hbm, first_hbm, taps_ref, out_ref, weight_ref, columns_ref, first_ref, sems):
    for copy in copy_in([(columns_hbm, columns_ref), (first_hbm, first_ref), (taps_ref, weight_ref)], sems):
        copy.wait()
    for f in range(FRAMES):
        out_ref[0, f] = first_ref[f, 1 : 1 + ROWS]
        out_ref[1, f] = conv_frame(
            lambda g, start, size: columns_ref[g, start : start + size], weight_ref, params_ref, 1, f, ROWS
        )


def total_kernel(scale, terms_ref, out_ref):
    chunk = out_ref.shape[0]
    total = jnp.sum(terms_ref[...].astype(F32), axis=0)
    out_ref[...] = (total[0:chunk] * scale).reshape(chunk, 1, CH)


def call(kernel, name, args, outs, scratch=(), specs="", flops=1_000_000):
    specs = specs or "v" * len(args)
    size = sum(a.size * a.dtype.itemsize for a in args)
    space = {"k": pltpu.VMEM, "h": pltpu.HBM}
    args = [pltpu.with_memory_space_constraint(a, space[x]) if x in space else a for a, x in zip(args, specs)]
    return pl.pallas_call(
        kernel,
        out_shape=tuple(outs),
        in_specs=[{"v": VMEM, "k": VMEM, "s": SMEM, "h": HBM}[x] for x in specs],
        out_specs=tuple(HBM if getattr(o, "memory_space", None) is pltpu.HBM else VMEM for o in outs),
        scratch_shapes=list(scratch),
        compiler_params=pltpu.CompilerParams(vmem_limit_bytes=24 * 1024 * 1024),
        cost_estimate=pl.CostEstimate(flops=flops, bytes_accessed=size, transcendentals=0),
        name=name,
    )(*args)


def shape(dims, dtype=F32):
    return jax.ShapeDtypeStruct(dims, dtype)


def kept(dims, dtype=F32):
    return pltpu.VMEM(dims, dtype)


def in_hbm(dims, dtype=F32):
    return pltpu.HBM(dims, dtype)


def local(activations, pre_norm, cot_first, loss_grad, frame_clip, weight, norm_gain, norm_shift):
    dp = lax.axis_size("dp")
    me = lax.axis_index("dp")
    cells = float(dp * ROWS * COLS * PER)
    chips, chunk = dp // 2, TAPS * CH // dp
    padded = -(-chunk // 8) * 8
    other = me ^ 1
    last = lax.axis_index("segment") == lax.axis_size("segment") - 1
    flags = [me != 0, me != dp - 1, other != 0, other != dp - 1, me & 1, last]
    flags = jnp.stack([x.astype(jnp.int32) for x in flags])
    pre, act = pre_norm[0], activations[0]
    cot, loss = cot_first[0], loss_grad[0]
    taps = weight[0].reshape(9, 3, CH, CH).transpose(0, 1, 3, 2).reshape(9, 3 * CH, CH)
    edge = (FRAMES, ROWS + 2, COLS, CH)
    strip = (FRAMES, ROWS, COLS, CH)
    bundled = (FRAMES, 3 * (ROWS + 2) + 2 * ROWS, COLS, CH)
    mates = [(i, i ^ 1) for i in range(dp)]
    columns_of = lambda rows: (FRAMES, rows * COLS, 3 * CH)
    sems = lambda n: pltpu.SemaphoreType.DMA((n,))

    def exchange(table):
        return lax.all_to_all(table, "dp", 0, 0, tiled=True)

    table, head, tail = call(
        sums_kernel, "sums", (pre, cot, loss), (shape((dp, 4, CH)), shape(edge, BF16), shape(edge, BF16)),
        scratch=[pltpu.VMEM((2,) + strip, BF16), sems(9)], specs="hhh",
    )
    table = exchange(table)
    down = lax.ppermute(head, "dp", [(i + 1, i) for i in range(dp - 1)])
    up = lax.ppermute(tail, "dp", [(i, i + 1) for i in range(dp - 1)])

    own, params = call(
        functools.partial(prepare_kernel, cells), "prepare", (flags, frame_clip, pre, cot, norm_gain, norm_shift),
        (kept((2,) + strip), kept((PARAM_ROWS, CH))),
        scratch=[
            pltpu.SMEM((1, 2, 1, FRAMES), jnp.int32), pltpu.VMEM((2,) + strip, BF16), pltpu.VMEM(strip, BF16), sems(5)
        ],
        specs="shhhhh",
    )
    table, stats = call(
        act_first_kernel, "act_first", (table, own, params), (shape((dp, 2, CH)), kept((STAT_ROWS, CH))), specs="vkk"
    )
    table = exchange(table)

    first_fields, bundle, loss_rows = call(
        fields_first_kernel, "fields_first", (up, down, params, stats, pre, cot, loss, act),
        (
            kept((2, FRAMES, ROWS + 4, COLS, CH)), in_hbm(bundled, BF16),
            kept(edge, BF16),
        ),
        scratch=[pltpu.VMEM(strip, BF16)] * 3 + [sems(14)],
        specs="vvkkhhhh",
    )
    other_bundle = lax.ppermute(bundle, "dp", mates)

    weights = pltpu.VMEM((9, 3 * CH, CH), BF16)
    grad_first, value = call(
        conv_first_kernel, "conv_first", (table, first_fields, params, stats, taps),
        (shape(edge, BF16), in_hbm(edge, BF16)),
        scratch=[pltpu.VMEM(columns_of(ROWS + 4), BF16), weights, pltpu.VMEM(edge, BF16), sems(2)],
        specs="vkkkh", flops=20_000_000_000,
    )
    count = lax.axis_size("segment")
    hand = lax.ppermute(grad_first, "segment", [(i + 1, i) for i in range(count - 1)])

    both = pltpu.VMEM((2,) + columns_of(ROWS + 2), BF16)
    acts_dims, taps_dims = (CH, 2 * 9 * CH), (TAPS, CH, CH)
    slope, acts, weight_first = call(
        weight_first_kernel, "weight_first", (table, params, stats, value, bundle, other_bundle),
        (kept((2,) + strip), in_hbm(acts_dims, BF16), in_hbm(taps_dims)),
        scratch=[both, pltpu.VMEM(acts_dims, BF16), pltpu.VMEM(acts_dims, BF16), pltpu.VMEM(taps_dims, F32)]
        + [pltpu.VMEM(edge, BF16)] + [pltpu.VMEM(bundled, BF16)] * 2 + [pltpu.VMEM((2,) + edge, F32), sems(5)],
        specs="vkkhhh",
    )

    table, incoming = call(
        act_second_kernel, "act_second", (hand, loss_rows, slope, params, stats),
        (shape((dp, 4, CH)), shape(edge, BF16)), specs="vkkkk",
    )
    table = exchange(table)
    arrived = lax.ppermute(incoming, "dp", mates)
    (second_fields,) = call(
        fields_second_kernel, "fields_second", (incoming, arrived, bundle, other_bundle, params, stats),
        (kept((2, 2) + edge),), scratch=[pltpu.VMEM(edge, BF16)] * 2 + [sems(2)], specs="vvhhkk",
    )

    terms, columns, parts = call(
        functools.partial(weight_second_kernel, 1.0 / dp, chunk), "weight_second",
        (table, second_fields, params, stats, weight_first, acts),
        (in_hbm((chips, padded, CH), BF16), in_hbm(columns_of(ROWS + 2), BF16), shape((2, CH))),
        scratch=[
            both, pltpu.VMEM((TAPS * CH, CH), F32), pltpu.VMEM(acts_dims, BF16), pltpu.VMEM(taps_dims, F32),
            pltpu.VMEM((chips, padded, CH), BF16), sems(6),
        ],
        specs="vkkkhh",
    )
    sides = [[2 * i + core for i in range(chips)] for core in range(2)]
    terms = lax.all_to_all(terms, "dp", 0, 0, axis_index_groups=sides, tiled=True)
    (grad_weight,) = call(
        functools.partial(total_kernel, 1.0 / dp), "total", (terms,), (shape((chunk, 1, CH)),)
    )
    (grad_inputs,) = call(
        conv_second_kernel, "conv_second", (params, columns, grad_first, taps),
        (shape((2, FRAMES, ROWS, COLS, CH), BF16),),
        scratch=[weights, pltpu.VMEM(columns_of(ROWS + 2), BF16), pltpu.VMEM(edge, BF16), sems(3)], specs="khhh",
    )
    width = CH // dp
    mine = lax.dynamic_slice_in_dim(parts, me * width, width, axis=1)
    return (grad_inputs[None], grad_weight.transpose(1, 0, 2), mine[0:1], mine[1:2])


def solution(mesh):
    in_specs = (
        P("segment", None, None, "dp", None, None),
        P("segment", None, None, "dp", None, None),
        P("segment", None, "dp", None, None),
        P(None, None, "dp", None, None),
        P("segment", None, "dp", None),
        P("segment", None, None),
        P("segment", None),
        P("segment", None),
    )
    out_specs = (
        P("segment", None, None, "dp", None, None),
        P("segment", "dp", None),
        P("segment", "dp"),
        P("segment", "dp"),
    )
    return jax.shard_map(local, mesh=mesh, in_specs=in_specs, out_specs=out_specs, check_vma=False)
```

time: 123 us -> 124 us (level)
  Pallas kernels: 12.8 us -> 42.6 us
  local copies, waits for them, and re-layouts: 18.7 us -> 3.24 us
  waiting for transfers between devices: 38 us -> 24.7 us
  starting transfers between devices: 45.6 us -> 52.1 us
  blocking collectives: 4.43 us -> 0 us
  other arithmetic: 1.98 us -> 0 us
    pallas_call x7 -> x11, Pallas kernels: 12.8 us -> 42.6 us  [call(): pl.pallas_call(kernel, out_shape=tuple(outs), in_specs=[{'v': VMEM, 'k':...]
    unnamed x41 -> x6, local copies, waits for them, and re-layouts: 12.7 us -> 0.91 us
    all_to_all x3, waiting for transfers between devices: 16.5 us -> 8.07 us  [exchange(): return lax.all_to_all(table, 'dp', 0, 0, tiled=True)]
    all_to_all x1 -> x0, blocking collectives: 4.43 us -> none  [local(): lax.all_to_all(terms, 'dp', 0, 0, axis_index_groups=pairs, tiled=True)]
    ppermute x0 -> x2, starting transfers between devices: none -> 4.11 us  [the longest x1 2.06 us: local(): arrived = lax.ppermute(incoming, 'dp', mates)]
    ppermute x1, waiting for transfers between devices: 6.42 us -> 2.4 us  [local(): lax.ppermute(grad_first, 'segment', [(i + 1, i) for i in range(count - 1)])]
    all_to_all x3, starting transfers between devices: 33.9 us -> 36.3 us  [exchange(): return lax.all_to_all(table, 'dp', 0, 0, tiled=True)]
    unnamed x1 -> x0, other arithmetic: 1.34 us -> none
  transfers between devices with their start and end apart: 7 -> 9, of which waited for: 6 -> 5; matrix products, arithmetic and copies ran while one was open for 5% -> 2% of each run, Pallas kernels for 3% -> 28%
where the time goes in v2:
time: 124 us; the launch traced here: 123 us
  starting transfers between devices  52.1 us (42%)
  Pallas kernels  42.6 us (34%)
  waiting for transfers between devices  24.7 us (20%)
  local copies, waits for them, and re-layouts  3.24 us (3%)
    pallas_call x11, Pallas kernels, call(): pl.pallas_call(kernel, out_shape=tuple(outs), in_specs=[{'v': VMEM, 'k':...  42.6 us
    all_to_all x3, starting transfers between devices, exchange(): return lax.all_to_all(table, 'dp', 0, 0, tiled=True)  36.3 us
    all_to_all x1, waiting for transfers between devices, local(): lax.all_to_all(terms, 'dp', 0, 0, axis_index_groups=sides, tiled=True)  13 us
    all_to_all x3, waiting for transfers between devices, exchange(): return lax.all_to_all(table, 'dp', 0, 0, tiled=True)  8.07 us
    all_to_all x1, starting transfers between devices, local(): lax.all_to_all(terms, 'dp', 0, 0, axis_index_groups=sides, tiled=True)  4.81 us
    ppermute x1, starting transfers between devices, local(): down = lax.ppermute(head, 'dp', [(i + 1, i) for i in range(dp - 1)])  3.51 us
  transfers between devices with their start and end apart: 9, of which 5 were waited for; matrix products, arithmetic and copies ran while one was open for 2% of the time, Pallas kernels for 28%

profile of v2, /device:TPU:8, one launch (start us, length us, event | category | flops | bytes accessed | tf_op | source)
XLA Modules:
  0.0 123.5 jit_solution(8892336273574095265)
XLA Ops:
  0.6 0.0 copy-start.2
  0.6 2.0 %sums.1 = (f32[64,4,128]{2,1,0:T(4,128)}, bf16[4,6,32,128]{3,2,1,0:T(8,128)(2,1)S(1)}, bf16[4,6,32,128]{3,2,1,0:T(8,128)(2,1)S(1)}) custom-call(bf16[2,4,4,32,128]{4,3,2,1,0:T(8,128)(2,1)} %bitcast.18, bf16[4,4,32,128]{3,2,1,0:T(8,128)(2,1)} %bitcast.21, bf16[4,4,32,128]{3,2,1,0:T(8,128)(2,1)} %bitcast.25), custom_call_target="tpu_custom_call" | custom-call | flops 1000000 | bytes 524288 | tf_op jit(solution)/shard_map/sums/pallas_call | solution.py:482
  2.7 17.2 %all-to-all-start = ((f32[64,4,128]{2,1,0:T(4,128)}), f32[64,4,128]{2,1,0:T(4,128)S(1)}, u32[]{:S(2)}, u32[]{:S(2)}) async-start(f32[64,4,128]{2,1,0:T(4,128)} %get-tuple-element.25), calls=%async_computation | async-start | bytes 262144 | tf_op jit(solution)/shard_map/all_to_all | solution.py:527
  19.9 2.1 %collective-permute-start = (bf16[4,6,32,128]{3,2,1,0:T(8,128)(2,1)S(1)}, bf16[4,6,32,128]{3,2,1,0:T(8,128)(2,1)S(1)}, u32[]{:S(2)}, u32[]{:S(2)}) collective-permute-start(bf16[4,6,32,128]{3,2,1,0:T(8,128)(2,1)S(1)} %get-tuple-element.28), channel_id=1, source_target_pairs={{0,1},{1,2},{2,3},{3,4},{4,5},{5,6},{6,7},{7,8},{8,9},{9,10},{10,1... | collective-permute-start | bytes 589832 | tf_op jit(solution)/shard_map/ppermute | solution.py:535
  21.9 3.5 %collective-permute-start.1 = (bf16[4,6,32,128]{3,2,1,0:T(8,128)(2,1)S(1)}, bf16[4,6,32,128]{3,2,1,0:T(8,128)(2,1)S(1)}, u32[]{:S(2)}, u32[]{:S(2)}) collective-permute-start(bf16[4,6,32,128]{3,2,1,0:T(8,128)(2,1)S(1)} %get-tuple-element.29), channel_id=1, source_target_pairs={{1,0},{2,1},{3,2},{4,3},{5,4},{6,5},{7,6},{8,7},{9,8},{10,9},{11,1... | collective-permute-start | bytes 589832 | tf_op jit(solution)/shard_map/ppermute | solution.py:534
  25.5 0.1 stack.47.flag_ref
  25.5 1.6 %prepare.1 = (f32[2,4,4,32,128]{4,3,2,1,0:T(8,128)S(1)}, f32[80,128]{1,0:T(8,128)S(1)}) custom-call(s32[6]{0:T(128)S(1)} %stack.47.flag_ref, s32[1,2,1,4]{3,2,1,0:T(1,128)} %clip_hbm.1, bf16[2,4,4,32,128]{4,3,2,1,0:T(8,128)(2,1)} %bitcast.19, bf16[4,4,32,128]{3,2,1,0:T(8,128)(2,1)} %bitcast.22, f32[1,128]{1,0:T(1,128)} %gain_ref.1, f32[1,128]{1,0:T(1,128)} %shift_ref.1), custom_call_target="tpu_custom_call" | custom-call | flops 1000000 | bytes 394296 | tf_op jit(solution)/shard_map/prepare/pallas_call | solution.py:482
  27.2 2.8 %all-to-all-done.table_ref = f32[64,4,128]{2,1,0:T(4,128)S(1)} async-done(((f32[64,4,128]{2,1,0:T(4,128)}), f32[64,4,128]{2,1,0:T(4,128)S(1)}, u32[]{:S(2)}, u32[]{:S(2)}) %all-to-all-start) | async-done | bytes 131104 | tf_op jit(solution)/shard_map/all_to_all | solution.py:527
  30.0 1.2 act_first.1
  31.2 8.8 %all-to-all-start.1 = ((f32[64,2,128]{2,1,0:T(2,128)}), f32[64,2,128]{2,1,0:T(2,128)S(1)}, u32[]{:S(2)}, u32[]{:S(2)}) async-start(f32[64,2,128]{2,1,0:T(2,128)} %get-tuple-element.27), calls=%async_computation.1 | async-start | bytes 131072 | tf_op jit(solution)/shard_map/all_to_all | solution.py:527
  40.0 0.0 copy-done.2
  40.0 1.6 %copy.12 = bf16[9,3,128,128]{2,3,1,0:T(8,128)(2,1)} copy(bf16[9,3,128,128]{3,2,1,0:T(8,128)(2,1)S(1)} %bitcast.24) | data formatting | bytes 1769472 | tf_op jit(solution)/shard_map/reshape;squeeze | solution.py:518
  41.7 0.0 collective-permute-done.up_ref
  41.7 0.0 collective-permute-done.1.down_ref
  41.7 21.1 %fields_first.1 = (f32[2,4,8,32,128]{4,3,2,1,0:T(8,128)S(1)}, bf16[4,26,32,128]{3,2,1,0:T(8,128)(2,1)}, bf16[4,6,32,128]{3,2,1,0:T(8,128)(2,1)S(1)}) custom-call(bf16[4,6,32,128]{3,2,1,0:T(8,128)(2,1)S(1)} %collective-permute-done.up_ref, bf16[4,6,32,128]{3,2,1,0:T(8,128)(2,1)S(1)} %collective-permute-done.1.down_ref, ...), custom_call_target="tpu_custom_call" | custom-call | flops 1000000 | bytes 1232896 | tf_op jit(solution)/shard_map/fields_first/pallas_call | solution.py:482
  62.8 2.1 %collective-permute-start.3 = (bf16[4,26,32,128]{3,2,1,0:T(8,128)(2,1)}, bf16[4,26,32,128]{3,2,1,0:T(8,128)(2,1)S(1)}, u32[]{:S(2)}, u32[]{:S(2)}) collective-permute-start(bf16[4,26,32,128]{3,2,1,0:T(8,128)(2,1)} %get-tuple-element.35.bundle_hbm), channel_id=1, source_target_pairs={{0,1},{1,0},{2,3},{3,2},{4,5},{5,4},{6,7},{7,6},{8,9},{9,8},{10,11... | collective-permute-start | bytes 2555912 | tf_op jit(solution)/shard_map/ppermute | solution.py:559
  64.8 0.0 all-to-all-done.1.table_ref
  64.8 2.4 %conv_first.1 = (bf16[4,6,32,128]{3,2,1,0:T(8,128)(2,1)S(1)}, bf16[4,6,32,128]{3,2,1,0:T(8,128)(2,1)}) custom-call(f32[64,2,128]{2,1,0:T(2,128)S(1)} %all-to-all-done.1.table_ref, f32[2,4,8,32,128]{4,3,2,1,0:T(8,128)S(1)} %get-tuple-element.31.fields_ref, f32[80,128]{1,0:T(8,128)S(1)} %get-tuple-element.24.params_ref, ...), custom_call_target="tpu_custom_call" | custom-call | flops 20000000000 | bytes 2052096 | tf_op jit(solution)/shard_map/conv_first/pallas_call | solution.py:482
  67.2 0.0 copy-start
  67.2 1.3 %collective-permute-start.2 = (bf16[4,6,32,128]{3,2,1,0:T(8,128)(2,1)S(1)}, bf16[4,6,32,128]{3,2,1,0:T(8,128)(2,1)S(1)}, u32[]{:S(2)}, u32[]{:S(2)}) collective-permute-start(bf16[4,6,32,128]{3,2,1,0:T(8,128)(2,1)S(1)} %get-tuple-element.32.first_hbm), channel_id=1, source_target_pairs={{64,0},{128,64},{192,128},{256,192},{320,256},{384,320},{448,384},... | collective-permute-start | bytes 589832 | tf_op jit(solution)/shard_map/ppermute | solution.py:569
  68.5 0.0 collective-permute-done.3.other_hbm
  68.5 0.0 copy-start.1
  68.6 0.9 copy-done.1
  69.5 4.4 %weight_first.1 = (f32[2,4,4,32,128]{4,3,2,1,0:T(8,128)S(1)}, bf16[128,2304]{1,0:T(8,128)(2,1)}, f32[27,128,128]{2,1,0:T(8,128)}) custom-call(f32[64,2,128]{2,1,0:T(2,128)S(1)} %all-to-all-done.1.table_ref, f32[80,128]{1,0:T(8,128)S(1)} %get-tuple-element.24.params_ref, f32[24,128]{1,0:T(8,128)S(1)} %get-tuple-element.30.stats_ref, ...), custom_call_target="tpu_custom_call" | custom-call | flops 1000000 | bytes 2019328 | tf_op jit(solution)/shard_map/weight_first/pallas_call | solution.py:482
  73.9 2.4 %collective-permute-done.2.hand_ref = bf16[4,6,32,128]{3,2,1,0:T(8,128)(2,1)S(1)} collective-permute-done((bf16[4,6,32,128]{3,2,1,0:T(8,128)(2,1)S(1)}, bf16[4,6,32,128]{3,2,1,0:T(8,128)(2,1)S(1)}, u32[]{:S(2)}, u32[]{:S(2)}) %collective-permute-start.2) | collective-permute-done | bytes 196640 | tf_op jit(solution)/shard_map/ppermute | solution.py:569
  76.3 0.9 act_second.1
  77.2 10.3 %all-to-all-start.2 = ((f32[64,4,128]{2,1,0:T(4,128)}), f32[64,4,128]{2,1,0:T(4,128)S(1)}, u32[]{:S(2)}, u32[]{:S(2)}) async-start(f32[64,4,128]{2,1,0:T(4,128)} %get-tuple-element.37), calls=%async_computation.2 | async-start | bytes 262144 | tf_op jit(solution)/shard_map/all_to_all | solution.py:527
  87.6 2.1 %collective-permute-start.4 = (bf16[4,6,32,128]{3,2,1,0:T(8,128)(2,1)S(1)}, bf16[4,6,32,128]{3,2,1,0:T(8,128)(2,1)S(1)}, u32[]{:S(2)}, u32[]{:S(2)}) collective-permute-start(bf16[4,6,32,128]{3,2,1,0:T(8,128)(2,1)S(1)} %get-tuple-element.38.incoming_ref), channel_id=1, source_target_pairs={{0,1},{1,0},{2,3},{3,2},{4,5},{5,4},{6,7},{7,6},{8,9},{9,8},{10,11... | collective-permute-start | bytes 589832 | tf_op jit(solution)/shard_map/ppermute | solution.py:586
  89.6 1.3 %collective-permute-done.4.arrived_ref = bf16[4,6,32,128]{3,2,1,0:T(8,128)(2,1)S(1)} collective-permute-done((bf16[4,6,32,128]{3,2,1,0:T(8,128)(2,1)S(1)}, bf16[4,6,32,128]{3,2,1,0:T(8,128)(2,1)S(1)}, u32[]{:S(2)}, u32[]{:S(2)}) %collective-permute-start.4) | collective-permute-done | bytes 196640 | tf_op jit(solution)/shard_map/ppermute | solution.py:586
  90.9 1.5 %fields_second.1.fields_ref = f32[2,2,4,6,32,128]{5,4,3,2,1,0:T(8,128)S(1)} custom-call(bf16[4,6,32,128]{3,2,1,0:T(8,128)(2,1)S(1)} %get-tuple-element.38.incoming_ref, bf16[4,6,32,128]{3,2,1,0:T(8,128)(2,1)S(1)} %collective-permute-done.4.arrived_ref, bf16[4,26,32,128]{3,2,1,0:T(8,128)(2,1)} %get-tuple-element.35.bundle_hbm, ...), custom_call_target="tpu_custom_call" | custom-call | flops 1000000 | bytes 2150400 | tf_op jit(solution)/shard_map/fields_second/pallas_call | solution.py:482
  92.4 0.0 copy-done
  92.4 5.2 %all-to-all-done.2.table_ref = f32[64,4,128]{2,1,0:T(4,128)S(1)} async-done(((f32[64,4,128]{2,1,0:T(4,128)}), f32[64,4,128]{2,1,0:T(4,128)S(1)}, u32[]{:S(2)}, u32[]{:S(2)}) %all-to-all-start.2) | async-done | bytes 131104 | tf_op jit(solution)/shard_map/all_to_all | solution.py:527
  97.6 3.8 %weight_second.1 = (bf16[32,56,128]{2,1,0:T(8,128)(2,1)}, bf16[4,192,384]{2,1,0:T(8,128)(2,1)}, f32[2,128]{1,0:T(2,128)S(1)}) custom-call(f32[64,4,128]{2,1,0:T(4,128)S(1)} %all-to-all-done.2.table_ref, f32[2,2,4,6,32,128]{5,4,3,2,1,0:T(8,128)S(1)} %fields_second.1.fields_ref, f32[80,128]{1,0:T(8,128)S(1)} %get-tuple-element.24.params_ref, ...), custom_call_target="tpu_custom_call" | custom-call | flops 1000000 | bytes 4116480 | tf_op jit(solution)/shard_map/weight_second/pallas_call | solution.py:482
  101.4 4.8 %all-to-all-start.3 = ((bf16[32,56,128]{2,1,0:T(8,128)(2,1)}), bf16[32,56,128]{2,1,0:T(8,128)(2,1)S(1)}, u32[]{:S(2)}, u32[]{:S(2)}) async-start(bf16[32,56,128]{2,1,0:T(8,128)(2,1)} %get-tuple-element.42), calls=%async_computation.3 | async-start | bytes 917504 | tf_op jit(solution)/shard_map/all_to_all | solution.py:603
  106.2 3.0 %conv_second.1 = bf16[2,4,4,32,128]{4,3,2,1,0:T(8,128)(2,1)} custom-call(f32[80,128]{1,0:T(8,128)S(1)} %get-tuple-element.24.params_ref, bf16[4,192,384]{2,1,0:T(8,128)(2,1)} %get-tuple-element.41.columns_hbm, bf16[4,6,32,128]{3,2,1,0:T(8,128)(2,1)} %copy-done, bf16[9,384,128]{2,1,0:T(8,128)(2,1)} %bitcast.17), custom_call_target="tpu_custom_call" | custom-call | flops 1000000 | bytes 1712128 | tf_op jit(solution)/shard_map/conv_second/pallas_call | solution.py:482
  109.2 0.1 constant_dynamic-slice_fusion
  109.3 0.5 fusion
  109.8 13.0 %all-to-all-done.3.terms_ref = bf16[32,56,128]{2,1,0:T(8,128)(2,1)S(1)} async-done(((bf16[32,56,128]{2,1,0:T(8,128)(2,1)}), bf16[32,56,128]{2,1,0:T(8,128)(2,1)S(1)}, u32[]{:S(2)}, u32[]{:S(2)}) %all-to-all-start.3) | async-done | bytes 458784 | tf_op jit(solution)/shard_map/all_to_all | solution.py:603
  122.8 0.7 total.1
Async XLA Ops:
  0.6 39.4 %copy-start.2 = (bf16[1,3456,128]{2,1,0:T(8,128)(2,1)S(1)}, bf16[1,3456,128]{2,1,0:T(8,128)(2,1)}, u32[]{:S(2)}) copy-start(bf16[1,3456,128]{2,1,0:T(8,128)(2,1)} %param.13) | copy-start | bytes 2654212
  2.7 27.3 %all-to-all-start = ((f32[64,4,128]{2,1,0:T(4,128)}), f32[64,4,128]{2,1,0:T(4,128)S(1)}, u32[]{:S(2)}, u32[]{:S(2)}) async-start(f32[64,4,128]{2,1,0:T(4,128)} %get-tuple-element.25), calls=%async_computation | async-start | bytes 262144 | tf_op jit(solution)/shard_map/all_to_all | solution.py:527
  19.9 21.8 %collective-permute-start = (bf16[4,6,32,128]{3,2,1,0:T(8,128)(2,1)S(1)}, bf16[4,6,32,128]{3,2,1,0:T(8,128)(2,1)S(1)}, u32[]{:S(2)}, u32[]{:S(2)}) collective-permute-start(bf16[4,6,32,128]{3,2,1,0:T(8,128)(2,1)S(1)} %get-tuple-element.28), channel_id=1, source_target_pairs={{0,1},{1,2},{2,3},{3,4},{4,5},{5,6},{6,7},{7,8},{8,9},{9,10},{10,1... | collective-permute-start | bytes 589832 | tf_op jit(solution)/shard_map/ppermute | solution.py:535
  21.9 19.7 %collective-permute-start.1 = (bf16[4,6,32,128]{3,2,1,0:T(8,128)(2,1)S(1)}, bf16[4,6,32,128]{3,2,1,0:T(8,128)(2,1)S(1)}, u32[]{:S(2)}, u32[]{:S(2)}) collective-permute-start(bf16[4,6,32,128]{3,2,1,0:T(8,128)(2,1)S(1)} %get-tuple-element.29), channel_id=1, source_target_pairs={{1,0},{2,1},{3,2},{4,3},{5,4},{6,5},{7,6},{8,7},{9,8},{10,9},{11,1... | collective-permute-start | bytes 589832 | tf_op jit(solution)/shard_map/ppermute | solution.py:534
  31.2 33.6 %all-to-all-start.1 = ((f32[64,2,128]{2,1,0:T(2,128)}), f32[64,2,128]{2,1,0:T(2,128)S(1)}, u32[]{:S(2)}, u32[]{:S(2)}) async-start(f32[64,2,128]{2,1,0:T(2,128)} %get-tuple-element.27), calls=%async_computation.1 | async-start | bytes 131072 | tf_op jit(solution)/shard_map/all_to_all | solution.py:527
  62.8 5.8 %collective-permute-start.3 = (bf16[4,26,32,128]{3,2,1,0:T(8,128)(2,1)}, bf16[4,26,32,128]{3,2,1,0:T(8,128)(2,1)S(1)}, u32[]{:S(2)}, u32[]{:S(2)}) collective-permute-start(bf16[4,26,32,128]{3,2,1,0:T(8,128)(2,1)} %get-tuple-element.35.bundle_hbm), channel_id=1, source_target_pairs={{0,1},{1,0},{2,3},{3,2},{4,5},{5,4},{6,7},{7,6},{8,9},{9,8},{10,11... | collective-permute-start | bytes 2555912 | tf_op jit(solution)/shard_map/ppermute | solution.py:559
  67.2 25.1 %copy-start = (bf16[4,6,32,128]{3,2,1,0:T(8,128)(2,1)}, bf16[4,6,32,128]{3,2,1,0:T(8,128)(2,1)S(1)}, u32[]{:S(2)}) copy-start(bf16[4,6,32,128]{3,2,1,0:T(8,128)(2,1)S(1)} %get-tuple-element.32.first_hbm) | copy-start | bytes 589828
  67.2 9.1 %collective-permute-start.2 = (bf16[4,6,32,128]{3,2,1,0:T(8,128)(2,1)S(1)}, bf16[4,6,32,128]{3,2,1,0:T(8,128)(2,1)S(1)}, u32[]{:S(2)}, u32[]{:S(2)}) collective-permute-start(bf16[4,6,32,128]{3,2,1,0:T(8,128)(2,1)S(1)} %get-tuple-element.32.first_hbm), channel_id=1, source_target_pairs={{64,0},{128,64},{192,128},{256,192},{320,256},{384,320},{448,384},... | collective-permute-start | bytes 589832 | tf_op jit(solution)/shard_map/ppermute | solution.py:569
  68.5 0.9 copy-start.1
  77.2 20.4 %all-to-all-start.2 = ((f32[64,4,128]{2,1,0:T(4,128)}), f32[64,4,128]{2,1,0:T(4,128)S(1)}, u32[]{:S(2)}, u32[]{:S(2)}) async-start(f32[64,4,128]{2,1,0:T(4,128)} %get-tuple-element.37), calls=%async_computation.2 | async-start | bytes 262144 | tf_op jit(solution)/shard_map/all_to_all | solution.py:527
  87.6 3.3 %collective-permute-start.4 = (bf16[4,6,32,128]{3,2,1,0:T(8,128)(2,1)S(1)}, bf16[4,6,32,128]{3,2,1,0:T(8,128)(2,1)S(1)}, u32[]{:S(2)}, u32[]{:S(2)}) collective-permute-start(bf16[4,6,32,128]{3,2,1,0:T(8,128)(2,1)S(1)} %get-tuple-element.38.incoming_ref), channel_id=1, source_target_pairs={{0,1},{1,0},{2,3},{3,2},{4,5},{5,4},{6,7},{7,6},{8,9},{9,8},{10,11... | collective-permute-start | bytes 589832 | tf_op jit(solution)/shard_map/ppermute | solution.py:586
  101.4 21.4 %all-to-all-start.3 = ((bf16[32,56,128]{2,1,0:T(8,128)(2,1)}), bf16[32,56,128]{2,1,0:T(8,128)(2,1)S(1)}, u32[]{:S(2)}, u32[]{:S(2)}) async-start(bf16[32,56,128]{2,1,0:T(8,128)(2,1)} %get-tuple-element.42), calls=%async_computation.3 | async-start | bytes 917504 | tf_op jit(solution)/shard_map/all_to_all | solution.py:603

commit v3 on v2

--- a/solution.py
+++ b/solution.py
@@ -197,22 +197,24 @@
 
 def fields_first_kernel(
     up_ref, down_ref, params_ref, stats_ref, pre_ref, cot_ref, loss_ref, act_ref,
-    out_ref, bundle_ref, loss_out_ref, held_pre, held_cot, held_loss, sems,
+    out_ref, bundle_hbm, loss_out_ref, bundle_ref, held_loss, sems,
 ):
-    pairs = [
-        (pre_ref.at[0], held_pre), (cot_ref, held_cot), (loss_ref, held_loss),
-        (act_ref.at[0], bundle_ref.at[:, 6 : 6 + ROWS]), (act_ref.at[1], bundle_ref.at[:, 6 + ROWS : 6 + 2 * ROWS]),
-    ]
-    for at, edge, own in ((0, 4, pre_ref.at[1]), (14, 1, pre_ref.at[0]), (20, 3, cot_ref)):
-        below = 0 if at == 14 else 2 if at == 20 else 4
-        pairs += [
-            (up_ref.at[:, edge : edge + 1], bundle_ref.at[:, at : at + 1]),
-            (own, bundle_ref.at[:, at + 1 : at + 1 + ROWS]),
-            (down_ref.at[:, below : below + 1], bundle_ref.at[:, at + 1 + ROWS : at + 2 + ROWS]),
-        ]
-    copies = copy_in(pairs, sems)
-    for copy in copies[:3]:
+    copies = copy_in(
+        [
+            (pre_ref.at[0], bundle_ref.at[:, 15 : 15 + ROWS]), (cot_ref, bundle_ref.at[:, 21 : 21 + ROWS]),
+            (loss_ref, held_loss), (pre_ref.at[1], bundle_ref.at[:, 1 : 1 + ROWS]),
+            (act_ref.at[0], bundle_ref.at[:, 6 : 6 + ROWS]),
+            (act_ref.at[1], bundle_ref.at[:, 6 + ROWS : 6 + 2 * ROWS]),
+        ],
+        sems,
+    )
+    for at, edge, below in ((0, 4, 4), (14, 1, 0), (20, 3, 2)):
+        bundle_ref[:, at : at + 1] = up_ref[:, edge : edge + 1]
+        bundle_ref[:, at + 1 + ROWS : at + 2 + ROWS] = down_ref[:, below : below + 1]
+    for copy in copies:
         copy.wait()
+    bundle_out = pltpu.make_async_copy(bundle_ref, bundle_hbm, sems.at[6])
+    bundle_out.start()
     gain, shift = row(params_ref, GAIN), row(params_ref, SHIFT)
     last = row(params_ref, LAST).reshape(1, 1, 1, CH)
     loss_out_ref[:, 0:1] = (up_ref[:, 5:6].astype(F32) * last).astype(BF16)
@@ -222,14 +224,13 @@
         mean, rstd = row(stats_ref, MEAN0 + f), row(stats_ref, RSTD0 + f)
         for at, count, pre, cot, mask in (
             (0, 2, up_ref[f, 0:2], up_ref[f, 2:4], TOP),
-            (2, ROWS, held_pre[f], held_cot[f], LIVE),
+            (2, ROWS, bundle_ref[f, 15 : 15 + ROWS], bundle_ref[f, 21 : 21 + ROWS], LIVE),
             (2 + ROWS, 2, down_ref[f, 0:2], down_ref[f, 2:4], BOTTOM),
         ):
             pair = fields(pre, cot, mean, rstd, gain, shift, row(params_ref, mask + f))
             for n in range(2):
                 out_ref[n, f, at : at + count] = pair[n].reshape(count, COLS, CH)
-    for copy in copies[3:]:
-        copy.wait()
+    bundle_out.wait()
 
 
 def write_columns(store, table, fields_ref, at_fields, params_ref, stats_ref, rstd_at, turn, halo, masks):
@@ -553,7 +554,7 @@
             kept((2, FRAMES, ROWS + 4, COLS, CH)), in_hbm(bundled, BF16),
             kept(edge, BF16),
         ),
-        scratch=[pltpu.VMEM(strip, BF16)] * 3 + [sems(14)],
+        scratch=[pltpu.VMEM(bundled, BF16), pltpu.VMEM(strip, BF16), sems(7)],
         specs="vvkkhhhh",
     )
     other_bundle = lax.ppermute(bundle, "dp", mates)

time: 124 us -> 105 us (0.85)
  Pallas kernels: 42.6 us -> 23.7 us
  starting transfers between devices: 52.1 us -> 49.3 us
  waiting for transfers between devices: 24.7 us -> 27.5 us
    pallas_call x11, Pallas kernels: 42.6 us -> 23.7 us  [call(): pl.pallas_call(kernel, out_shape=tuple(outs), in_specs=[{'v': VMEM, 'k':...]
    all_to_all x3, waiting for transfers between devices: 8.07 us -> 11.1 us  [exchange(): return lax.all_to_all(table, 'dp', 0, 0, tiled=True)]
    all_to_all x3, starting transfers between devices: 36.3 us -> 33.5 us  [exchange(): return lax.all_to_all(table, 'dp', 0, 0, tiled=True)]
  transfers between devices with their start and end apart: 9 -> 9, of which waited for: 5 -> 6; matrix products, arithmetic and copies ran while one was open for 2% -> 2% of each run, Pallas kernels for 28% -> 16%
where the time goes in v3:
time: 105 us
  starting transfers between devices  49.3 us (47%)
  waiting for transfers between devices  27.5 us (26%)
  Pallas kernels  23.7 us (23%)
  local copies, waits for them, and re-layouts  3.24 us (3%)
    all_to_all x3, starting transfers between devices, exchange(): return lax.all_to_all(table, 'dp', 0, 0, tiled=True)  33.5 us
    pallas_call x11, Pallas kernels, call(): pl.pallas_call(kernel, out_shape=tuple(outs), in_specs=[{'v': VMEM, 'k':...  23.7 us
    all_to_all x1, waiting for transfers between devices, local(): lax.all_to_all(terms, 'dp', 0, 0, axis_index_groups=sides, tiled=True)  13 us
    all_to_all x3, waiting for transfers between devices, exchange(): return lax.all_to_all(table, 'dp', 0, 0, tiled=True)  11.1 us
    all_to_all x1, starting transfers between devices, local(): lax.all_to_all(terms, 'dp', 0, 0, axis_index_groups=sides, tiled=True)  4.81 us
    ppermute x1, starting transfers between devices, local(): down = lax.ppermute(head, 'dp', [(i + 1, i) for i in range(dp - 1)])  3.51 us
    ppermute x1, waiting for transfers between devices, local(): lax.ppermute(grad_first, 'segment', [(i + 1, i) for i in range(count - 1)])  2.15 us
  transfers between devices with their start and end apart: 9, of which 6 were waited for; matrix products, arithmetic and copies ran while one was open for 2% of the time, Pallas kernels for 16%

profile of v3, /device:TPU:8, one launch (start us, length us, event | category | flops | bytes accessed | tf_op | source)
XLA Modules:
  0.0 104.6 jit_solution(12513071818726896741)
XLA Ops:
  0.6 0.0 copy-start.2
  0.6 2.0 %sums.1 = (f32[64,4,128]{2,1,0:T(4,128)}, bf16[4,6,32,128]{3,2,1,0:T(8,128)(2,1)S(1)}, bf16[4,6,32,128]{3,2,1,0:T(8,128)(2,1)S(1)}) custom-call(bf16[2,4,4,32,128]{4,3,2,1,0:T(8,128)(2,1)} %bitcast.18, bf16[4,4,32,128]{3,2,1,0:T(8,128)(2,1)} %bitcast.21, bf16[4,4,32,128]{3,2,1,0:T(8,128)(2,1)} %bitcast.25), custom_call_target="tpu_custom_call" | custom-call | flops 1000000 | bytes 524288 | tf_op jit(solution)/shard_map/sums/pallas_call | solution.py:483
  2.7 17.2 %all-to-all-start = ((f32[64,4,128]{2,1,0:T(4,128)}), f32[64,4,128]{2,1,0:T(4,128)S(1)}, u32[]{:S(2)}, u32[]{:S(2)}) async-start(f32[64,4,128]{2,1,0:T(4,128)} %get-tuple-element.25), calls=%async_computation | async-start | bytes 262144 | tf_op jit(solution)/shard_map/all_to_all | solution.py:528
  19.9 2.1 %collective-permute-start = (bf16[4,6,32,128]{3,2,1,0:T(8,128)(2,1)S(1)}, bf16[4,6,32,128]{3,2,1,0:T(8,128)(2,1)S(1)}, u32[]{:S(2)}, u32[]{:S(2)}) collective-permute-start(bf16[4,6,32,128]{3,2,1,0:T(8,128)(2,1)S(1)} %get-tuple-element.28), channel_id=1, source_target_pairs={{0,1},{1,2},{2,3},{3,4},{4,5},{5,6},{6,7},{7,8},{8,9},{9,10},{10,1... | collective-permute-start | bytes 589832 | tf_op jit(solution)/shard_map/ppermute | solution.py:536
  21.9 3.5 %collective-permute-start.1 = (bf16[4,6,32,128]{3,2,1,0:T(8,128)(2,1)S(1)}, bf16[4,6,32,128]{3,2,1,0:T(8,128)(2,1)S(1)}, u32[]{:S(2)}, u32[]{:S(2)}) collective-permute-start(bf16[4,6,32,128]{3,2,1,0:T(8,128)(2,1)S(1)} %get-tuple-element.29), channel_id=1, source_target_pairs={{1,0},{2,1},{3,2},{4,3},{5,4},{6,5},{7,6},{8,7},{9,8},{10,9},{11,1... | collective-permute-start | bytes 589832 | tf_op jit(solution)/shard_map/ppermute | solution.py:535
  25.5 0.1 stack.47.flag_ref
  25.5 1.6 %prepare.1 = (f32[2,4,4,32,128]{4,3,2,1,0:T(8,128)S(1)}, f32[80,128]{1,0:T(8,128)S(1)}) custom-call(s32[6]{0:T(128)S(1)} %stack.47.flag_ref, s32[1,2,1,4]{3,2,1,0:T(1,128)} %clip_hbm.1, bf16[2,4,4,32,128]{4,3,2,1,0:T(8,128)(2,1)} %bitcast.19, bf16[4,4,32,128]{3,2,1,0:T(8,128)(2,1)} %bitcast.22, f32[1,128]{1,0:T(1,128)} %gain_ref.1, f32[1,128]{1,0:T(1,128)} %shift_ref.1), custom_call_target="tpu_custom_call" | custom-call | flops 1000000 | bytes 394296 | tf_op jit(solution)/shard_map/prepare/pallas_call | solution.py:483
  27.2 2.8 %all-to-all-done.table_ref = f32[64,4,128]{2,1,0:T(4,128)S(1)} async-done(((f32[64,4,128]{2,1,0:T(4,128)}), f32[64,4,128]{2,1,0:T(4,128)S(1)}, u32[]{:S(2)}, u32[]{:S(2)}) %all-to-all-start) | async-done | bytes 131104 | tf_op jit(solution)/shard_map/all_to_all | solution.py:528
  30.0 1.2 %act_first.1 = (f32[64,2,128]{2,1,0:T(2,128)}, f32[24,128]{1,0:T(8,128)S(1)}) custom-call(f32[64,4,128]{2,1,0:T(4,128)S(1)} %all-to-all-done.table_ref, f32[2,4,4,32,128]{4,3,2,1,0:T(8,128)S(1)} %get-tuple-element.26.own_ref, f32[80,128]{1,0:T(8,128)S(1)} %get-tuple-element.24.params_ref), custom_call_target="tpu_custom_call" | custom-call | flops 1000000 | bytes 696320 | tf_op jit(solution)/shard_map/act_first/pallas_call | solution.py:483
  31.2 8.8 %all-to-all-start.1 = ((f32[64,2,128]{2,1,0:T(2,128)}), f32[64,2,128]{2,1,0:T(2,128)S(1)}, u32[]{:S(2)}, u32[]{:S(2)}) async-start(f32[64,2,128]{2,1,0:T(2,128)} %get-tuple-element.27), calls=%async_computation.1 | async-start | bytes 131072 | tf_op jit(solution)/shard_map/all_to_all | solution.py:528
  40.0 0.0 copy-done.2
  40.0 1.6 %copy.12 = bf16[9,3,128,128]{2,3,1,0:T(8,128)(2,1)} copy(bf16[9,3,128,128]{3,2,1,0:T(8,128)(2,1)S(1)} %bitcast.24) | data formatting | bytes 1769472 | tf_op jit(solution)/shard_map/reshape;squeeze | solution.py:519
  41.7 0.0 collective-permute-done.up_ref
  41.7 0.0 collective-permute-done.1.down_ref
  41.7 2.2 %fields_first.1 = (f32[2,4,8,32,128]{4,3,2,1,0:T(8,128)S(1)}, bf16[4,26,32,128]{3,2,1,0:T(8,128)(2,1)}, bf16[4,6,32,128]{3,2,1,0:T(8,128)(2,1)S(1)}) custom-call(bf16[4,6,32,128]{3,2,1,0:T(8,128)(2,1)S(1)} %collective-permute-done.up_ref, bf16[4,6,32,128]{3,2,1,0:T(8,128)(2,1)S(1)} %collective-permute-done.1.down_ref, ...), custom_call_target="tpu_custom_call" | custom-call | flops 1000000 | bytes 1232896 | tf_op jit(solution)/shard_map/fields_first/pallas_call | solution.py:483
  43.9 2.1 %collective-permute-start.3 = (bf16[4,26,32,128]{3,2,1,0:T(8,128)(2,1)}, bf16[4,26,32,128]{3,2,1,0:T(8,128)(2,1)S(1)}, u32[]{:S(2)}, u32[]{:S(2)}) collective-permute-start(bf16[4,26,32,128]{3,2,1,0:T(8,128)(2,1)} %get-tuple-element.35.bundle_hbm), channel_id=1, source_target_pairs={{0,1},{1,0},{2,3},{3,2},{4,5},{5,4},{6,7},{7,6},{8,9},{9,8},{10,11... | collective-permute-start | bytes 2555912 | tf_op jit(solution)/shard_map/ppermute | solution.py:560
  45.9 3.0 %all-to-all-done.1.table_ref = f32[64,2,128]{2,1,0:T(2,128)S(1)} async-done(((f32[64,2,128]{2,1,0:T(2,128)}), f32[64,2,128]{2,1,0:T(2,128)S(1)}, u32[]{:S(2)}, u32[]{:S(2)}) %all-to-all-start.1) | async-done | bytes 65568 | tf_op jit(solution)/shard_map/all_to_all | solution.py:528
  49.0 2.4 %conv_first.1 = (bf16[4,6,32,128]{3,2,1,0:T(8,128)(2,1)S(1)}, bf16[4,6,32,128]{3,2,1,0:T(8,128)(2,1)}) custom-call(f32[64,2,128]{2,1,0:T(2,128)S(1)} %all-to-all-done.1.table_ref, f32[2,4,8,32,128]{4,3,2,1,0:T(8,128)S(1)} %get-tuple-element.31.fields_ref, f32[80,128]{1,0:T(8,128)S(1)} %get-tuple-element.24.params_ref, ...), custom_call_target="tpu_custom_call" | custom-call | flops 20000000000 | bytes 2052096 | tf_op jit(solution)/shard_map/conv_first/pallas_call | solution.py:483
  51.3 0.0 copy-start
  51.4 1.3 %collective-permute-start.2 = (bf16[4,6,32,128]{3,2,1,0:T(8,128)(2,1)S(1)}, bf16[4,6,32,128]{3,2,1,0:T(8,128)(2,1)S(1)}, u32[]{:S(2)}, u32[]{:S(2)}) collective-permute-start(bf16[4,6,32,128]{3,2,1,0:T(8,128)(2,1)S(1)} %get-tuple-element.32.first_hbm), channel_id=1, source_target_pairs={{64,0},{128,64},{192,128},{256,192},{320,256},{384,320},{448,384},... | collective-permute-start | bytes 589832 | tf_op jit(solution)/shard_map/ppermute | solution.py:570
  52.7 0.0 collective-permute-done.3.other_hbm
  52.7 0.0 copy-start.1
  52.7 0.9 copy-done.1
  53.6 4.4 %weight_first.1 = (f32[2,4,4,32,128]{4,3,2,1,0:T(8,128)S(1)}, bf16[128,2304]{1,0:T(8,128)(2,1)}, f32[27,128,128]{2,1,0:T(8,128)}) custom-call(f32[64,2,128]{2,1,0:T(2,128)S(1)} %all-to-all-done.1.table_ref, f32[80,128]{1,0:T(8,128)S(1)} %get-tuple-element.24.params_ref, f32[24,128]{1,0:T(8,128)S(1)} %get-tuple-element.30.stats_ref, ...), custom_call_target="tpu_custom_call" | custom-call | flops 1000000 | bytes 2019328 | tf_op jit(solution)/shard_map/weight_first/pallas_call | solution.py:483
  58.0 2.1 %collective-permute-done.2.hand_ref = bf16[4,6,32,128]{3,2,1,0:T(8,128)(2,1)S(1)} collective-permute-done((bf16[4,6,32,128]{3,2,1,0:T(8,128)(2,1)S(1)}, bf16[4,6,32,128]{3,2,1,0:T(8,128)(2,1)S(1)}, u32[]{:S(2)}, u32[]{:S(2)}) %collective-permute-start.2) | collective-permute-done | bytes 196640 | tf_op jit(solution)/shard_map/ppermute | solution.py:570
  60.2 0.9 act_second.1
  61.1 7.5 %all-to-all-start.2 = ((f32[64,4,128]{2,1,0:T(4,128)}), f32[64,4,128]{2,1,0:T(4,128)S(1)}, u32[]{:S(2)}, u32[]{:S(2)}) async-start(f32[64,4,128]{2,1,0:T(4,128)} %get-tuple-element.37), calls=%async_computation.2 | async-start | bytes 262144 | tf_op jit(solution)/shard_map/all_to_all | solution.py:528
  68.7 2.1 %collective-permute-start.4 = (bf16[4,6,32,128]{3,2,1,0:T(8,128)(2,1)S(1)}, bf16[4,6,32,128]{3,2,1,0:T(8,128)(2,1)S(1)}, u32[]{:S(2)}, u32[]{:S(2)}) collective-permute-start(bf16[4,6,32,128]{3,2,1,0:T(8,128)(2,1)S(1)} %get-tuple-element.38.incoming_ref), channel_id=1, source_target_pairs={{0,1},{1,0},{2,3},{3,2},{4,5},{5,4},{6,7},{7,6},{8,9},{9,8},{10,11... | collective-permute-start | bytes 589832 | tf_op jit(solution)/shard_map/ppermute | solution.py:587
  70.7 1.3 %collective-permute-done.4.arrived_ref = bf16[4,6,32,128]{3,2,1,0:T(8,128)(2,1)S(1)} collective-permute-done((bf16[4,6,32,128]{3,2,1,0:T(8,128)(2,1)S(1)}, bf16[4,6,32,128]{3,2,1,0:T(8,128)(2,1)S(1)}, u32[]{:S(2)}, u32[]{:S(2)}) %collective-permute-start.4) | collective-permute-done | bytes 196640 | tf_op jit(solution)/shard_map/ppermute | solution.py:587
  72.0 1.5 %fields_second.1.fields_ref = f32[2,2,4,6,32,128]{5,4,3,2,1,0:T(8,128)S(1)} custom-call(bf16[4,6,32,128]{3,2,1,0:T(8,128)(2,1)S(1)} %get-tuple-element.38.incoming_ref, bf16[4,6,32,128]{3,2,1,0:T(8,128)(2,1)S(1)} %collective-permute-done.4.arrived_ref, bf16[4,26,32,128]{3,2,1,0:T(8,128)(2,1)} %get-tuple-element.35.bundle_hbm, ...), custom_call_target="tpu_custom_call" | custom-call | flops 1000000 | bytes 2150400 | tf_op jit(solution)/shard_map/fields_second/pallas_call | solution.py:483
  73.5 0.0 copy-done
  73.5 5.2 %all-to-all-done.2.table_ref = f32[64,4,128]{2,1,0:T(4,128)S(1)} async-done(((f32[64,4,128]{2,1,0:T(4,128)}), f32[64,4,128]{2,1,0:T(4,128)S(1)}, u32[]{:S(2)}, u32[]{:S(2)}) %all-to-all-start.2) | async-done | bytes 131104 | tf_op jit(solution)/shard_map/all_to_all | solution.py:528
  78.7 3.8 %weight_second.1 = (bf16[32,56,128]{2,1,0:T(8,128)(2,1)}, bf16[4,192,384]{2,1,0:T(8,128)(2,1)}, f32[2,128]{1,0:T(2,128)S(1)}) custom-call(f32[64,4,128]{2,1,0:T(4,128)S(1)} %all-to-all-done.2.table_ref, f32[2,2,4,6,32,128]{5,4,3,2,1,0:T(8,128)S(1)} %fields_second.1.fields_ref, f32[80,128]{1,0:T(8,128)S(1)} %get-tuple-element.24.params_ref, ...), custom_call_target="tpu_custom_call" | custom-call | flops 1000000 | bytes 4116480 | tf_op jit(solution)/shard_map/weight_second/pallas_call | solution.py:483
  82.5 4.8 %all-to-all-start.3 = ((bf16[32,56,128]{2,1,0:T(8,128)(2,1)}), bf16[32,56,128]{2,1,0:T(8,128)(2,1)S(1)}, u32[]{:S(2)}, u32[]{:S(2)}) async-start(bf16[32,56,128]{2,1,0:T(8,128)(2,1)} %get-tuple-element.42), calls=%async_computation.3 | async-start | bytes 917504 | tf_op jit(solution)/shard_map/all_to_all | solution.py:604
  87.3 3.0 %conv_second.1 = bf16[2,4,4,32,128]{4,3,2,1,0:T(8,128)(2,1)} custom-call(f32[80,128]{1,0:T(8,128)S(1)} %get-tuple-element.24.params_ref, bf16[4,192,384]{2,1,0:T(8,128)(2,1)} %get-tuple-element.41.columns_hbm, bf16[4,6,32,128]{3,2,1,0:T(8,128)(2,1)} %copy-done, bf16[9,384,128]{2,1,0:T(8,128)(2,1)} %bitcast.17), custom_call_target="tpu_custom_call" | custom-call | flops 1000000 | bytes 1712128 | tf_op jit(solution)/shard_map/conv_second/pallas_call | solution.py:483
  90.3 0.1 constant_dynamic-slice_fusion
  90.4 0.5 fusion
  90.9 13.0 %all-to-all-done.3.terms_ref = bf16[32,56,128]{2,1,0:T(8,128)(2,1)S(1)} async-done(((bf16[32,56,128]{2,1,0:T(8,128)(2,1)}), bf16[32,56,128]{2,1,0:T(8,128)(2,1)S(1)}, u32[]{:S(2)}, u32[]{:S(2)}) %all-to-all-start.3) | async-done | bytes 458784 | tf_op jit(solution)/shard_map/all_to_all | solution.py:604
  103.9 0.7 total.1
Async XLA Ops:
  0.6 39.4 %copy-start.2 = (bf16[1,3456,128]{2,1,0:T(8,128)(2,1)S(1)}, bf16[1,3456,128]{2,1,0:T(8,128)(2,1)}, u32[]{:S(2)}) copy-start(bf16[1,3456,128]{2,1,0:T(8,128)(2,1)} %param.13) | copy-start | bytes 2654212
  2.7 27.3 %all-to-all-start = ((f32[64,4,128]{2,1,0:T(4,128)}), f32[64,4,128]{2,1,0:T(4,128)S(1)}, u32[]{:S(2)}, u32[]{:S(2)}) async-start(f32[64,4,128]{2,1,0:T(4,128)} %get-tuple-element.25), calls=%async_computation | async-start | bytes 262144 | tf_op jit(solution)/shard_map/all_to_all | solution.py:528
  19.9 21.8 %collective-permute-start = (bf16[4,6,32,128]{3,2,1,0:T(8,128)(2,1)S(1)}, bf16[4,6,32,128]{3,2,1,0:T(8,128)(2,1)S(1)}, u32[]{:S(2)}, u32[]{:S(2)}) collective-permute-start(bf16[4,6,32,128]{3,2,1,0:T(8,128)(2,1)S(1)} %get-tuple-element.28), channel_id=1, source_target_pairs={{0,1},{1,2},{2,3},{3,4},{4,5},{5,6},{6,7},{7,8},{8,9},{9,10},{10,1... | collective-permute-start | bytes 589832 | tf_op jit(solution)/shard_map/ppermute | solution.py:536
  21.9 19.7 %collective-permute-start.1 = (bf16[4,6,32,128]{3,2,1,0:T(8,128)(2,1)S(1)}, bf16[4,6,32,128]{3,2,1,0:T(8,128)(2,1)S(1)}, u32[]{:S(2)}, u32[]{:S(2)}) collective-permute-start(bf16[4,6,32,128]{3,2,1,0:T(8,128)(2,1)S(1)} %get-tuple-element.29), channel_id=1, source_target_pairs={{1,0},{2,1},{3,2},{4,3},{5,4},{6,5},{7,6},{8,7},{9,8},{10,9},{11,1... | collective-permute-start | bytes 589832 | tf_op jit(solution)/shard_map/ppermute | solution.py:535
  31.2 17.8 %all-to-all-start.1 = ((f32[64,2,128]{2,1,0:T(2,128)}), f32[64,2,128]{2,1,0:T(2,128)S(1)}, u32[]{:S(2)}, u32[]{:S(2)}) async-start(f32[64,2,128]{2,1,0:T(2,128)} %get-tuple-element.27), calls=%async_computation.1 | async-start | bytes 131072 | tf_op jit(solution)/shard_map/all_to_all | solution.py:528
  43.9 8.8 %collective-permute-start.3 = (bf16[4,26,32,128]{3,2,1,0:T(8,128)(2,1)}, bf16[4,26,32,128]{3,2,1,0:T(8,128)(2,1)S(1)}, u32[]{:S(2)}, u32[]{:S(2)}) collective-permute-start(bf16[4,26,32,128]{3,2,1,0:T(8,128)(2,1)} %get-tuple-element.35.bundle_hbm), channel_id=1, source_target_pairs={{0,1},{1,0},{2,3},{3,2},{4,5},{5,4},{6,7},{7,6},{8,9},{9,8},{10,11... | collective-permute-start | bytes 2555912 | tf_op jit(solution)/shard_map/ppermute | solution.py:560
  51.3 22.1 %copy-start = (bf16[4,6,32,128]{3,2,1,0:T(8,128)(2,1)}, bf16[4,6,32,128]{3,2,1,0:T(8,128)(2,1)S(1)}, u32[]{:S(2)}) copy-start(bf16[4,6,32,128]{3,2,1,0:T(8,128)(2,1)S(1)} %get-tuple-element.32.first_hbm) | copy-start | bytes 589828
  51.4 8.8 %collective-permute-start.2 = (bf16[4,6,32,128]{3,2,1,0:T(8,128)(2,1)S(1)}, bf16[4,6,32,128]{3,2,1,0:T(8,128)(2,1)S(1)}, u32[]{:S(2)}, u32[]{:S(2)}) collective-permute-start(bf16[4,6,32,128]{3,2,1,0:T(8,128)(2,1)S(1)} %get-tuple-element.32.first_hbm), channel_id=1, source_target_pairs={{64,0},{128,64},{192,128},{256,192},{320,256},{384,320},{448,384},... | collective-permute-start | bytes 589832 | tf_op jit(solution)/shard_map/ppermute | solution.py:570
  52.7 0.9 copy-start.1
  61.1 17.6 %all-to-all-start.2 = ((f32[64,4,128]{2,1,0:T(4,128)}), f32[64,4,128]{2,1,0:T(4,128)S(1)}, u32[]{:S(2)}, u32[]{:S(2)}) async-start(f32[64,4,128]{2,1,0:T(4,128)} %get-tuple-element.37), calls=%async_computation.2 | async-start | bytes 262144 | tf_op jit(solution)/shard_map/all_to_all | solution.py:528
  68.7 3.3 %collective-permute-start.4 = (bf16[4,6,32,128]{3,2,1,0:T(8,128)(2,1)S(1)}, bf16[4,6,32,128]{3,2,1,0:T(8,128)(2,1)S(1)}, u32[]{:S(2)}, u32[]{:S(2)}) collective-permute-start(bf16[4,6,32,128]{3,2,1,0:T(8,128)(2,1)S(1)} %get-tuple-element.38.incoming_ref), channel_id=1, source_target_pairs={{0,1},{1,0},{2,3},{3,2},{4,5},{5,4},{6,7},{7,6},{8,9},{9,8},{10,11... | collective-permute-start | bytes 589832 | tf_op jit(solution)/shard_map/ppermute | solution.py:587
  82.5 21.4 %all-to-all-start.3 = ((bf16[32,56,128]{2,1,0:T(8,128)(2,1)}), bf16[32,56,128]{2,1,0:T(8,128)(2,1)S(1)}, u32[]{:S(2)}, u32[]{:S(2)}) async-start(bf16[32,56,128]{2,1,0:T(8,128)(2,1)} %get-tuple-element.42), calls=%async_computation.3 | async-start | bytes 917504 | tf_op jit(solution)/shard_map/all_to_all | solution.py:604

commit v4 on v3

--- a/solution.py
+++ b/solution.py
@@ -81,8 +81,14 @@
     return copies
 
 
-def sums_kernel(pre_ref, cot_ref, loss_ref, out_ref, head_ref, tail_ref, held_ref, sems):
-    pairs = [(pre_ref, held_ref)]
+def sums_kernel(
+    cells, clip_hbm, pre_ref, cot_ref, loss_ref, gain_ref, shift_ref,
+    out_ref, head_ref, tail_ref, own_ref, params_ref, clip_ref, held_ref, held_cot, sems,
+):
+    pairs = [
+        (clip_hbm, clip_ref), (pre_ref, held_ref), (cot_ref, held_cot),
+        (gain_ref, params_ref.at[GAIN : GAIN + 1]), (shift_ref, params_ref.at[SHIFT : SHIFT + 1]),
+    ]
     for ref, two, one in ((head_ref, 0, 0), (tail_ref, ROWS - 2, ROWS - 1)):
         pairs += [
             (pre_ref.at[0, :, two : two + 2], ref.at[:, 0:2]),
@@ -91,49 +97,11 @@
             (loss_ref.at[:, one : one + 1], ref.at[:, 5:6]),
         ]
     copies = copy_in(pairs, sems)
-    copies[0].wait()
-    per_frame = []
-    for f in range(FRAMES):
-        rows = []
-        for t in range(2):
-            x = flat(held_ref[t, f].astype(F32))
-            rows += [colsum(x), colsum(x * x)]
-        per_frame.append(jnp.concatenate(rows, axis=0))
-    out_ref[...] = jnp.broadcast_to(pack_rows(per_frame)[None], out_ref.shape)
-    for copy in copies[1:]:
-        copy.wait()
-
-
-def clip_marks(params_ref, turn):
-    slot = iota(0) >> 5
-    clips = [row(params_ref, CLIPS + FRAMES * turn + f) for f in range(FRAMES)]
-    clip_of_row = jnp.where(
-        slot == 0, clips[0], jnp.where(slot == 1, clips[1], jnp.where(slot == 2, clips[2], clips[3]))
-    )
-    same_group = (iota(0) & (GROUPS - 1)) == (iota(1) >> 2)
-    blocks = [(same_group & (clip_of_row == clips[f])).astype(F32).astype(BF16) for f in range(FRAMES)]
-    return jnp.concatenate(blocks, axis=1)
-
-
-def prepare_kernel(
-    cells, flag_ref, clip_hbm, pre_ref, cot_ref, gain_ref, shift_ref,
-    own_ref, params_ref, clip_ref, held_pre, held_cot, sems,
-):
-    copies = copy_in(
-        [
-            (clip_hbm, clip_ref), (pre_ref, held_pre), (cot_ref, held_cot),
-            (gain_ref, params_ref.at[GAIN : GAIN + 1]), (shift_ref, params_ref.at[SHIFT : SHIFT + 1]),
-        ],
-        sems,
-    )
+    params_ref[SHIFT + 1 :] = jnp.zeros((PARAM_ROWS - SHIFT - 1, CH), F32)
 
     def put(at, scalar):
         params_ref[at : at + 1] = jnp.full((1, CH), scalar, F32)
 
-    put(CORE, flag_ref[4].astype(F32))
-    put(LAST, flag_ref[5].astype(F32))
-    params_ref[LAST + 1 : INV] = jnp.zeros((INV - LAST - 1, CH), F32)
-    flag = [flag_ref[n].astype(F32) for n in range(4)]
     copies[0].wait()
     for t in range(2):
         clips = [clip_ref[0, t, 0, f] for f in range(FRAMES)]
@@ -145,18 +113,36 @@
             base = TURN * t + f
             params_ref[base + INV : base + INV + 1] = 1.0 / jnp.full((1, CH), count.astype(F32) * cells, F32)
             put(base + LIVE, live)
-            put(base + TOP, live * flag[0])
-            put(base + BOTTOM, live * flag[1])
             put(CLIPS + FRAMES * t + f, clips[f].astype(F32))
             for kt, at in ((1, PAIR1), (2, PAIR2)):
                 pair = live * (clips[f - kt] == clips[f]).astype(F32) if f >= kt else live * 0.0
                 put(base + at, pair)
-            put(OTHER_TURN * t + OTHER_TOP + f, live * flag[2])
-            put(OTHER_TURN * t + OTHER_BOTTOM + f, live * flag[3])
-    for copy in copies[1:]:
+    copies[1].wait()
+    per_frame = []
+    for f in range(FRAMES):
+        rows = []
+        for t in range(2):
+            x = flat(held_ref[t, f].astype(F32))
+            if t == 0:
+                own_ref[0, f] = x.reshape(ROWS, COLS, CH)
+            rows += [colsum(x), colsum(x * x)]
+        per_frame.append(jnp.concatenate(rows, axis=0))
+    out_ref[...] = jnp.broadcast_to(pack_rows(per_frame)[None], out_ref.shape)
+    copies[2].wait()
+    own_ref[1] = held_cot[...].astype(F32)
+    for copy in copies[3:]:
         copy.wait()
-    own_ref[0] = held_pre[0].astype(F32)
-    own_ref[1] = held_cot[...].astype(F32)
+
+
+def clip_marks(params_ref, turn):
+    slot = iota(0) >> 5
+    clips = [row(params_ref, CLIPS + FRAMES * turn + f) for f in range(FRAMES)]
+    clip_of_row = jnp.where(
+        slot == 0, clips[0], jnp.where(slot == 1, clips[1], jnp.where(slot == 2, clips[2], clips[3]))
+    )
+    same_group = (iota(0) & (GROUPS - 1)) == (iota(1) >> 2)
+    blocks = [(same_group & (clip_of_row == clips[f])).astype(F32).astype(BF16) for f in range(FRAMES)]
+    return jnp.concatenate(blocks, axis=1)
 
 
 def act_first_kernel(table_ref, own_ref, params_ref, out_ref, stats_ref):
@@ -196,8 +182,8 @@
 
 
 def fields_first_kernel(
-    up_ref, down_ref, params_ref, stats_ref, pre_ref, cot_ref, loss_ref, act_ref,
-    out_ref, bundle_hbm, loss_out_ref, bundle_ref, held_loss, sems,
+    flag_ref, up_ref, down_ref, plain_ref, stats_ref, pre_ref, cot_ref, loss_ref, act_ref,
+    out_ref, bundle_hbm, loss_out_ref, params_ref, bundle_ref, held_loss, sems,
 ):
     copies = copy_in(
         [
@@ -208,6 +194,18 @@
         ],
         sems,
     )
+    params_ref[...] = plain_ref[...]
+    flag = [flag_ref[n].astype(F32) for n in range(6)]
+    for at, n in ((CORE, 4), (LAST, 5)):
+        params_ref[at : at + 1] = jnp.full((1, CH), flag[n], F32)
+    for t in range(2):
+        for f in range(FRAMES):
+            live = plain_ref[TURN * t + LIVE + f : TURN * t + LIVE + f + 1]
+            for at, n in (
+                (TURN * t + TOP, 0), (TURN * t + BOTTOM, 1),
+                (OTHER_TURN * t + OTHER_TOP, 2), (OTHER_TURN * t + OTHER_BOTTOM, 3),
+            ):
+                params_ref[at + f : at + f + 1] = live * flag[n]
     for at, edge, below in ((0, 4, 4), (14, 1, 0), (20, 3, 2)):
         bundle_ref[:, at : at + 1] = up_ref[:, edge : edge + 1]
         bundle_ref[:, at + 1 + ROWS : at + 2 + ROWS] = down_ref[:, below : below + 1]
@@ -260,24 +258,33 @@
     return store
 
 
-def conv_frame(columns, weight_ref, params_ref, turn, f, rows):
-    total = None
-    for kt in range(min(3, FRAMES - f)):
+def conv(columns_ref, weight_ref, params_ref, turn, rows, sum_ref):
+    size = rows * COLS
+    for kt in range(3):
+        count = FRAMES - kt
         part = None
         for dy in (-1, 0, 1):
             start = (1 - dy) * COLS
-            term = jnp.dot(
-                columns(f + kt, start, rows * COLS), weight_ref[3 * kt + dy + 1], preferred_element_type=F32
-            )
-            part = term if part is None else part + term
-        if kt:
-            part = part * row(params_ref, TURN * turn + (PAIR1 if kt == 1 else PAIR2) + f + kt)
-        total = part if total is None else total + part
-    return total.astype(BF16).reshape(rows, COLS, CH)
+            block = columns_ref[kt:FRAMES, start : start + size, :].reshape(count * size, 3 * CH)
+            for dx in range(3):
+                at = (9 * kt + 3 * (dy + 1) + dx) * CH
+                term = lax.dot_general(
+                    block[:, dx * CH : (dx + 1) * CH], weight_ref[at : at + CH], (((1,), (1,)), ((), ())),
+                    preferred_element_type=F32,
+                )
+                part = term if part is None else part + term
+        for f in range(count):
+            mine = part[f * size : (f + 1) * size]
+            if kt:
+                mine = mine * row(params_ref, TURN * turn + (PAIR1 if kt == 1 else PAIR2) + f + kt)
+                sum_ref[f] = sum_ref[f] + mine
+            else:
+                sum_ref[f] = mine
 
 
 def conv_first_kernel(
-    table_ref, fields_ref, params_ref, stats_ref, taps_ref, grad_ref, value_hbm, columns_ref, weight_ref, value_ref, sems
+    table_ref, fields_ref, params_ref, stats_ref, taps_ref, grad_ref, value_hbm,
+    columns_ref, weight_ref, value_ref, sum_ref, sems,
 ):
     (copy,) = copy_in([(taps_ref, weight_ref)], sems)
     table = jnp.sum(table_ref[...], axis=0)
@@ -293,10 +300,8 @@
     value_out = pltpu.make_async_copy(value_ref, value_hbm, sems.at[1])
     value_out.start()
     copy.wait()
-    for f in range(FRAMES):
-        grad_ref[f] = conv_frame(
-            lambda g, start, size: columns_ref[g, start : start + size], weight_ref, params_ref, 0, f, ROWS + 2
-        )
+    conv(columns_ref, weight_ref, params_ref, 0, ROWS + 2, sum_ref)
+    grad_ref[...] = sum_ref[...].astype(BF16).reshape(grad_ref.shape)
     value_out.wait()
 
 
@@ -419,7 +424,9 @@
     scale, chunk, table_ref, fields_ref, params_ref, stats_ref, first_hbm, act_hbm,
     out_hbm, own_hbm, parts_ref, columns_ref, sum_ref, act_ref, first_ref, out_ref, sems,
 ):
-    copies = copy_in([(act_hbm, act_ref), (first_hbm, first_ref)], sems)
+    arrive = copy_in(
+        [(act_hbm, act_ref)] + [(first_hbm.at[n : n + 3], first_ref.at[n : n + 3]) for n in range(0, TAPS, 3)], sems
+    )
     table = jnp.sum(table_ref[...], axis=0)
     parts_ref[...] = table[2:4] * scale
     for strip, top, bottom in ((0, TURN + TOP, TURN + BOTTOM), (1, OTHER_TURN + OTHER_TOP, OTHER_TURN + OTHER_BOTTOM)):
@@ -427,10 +434,9 @@
             store_columns(columns_ref, (strip,)), table[0:2], fields_ref, (strip,), params_ref, stats_ref,
             RSTD1, 1, 1, (top, TURN + LIVE, bottom),
         )
-    copy_own = pltpu.make_async_copy(columns_ref.at[0], own_hbm, sems.at[2])
+    copy_own = pltpu.make_async_copy(columns_ref.at[0], own_hbm, sems.at[10])
     copy_own.start()
-    for copy in copies:
-        copy.wait()
+    arrive[0].wait()
     second = row(params_ref, CORE) > 0.5
     filler = jnp.zeros((out_ref.shape[1] - chunk, CH), F32)
     chips = out_ref.shape[0]
@@ -440,6 +446,7 @@
         for dy in (-1, 0, 1):
             terms = kernel_terms(columns_ref, act_ref, kt, dy)
             tap = 9 * kt + 3 * (dy + 1)
+            arrive[1 + tap // 3].wait()
             for dx in range(3):
                 at = (tap + dx) * CH
                 sum_ref[at : at + CH] = first_ref[tap + dx] + terms[:, dx * CH : (dx + 1) * CH]
@@ -452,21 +459,21 @@
             out_ref[done] = mine.astype(BF16)
             done += 1
         if done > begin:
-            send = pltpu.make_async_copy(out_ref.at[begin:done], out_hbm.at[begin:done], sems.at[3 + kt])
+            send = pltpu.make_async_copy(out_ref.at[begin:done], out_hbm.at[begin:done], sems.at[11 + kt])
             send.start()
             copies.append(send)
     for copy in copies:
         copy.wait()
 
 
-def conv_second_kernel(params_ref, columns_hbm, first_hbm, taps_ref, out_ref, weight_ref, columns_ref, first_ref, sems):
+def conv_second_kernel(
+    params_ref, columns_hbm, first_hbm, taps_ref, out_ref, weight_ref, columns_ref, first_ref, sum_ref, sems
+):
     for copy in copy_in([(columns_hbm, columns_ref), (first_hbm, first_ref), (taps_ref, weight_ref)], sems):
         copy.wait()
-    for f in range(FRAMES):
-        out_ref[0, f] = first_ref[f, 1 : 1 + ROWS]
-        out_ref[1, f] = conv_frame(
-            lambda g, start, size: columns_ref[g, start : start + size], weight_ref, params_ref, 1, f, ROWS
-        )
+    conv(columns_ref, weight_ref, params_ref, 1, ROWS, sum_ref)
+    out_ref[0] = first_ref[:, 1 : 1 + ROWS]
+    out_ref[1] = sum_ref[...].astype(BF16).reshape(first_ref[:, 1 : 1 + ROWS].shape)
 
 
 def total_kernel(scale, terms_ref, out_ref):
@@ -516,7 +523,7 @@
     flags = jnp.stack([x.astype(jnp.int32) for x in flags])
     pre, act = pre_norm[0], activations[0]
     cot, loss = cot_first[0], loss_grad[0]
-    taps = weight[0].reshape(9, 3, CH, CH).transpose(0, 1, 3, 2).reshape(9, 3 * CH, CH)
+    taps = weight[0]
     edge = (FRAMES, ROWS + 2, COLS, CH)
     strip = (FRAMES, ROWS, COLS, CH)
     bundled = (FRAMES, 3 * (ROWS + 2) + 2 * ROWS, COLS, CH)
@@ -527,43 +534,45 @@
     def exchange(table):
         return lax.all_to_all(table, "dp", 0, 0, tiled=True)
 
-    table, head, tail = call(
-        sums_kernel, "sums", (pre, cot, loss), (shape((dp, 4, CH)), shape(edge, BF16), shape(edge, BF16)),
-        scratch=[pltpu.VMEM((2,) + strip, BF16), sems(9)], specs="hhh",
+    table, head, tail, own, plain = call(
+        functools.partial(sums_kernel, cells), "sums", (frame_clip, pre, cot, loss, norm_gain, norm_shift),
+        (
+            shape((dp, 4, CH)), shape(edge, BF16), shape(edge, BF16),
+            kept((2,) + strip), kept((PARAM_ROWS, CH)),
+        ),
+        scratch=[
+            pltpu.SMEM((1, 2, 1, FRAMES), jnp.int32), pltpu.VMEM((2,) + strip, BF16), pltpu.VMEM(strip, BF16), sems(13)
+        ],
+        specs="hhhhhh",
     )
     table = exchange(table)
     down = lax.ppermute(head, "dp", [(i + 1, i) for i in range(dp - 1)])
     up = lax.ppermute(tail, "dp", [(i, i + 1) for i in range(dp - 1)])
 
-    own, params = call(
-        functools.partial(prepare_kernel, cells), "prepare", (flags, frame_clip, pre, cot, norm_gain, norm_shift),
-        (kept((2,) + strip), kept((PARAM_ROWS, CH))),
-        scratch=[
-            pltpu.SMEM((1, 2, 1, FRAMES), jnp.int32), pltpu.VMEM((2,) + strip, BF16), pltpu.VMEM(strip, BF16), sems(5)
-        ],
-        specs="shhhhh",
-    )
     table, stats = call(
-        act_first_kernel, "act_first", (table, own, params), (shape((dp, 2, CH)), kept((STAT_ROWS, CH))), specs="vkk"
+        act_first_kernel, "act_first", (table, own, plain), (shape((dp, 2, CH)), kept((STAT_ROWS, CH))), specs="vkk"
     )
     table = exchange(table)
 
-    first_fields, bundle, loss_rows = call(
-        fields_first_kernel, "fields_first", (up, down, params, stats, pre, cot, loss, act),
+    first_fields, bundle, loss_rows, params = call(
+        fields_first_kernel, "fields_first", (flags, up, down, plain, stats, pre, cot, loss, act),
         (
             kept((2, FRAMES, ROWS + 4, COLS, CH)), in_hbm(bundled, BF16),
-            kept(edge, BF16),
+            kept(edge, BF16), kept((PARAM_ROWS, CH)),
         ),
         scratch=[pltpu.VMEM(bundled, BF16), pltpu.VMEM(strip, BF16), sems(7)],
-        specs="vvkkhhhh",
+        specs="svvkkhhhh",
     )
     other_bundle = lax.ppermute(bundle, "dp", mates)
 
-    weights = pltpu.VMEM((9, 3 * CH, CH), BF16)
+    weights = pltpu.VMEM((TAPS * CH, CH), BF16)
     grad_first, value = call(
         conv_first_kernel, "conv_first", (table, first_fields, params, stats, taps),
         (shape(edge, BF16), in_hbm(edge, BF16)),
-        scratch=[pltpu.VMEM(columns_of(ROWS + 4), BF16), weights, pltpu.VMEM(edge, BF16), sems(2)],
+        scratch=[
+            pltpu.VMEM(columns_of(ROWS + 4), BF16), weights, pltpu.VMEM(edge, BF16),
+            pltpu.VMEM((FRAMES, (ROWS + 2) * COLS, CH), F32), sems(2),
+        ],
         specs="vkkkh", flops=20_000_000_000,
     )
     count = lax.axis_size("segment")
@@ -596,7 +605,7 @@
         (in_hbm((chips, padded, CH), BF16), in_hbm(columns_of(ROWS + 2), BF16), shape((2, CH))),
         scratch=[
             both, pltpu.VMEM((TAPS * CH, CH), F32), pltpu.VMEM(acts_dims, BF16), pltpu.VMEM(taps_dims, F32),
-            pltpu.VMEM((chips, padded, CH), BF16), sems(6),
+            pltpu.VMEM((chips, padded, CH), BF16), sems(14),
         ],
         specs="vkkkhh",
     )
@@ -608,7 +617,11 @@
     (grad_inputs,) = call(
         conv_second_kernel, "conv_second", (params, columns, grad_first, taps),
         (shape((2, FRAMES, ROWS, COLS, CH), BF16),),
-        scratch=[weights, pltpu.VMEM(columns_of(ROWS + 2), BF16), pltpu.VMEM(edge, BF16), sems(3)], specs="khhh",
+        scratch=[
+            weights, pltpu.VMEM(columns_of(ROWS + 2), BF16), pltpu.VMEM(edge, BF16),
+            pltpu.VMEM((FRAMES, ROWS * COLS, CH), F32), sems(3),
+        ],
+        specs="khhh",
     )
     width = CH // dp
     mine = lax.dynamic_slice_in_dim(parts, me * width, width, axis=1)

time: 105 us -> 103 us (0.981)
  waiting for transfers between devices: 27.5 us -> 30.2 us
  starting transfers between devices: 49.3 us -> 46.6 us
  local copies, waits for them, and re-layouts: 3.24 us -> 1.59 us
    all_to_all x3, waiting for transfers between devices: 11.1 us -> 13.8 us  [exchange(): return lax.all_to_all(table, 'dp', 0, 0, tiled=True)]
    all_to_all x3, starting transfers between devices: 33.5 us -> 30.8 us  [exchange(): return lax.all_to_all(table, 'dp', 0, 0, tiled=True)]
    another operation x1 -> x0, local copies, waits for them, and re-layouts: 1.64 us -> none  [local(): weight[0].reshape(9, 3, CH, CH).transpose(0, 1, 3, 2).reshape(9, 3 * CH, CH)]
    pallas_call x11 -> x10, Pallas kernels: 23.7 us -> 23.2 us  [call(): pl.pallas_call(kernel, out_shape=tuple(outs), in_specs=[{'v': VMEM, 'k':...]
  transfers between devices with their start and end apart: 9 -> 9, of which waited for: 6 -> 6; matrix products, arithmetic and copies ran while one was open for 2% -> 1% of each run, Pallas kernels for 16% -> 15%
where the time goes in v4:
time: 103 us; the launch traced here: 102 us
  starting transfers between devices  46.6 us (45%)
  waiting for transfers between devices  30.2 us (29%)
  Pallas kernels  23.2 us (23%)
  local copies, waits for them, and re-layouts  1.59 us (2%)
    all_to_all x3, starting transfers between devices, exchange(): return lax.all_to_all(table, 'dp', 0, 0, tiled=True)  30.8 us
    pallas_call x10, Pallas kernels, call(): pl.pallas_call(kernel, out_shape=tuple(outs), in_specs=[{'v': VMEM, 'k':...  23.2 us
    all_to_all x3, waiting for transfers between devices, exchange(): return lax.all_to_all(table, 'dp', 0, 0, tiled=True)  13.8 us
    all_to_all x1, waiting for transfers between devices, local(): lax.all_to_all(terms, 'dp', 0, 0, axis_index_groups=sides, tiled=True)  13 us
    all_to_all x1, starting transfers between devices, local(): lax.all_to_all(terms, 'dp', 0, 0, axis_index_groups=sides, tiled=True)  4.81 us
    ppermute x1, starting transfers between devices, local(): down = lax.ppermute(head, 'dp', [(i + 1, i) for i in range(dp - 1)])  3.51 us
    ppermute x1, waiting for transfers between devices, local(): lax.ppermute(grad_first, 'segment', [(i + 1, i) for i in range(count - 1)])  2.14 us
  transfers between devices with their start and end apart: 9, of which 6 were waited for; matrix products, arithmetic and copies ran while one was open for 1% of the time, Pallas kernels for 15%

profile of v4, /device:TPU:8, one launch (start us, length us, event | category | flops | bytes accessed | tf_op | source)
XLA Modules:
  0.0 102.4 jit_solution(12333966108502858948)
XLA Ops:
  0.6 2.0 %sums.1 = (f32[64,4,128]{2,1,0:T(4,128)}, bf16[4,6,32,128]{3,2,1,0:T(8,128)(2,1)S(1)}, bf16[4,6,32,128]{3,2,1,0:T(8,128)(2,1)S(1)}, f32[2,4,4,32,128]{4,3,2,1,0:T(8,128)S(1)}, f32[80,128]{1,0:T(8,128)S(1)}) custom-call(s32[1,2,1,4]{3,2,1,0:T(1,128)} %clip_hbm.1, bf16[2,4,4,32,128]{4,3,2,1,0:T(8,128)(2,1)} %bitcast.13, bf16[4,4,32,128]{3,2,1,0:T(8,128)(2,1)} %bitcast.17, ...), custom_call_target="tpu_custom_call" | custom-call | flops 1000000 | bytes 525344 | tf_op jit(solution)/shard_map/sums/pallas_call | solution.py:490
  2.7 17.2 %all-to-all-start = ((f32[64,4,128]{2,1,0:T(4,128)}), f32[64,4,128]{2,1,0:T(4,128)S(1)}, u32[]{:S(2)}, u32[]{:S(2)}) async-start(f32[64,4,128]{2,1,0:T(4,128)} %get-tuple-element.28), calls=%async_computation | async-start | bytes 262144 | tf_op jit(solution)/shard_map/all_to_all | solution.py:535
  19.8 2.1 %collective-permute-start = (bf16[4,6,32,128]{3,2,1,0:T(8,128)(2,1)S(1)}, bf16[4,6,32,128]{3,2,1,0:T(8,128)(2,1)S(1)}, u32[]{:S(2)}, u32[]{:S(2)}) collective-permute-start(bf16[4,6,32,128]{3,2,1,0:T(8,128)(2,1)S(1)} %get-tuple-element.25), channel_id=1, source_target_pairs={{0,1},{1,2},{2,3},{3,4},{4,5},{5,6},{6,7},{7,8},{8,9},{9,10},{10,1... | collective-permute-start | bytes 589832 | tf_op jit(solution)/shard_map/ppermute | solution.py:550
  21.9 3.5 %collective-permute-start.1 = (bf16[4,6,32,128]{3,2,1,0:T(8,128)(2,1)S(1)}, bf16[4,6,32,128]{3,2,1,0:T(8,128)(2,1)S(1)}, u32[]{:S(2)}, u32[]{:S(2)}) collective-permute-start(bf16[4,6,32,128]{3,2,1,0:T(8,128)(2,1)S(1)} %get-tuple-element.26), channel_id=1, source_target_pairs={{1,0},{2,1},{3,2},{4,3},{5,4},{6,5},{7,6},{8,7},{9,8},{10,9},{11,1... | collective-permute-start | bytes 589832 | tf_op jit(solution)/shard_map/ppermute | solution.py:549
  25.4 4.6 %all-to-all-done.table_ref = f32[64,4,128]{2,1,0:T(4,128)S(1)} async-done(((f32[64,4,128]{2,1,0:T(4,128)}), f32[64,4,128]{2,1,0:T(4,128)S(1)}, u32[]{:S(2)}, u32[]{:S(2)}) %all-to-all-start) | async-done | bytes 131104 | tf_op jit(solution)/shard_map/all_to_all | solution.py:535
  30.0 1.2 %act_first.1 = (f32[64,2,128]{2,1,0:T(2,128)}, f32[24,128]{1,0:T(8,128)S(1)}) custom-call(f32[64,4,128]{2,1,0:T(4,128)S(1)} %all-to-all-done.table_ref, f32[2,4,4,32,128]{4,3,2,1,0:T(8,128)S(1)} %get-tuple-element.29.own_ref, f32[80,128]{1,0:T(8,128)S(1)} %get-tuple-element.27.params_ref.plain_ref), custom_call_target="tpu_custom_call" | custom-call | flops 1000000 | bytes 696320 | tf_op jit(solution)/shard_map/act_first/pallas_call | solution.py:490
  31.2 7.1 %all-to-all-start.1 = ((f32[64,2,128]{2,1,0:T(2,128)}), f32[64,2,128]{2,1,0:T(2,128)S(1)}, u32[]{:S(2)}, u32[]{:S(2)}) async-start(f32[64,2,128]{2,1,0:T(2,128)} %get-tuple-element.32), calls=%async_computation.1 | async-start | bytes 131072 | tf_op jit(solution)/shard_map/all_to_all | solution.py:535
  38.3 0.1 stack.47.flag_ref
  38.4 0.0 collective-permute-done.up_ref
  38.4 0.0 collective-permute-done.1.down_ref
  38.4 2.7 %fields_first.1 = (f32[2,4,8,32,128]{4,3,2,1,0:T(8,128)S(1)}, bf16[4,26,32,128]{3,2,1,0:T(8,128)(2,1)}, bf16[4,6,32,128]{3,2,1,0:T(8,128)(2,1)S(1)}, f32[80,128]{1,0:T(8,128)S(1)}) custom-call(s32[6]{0:T(128)S(1)} %stack.47.flag_ref, bf16[4,6,32,128]{3,2,1,0:T(8,128)(2,1)S(1)} %collective-permute-done.up_ref, ...), custom_call_target="tpu_custom_call" | custom-call | flops 1000000 | bytes 1232920 | tf_op jit(solution)/shard_map/fields_first/pallas_call | solution.py:490
  41.1 2.1 %collective-permute-start.3 = (bf16[4,26,32,128]{3,2,1,0:T(8,128)(2,1)}, bf16[4,26,32,128]{3,2,1,0:T(8,128)(2,1)S(1)}, u32[]{:S(2)}, u32[]{:S(2)}) collective-permute-start(bf16[4,26,32,128]{3,2,1,0:T(8,128)(2,1)} %get-tuple-element.37.bundle_hbm), channel_id=1, source_target_pairs={{0,1},{1,0},{2,3},{3,2},{4,5},{5,4},{6,7},{7,6},{8,9},{9,8},{10,11... | collective-permute-start | bytes 2555912 | tf_op jit(solution)/shard_map/ppermute | solution.py:566
  43.2 4.1 %all-to-all-done.1.table_ref = f32[64,2,128]{2,1,0:T(2,128)S(1)} async-done(((f32[64,2,128]{2,1,0:T(2,128)}), f32[64,2,128]{2,1,0:T(2,128)S(1)}, u32[]{:S(2)}, u32[]{:S(2)}) %all-to-all-start.1) | async-done | bytes 65568 | tf_op jit(solution)/shard_map/all_to_all | solution.py:535
  47.2 2.4 %conv_first.1 = (bf16[4,6,32,128]{3,2,1,0:T(8,128)(2,1)S(1)}, bf16[4,6,32,128]{3,2,1,0:T(8,128)(2,1)}) custom-call(f32[64,2,128]{2,1,0:T(2,128)S(1)} %all-to-all-done.1.table_ref, f32[2,4,8,32,128]{4,3,2,1,0:T(8,128)S(1)} %get-tuple-element.33.fields_ref, f32[80,128]{1,0:T(8,128)S(1)} %get-tuple-element.31.params_ref, ...), custom_call_target="tpu_custom_call" | custom-call | flops 20000000000 | bytes 2052096 | tf_op jit(solution)/shard_map/conv_first/pallas_call | solution.py:490
  49.6 0.0 copy-start
  49.6 1.3 %collective-permute-start.2 = (bf16[4,6,32,128]{3,2,1,0:T(8,128)(2,1)S(1)}, bf16[4,6,32,128]{3,2,1,0:T(8,128)(2,1)S(1)}, u32[]{:S(2)}, u32[]{:S(2)}) collective-permute-start(bf16[4,6,32,128]{3,2,1,0:T(8,128)(2,1)S(1)} %get-tuple-element.34.first_hbm), channel_id=1, source_target_pairs={{64,0},{128,64},{192,128},{256,192},{320,256},{384,320},{448,384},... | collective-permute-start | bytes 589832 | tf_op jit(solution)/shard_map/ppermute | solution.py:579
  50.9 0.0 collective-permute-done.3.other_hbm
  50.9 0.0 copy-start.1
  50.9 0.9 copy-done.1
  51.8 4.4 %weight_first.1 = (f32[2,4,4,32,128]{4,3,2,1,0:T(8,128)S(1)}, bf16[128,2304]{1,0:T(8,128)(2,1)}, f32[27,128,128]{2,1,0:T(8,128)}) custom-call(f32[64,2,128]{2,1,0:T(2,128)S(1)} %all-to-all-done.1.table_ref, f32[80,128]{1,0:T(8,128)S(1)} %get-tuple-element.31.params_ref, f32[24,128]{1,0:T(8,128)S(1)} %get-tuple-element.30.stats_ref, ...), custom_call_target="tpu_custom_call" | custom-call | flops 1000000 | bytes 2019328 | tf_op jit(solution)/shard_map/weight_first/pallas_call | solution.py:490
  56.3 2.1 %collective-permute-done.2.hand_ref = bf16[4,6,32,128]{3,2,1,0:T(8,128)(2,1)S(1)} collective-permute-done((bf16[4,6,32,128]{3,2,1,0:T(8,128)(2,1)S(1)}, bf16[4,6,32,128]{3,2,1,0:T(8,128)(2,1)S(1)}, u32[]{:S(2)}, u32[]{:S(2)}) %collective-permute-start.2) | collective-permute-done | bytes 196640 | tf_op jit(solution)/shard_map/ppermute | solution.py:579
  58.4 0.9 act_second.1
  59.4 6.5 %all-to-all-start.2 = ((f32[64,4,128]{2,1,0:T(4,128)}), f32[64,4,128]{2,1,0:T(4,128)S(1)}, u32[]{:S(2)}, u32[]{:S(2)}) async-start(f32[64,4,128]{2,1,0:T(4,128)} %get-tuple-element.39), calls=%async_computation.2 | async-start | bytes 262144 | tf_op jit(solution)/shard_map/all_to_all | solution.py:535
  65.9 2.1 %collective-permute-start.4 = (bf16[4,6,32,128]{3,2,1,0:T(8,128)(2,1)S(1)}, bf16[4,6,32,128]{3,2,1,0:T(8,128)(2,1)S(1)}, u32[]{:S(2)}, u32[]{:S(2)}) collective-permute-start(bf16[4,6,32,128]{3,2,1,0:T(8,128)(2,1)S(1)} %get-tuple-element.40.incoming_ref), channel_id=1, source_target_pairs={{0,1},{1,0},{2,3},{3,2},{4,5},{5,4},{6,7},{7,6},{8,9},{9,8},{10,11... | collective-permute-start | bytes 589832 | tf_op jit(solution)/shard_map/ppermute | solution.py:596
  68.0 1.3 %collective-permute-done.4.arrived_ref = bf16[4,6,32,128]{3,2,1,0:T(8,128)(2,1)S(1)} collective-permute-done((bf16[4,6,32,128]{3,2,1,0:T(8,128)(2,1)S(1)}, bf16[4,6,32,128]{3,2,1,0:T(8,128)(2,1)S(1)}, u32[]{:S(2)}, u32[]{:S(2)}) %collective-permute-start.4) | collective-permute-done | bytes 196640 | tf_op jit(solution)/shard_map/ppermute | solution.py:596
  69.2 1.5 %fields_second.1.fields_ref = f32[2,2,4,6,32,128]{5,4,3,2,1,0:T(8,128)S(1)} custom-call(bf16[4,6,32,128]{3,2,1,0:T(8,128)(2,1)S(1)} %get-tuple-element.40.incoming_ref, bf16[4,6,32,128]{3,2,1,0:T(8,128)(2,1)S(1)} %collective-permute-done.4.arrived_ref, bf16[4,26,32,128]{3,2,1,0:T(8,128)(2,1)} %get-tuple-element.37.bundle_hbm, ...), custom_call_target="tpu_custom_call" | custom-call | flops 1000000 | bytes 2150400 | tf_op jit(solution)/shard_map/fields_second/pallas_call | solution.py:490
  70.7 0.0 copy-done
  70.7 5.2 %all-to-all-done.2.table_ref = f32[64,4,128]{2,1,0:T(4,128)S(1)} async-done(((f32[64,4,128]{2,1,0:T(4,128)}), f32[64,4,128]{2,1,0:T(4,128)S(1)}, u32[]{:S(2)}, u32[]{:S(2)}) %all-to-all-start.2) | async-done | bytes 131104 | tf_op jit(solution)/shard_map/all_to_all | solution.py:535
  75.9 4.4 %weight_second.1 = (bf16[32,56,128]{2,1,0:T(8,128)(2,1)}, bf16[4,192,384]{2,1,0:T(8,128)(2,1)}, f32[2,128]{1,0:T(2,128)S(1)}) custom-call(f32[64,4,128]{2,1,0:T(4,128)S(1)} %all-to-all-done.2.table_ref, f32[2,2,4,6,32,128]{5,4,3,2,1,0:T(8,128)S(1)} %fields_second.1.fields_ref, f32[80,128]{1,0:T(8,128)S(1)} %get-tuple-element.31.params_ref, ...), custom_call_target="tpu_custom_call" | custom-call | flops 1000000 | bytes 4116480 | tf_op jit(solution)/shard_map/weight_second/pallas_call | solution.py:490
  80.3 4.8 %all-to-all-start.3 = ((bf16[32,56,128]{2,1,0:T(8,128)(2,1)}), bf16[32,56,128]{2,1,0:T(8,128)(2,1)S(1)}, u32[]{:S(2)}, u32[]{:S(2)}) async-start(bf16[32,56,128]{2,1,0:T(8,128)(2,1)} %get-tuple-element.44), calls=%async_computation.3 | async-start | bytes 917504 | tf_op jit(solution)/shard_map/all_to_all | solution.py:613
  85.1 3.0 %conv_second.1 = bf16[2,4,4,32,128]{4,3,2,1,0:T(8,128)(2,1)} custom-call(f32[80,128]{1,0:T(8,128)S(1)} %get-tuple-element.31.params_ref, bf16[4,192,384]{2,1,0:T(8,128)(2,1)} %get-tuple-element.43.columns_hbm, bf16[4,6,32,128]{3,2,1,0:T(8,128)(2,1)} %copy-done, bf16[3456,128]{1,0:T(8,128)(2,1)} %bitcast.16), custom_call_target="tpu_custom_call" | custom-call | flops 1000000 | bytes 1712128 | tf_op jit(solution)/shard_map/conv_second/pallas_call | solution.py:490
  88.1 0.1 constant_dynamic-slice_fusion
  88.2 0.5 fusion
  88.7 13.0 %all-to-all-done.3.terms_ref = bf16[32,56,128]{2,1,0:T(8,128)(2,1)S(1)} async-done(((bf16[32,56,128]{2,1,0:T(8,128)(2,1)}), bf16[32,56,128]{2,1,0:T(8,128)(2,1)S(1)}, u32[]{:S(2)}, u32[]{:S(2)}) %all-to-all-start.3) | async-done | bytes 458784 | tf_op jit(solution)/shard_map/all_to_all | solution.py:613
  101.7 0.7 total.1
Async XLA Ops:
  2.7 27.3 %all-to-all-start = ((f32[64,4,128]{2,1,0:T(4,128)}), f32[64,4,128]{2,1,0:T(4,128)S(1)}, u32[]{:S(2)}, u32[]{:S(2)}) async-start(f32[64,4,128]{2,1,0:T(4,128)} %get-tuple-element.28), calls=%async_computation | async-start | bytes 262144 | tf_op jit(solution)/shard_map/all_to_all | solution.py:535
  19.8 18.5 %collective-permute-start = (bf16[4,6,32,128]{3,2,1,0:T(8,128)(2,1)S(1)}, bf16[4,6,32,128]{3,2,1,0:T(8,128)(2,1)S(1)}, u32[]{:S(2)}, u32[]{:S(2)}) collective-permute-start(bf16[4,6,32,128]{3,2,1,0:T(8,128)(2,1)S(1)} %get-tuple-element.25), channel_id=1, source_target_pairs={{0,1},{1,2},{2,3},{3,4},{4,5},{5,6},{6,7},{7,8},{8,9},{9,10},{10,1... | collective-permute-start | bytes 589832 | tf_op jit(solution)/shard_map/ppermute | solution.py:550
  21.9 16.5 %collective-permute-start.1 = (bf16[4,6,32,128]{3,2,1,0:T(8,128)(2,1)S(1)}, bf16[4,6,32,128]{3,2,1,0:T(8,128)(2,1)S(1)}, u32[]{:S(2)}, u32[]{:S(2)}) collective-permute-start(bf16[4,6,32,128]{3,2,1,0:T(8,128)(2,1)S(1)} %get-tuple-element.26), channel_id=1, source_target_pairs={{1,0},{2,1},{3,2},{4,3},{5,4},{6,5},{7,6},{8,7},{9,8},{10,9},{11,1... | collective-permute-start | bytes 589832 | tf_op jit(solution)/shard_map/ppermute | solution.py:549
  31.2 16.0 %all-to-all-start.1 = ((f32[64,2,128]{2,1,0:T(2,128)}), f32[64,2,128]{2,1,0:T(2,128)S(1)}, u32[]{:S(2)}, u32[]{:S(2)}) async-start(f32[64,2,128]{2,1,0:T(2,128)} %get-tuple-element.32), calls=%async_computation.1 | async-start | bytes 131072 | tf_op jit(solution)/shard_map/all_to_all | solution.py:535
  41.1 9.8 %collective-permute-start.3 = (bf16[4,26,32,128]{3,2,1,0:T(8,128)(2,1)}, bf16[4,26,32,128]{3,2,1,0:T(8,128)(2,1)S(1)}, u32[]{:S(2)}, u32[]{:S(2)}) collective-permute-start(bf16[4,26,32,128]{3,2,1,0:T(8,128)(2,1)} %get-tuple-element.37.bundle_hbm), channel_id=1, source_target_pairs={{0,1},{1,0},{2,3},{3,2},{4,5},{5,4},{6,7},{7,6},{8,9},{9,8},{10,11... | collective-permute-start | bytes 2555912 | tf_op jit(solution)/shard_map/ppermute | solution.py:566
  49.6 21.1 %copy-start = (bf16[4,6,32,128]{3,2,1,0:T(8,128)(2,1)}, bf16[4,6,32,128]{3,2,1,0:T(8,128)(2,1)S(1)}, u32[]{:S(2)}) copy-start(bf16[4,6,32,128]{3,2,1,0:T(8,128)(2,1)S(1)} %get-tuple-element.34.first_hbm) | copy-start | bytes 589828
  49.6 8.8 %collective-permute-start.2 = (bf16[4,6,32,128]{3,2,1,0:T(8,128)(2,1)S(1)}, bf16[4,6,32,128]{3,2,1,0:T(8,128)(2,1)S(1)}, u32[]{:S(2)}, u32[]{:S(2)}) collective-permute-start(bf16[4,6,32,128]{3,2,1,0:T(8,128)(2,1)S(1)} %get-tuple-element.34.first_hbm), channel_id=1, source_target_pairs={{64,0},{128,64},{192,128},{256,192},{320,256},{384,320},{448,384},... | collective-permute-start | bytes 589832 | tf_op jit(solution)/shard_map/ppermute | solution.py:579
  50.9 0.9 copy-start.1
  59.4 16.6 %all-to-all-start.2 = ((f32[64,4,128]{2,1,0:T(4,128)}), f32[64,4,128]{2,1,0:T(4,128)S(1)}, u32[]{:S(2)}, u32[]{:S(2)}) async-start(f32[64,4,128]{2,1,0:T(4,128)} %get-tuple-element.39), calls=%async_computation.2 | async-start | bytes 262144 | tf_op jit(solution)/shard_map/all_to_all | solution.py:535
  65.9 3.3 %collective-permute-start.4 = (bf16[4,6,32,128]{3,2,1,0:T(8,128)(2,1)S(1)}, bf16[4,6,32,128]{3,2,1,0:T(8,128)(2,1)S(1)}, u32[]{:S(2)}, u32[]{:S(2)}) collective-permute-start(bf16[4,6,32,128]{3,2,1,0:T(8,128)(2,1)S(1)} %get-tuple-element.40.incoming_ref), channel_id=1, source_target_pairs={{0,1},{1,0},{2,3},{3,2},{4,5},{5,4},{6,7},{7,6},{8,9},{9,8},{10,11... | collective-permute-start | bytes 589832 | tf_op jit(solution)/shard_map/ppermute | solution.py:596
  80.3 21.4 %all-to-all-start.3 = ((bf16[32,56,128]{2,1,0:T(8,128)(2,1)}), bf16[32,56,128]{2,1,0:T(8,128)(2,1)S(1)}, u32[]{:S(2)}, u32[]{:S(2)}) async-start(bf16[32,56,128]{2,1,0:T(8,128)(2,1)} %get-tuple-element.44), calls=%async_computation.3 | async-start | bytes 917504 | tf_op jit(solution)/shard_map/all_to_all | solution.py:613

commit v5 on v4

--- a/solution.py
+++ b/solution.py
@@ -262,17 +262,13 @@
     size = rows * COLS
     for kt in range(3):
         count = FRAMES - kt
-        part = None
-        for dy in (-1, 0, 1):
-            start = (1 - dy) * COLS
-            block = columns_ref[kt:FRAMES, start : start + size, :].reshape(count * size, 3 * CH)
-            for dx in range(3):
-                at = (9 * kt + 3 * (dy + 1) + dx) * CH
-                term = lax.dot_general(
-                    block[:, dx * CH : (dx + 1) * CH], weight_ref[at : at + CH], (((1,), (1,)), ((), ())),
-                    preferred_element_type=F32,
-                )
-                part = term if part is None else part + term
+        blocks = [
+            columns_ref[kt:FRAMES, start : start + size, :].reshape(count * size, 3 * CH)
+            for start in (2 * COLS, COLS, 0)
+        ]
+        part = lax.dot_general(
+            jnp.concatenate(blocks, axis=1), weight_ref[kt], (((1,), (1,)), ((), ())), preferred_element_type=F32
+        )
         for f in range(count):
             mine = part[f * size : (f + 1) * size]
             if kt:
@@ -282,11 +278,15 @@
                 sum_ref[f] = mine
 
 
+def weight_copies(taps_ref, weight_ref):
+    return [(taps_ref.at[:, n], weight_ref.at[:, :, n * CH : (n + 1) * CH]) for n in range(9)]
+
+
 def conv_first_kernel(
     table_ref, fields_ref, params_ref, stats_ref, taps_ref, grad_ref, value_hbm,
     columns_ref, weight_ref, value_ref, sum_ref, sems,
 ):
-    (copy,) = copy_in([(taps_ref, weight_ref)], sems)
+    copies = copy_in(weight_copies(taps_ref, weight_ref), sems)
     table = jnp.sum(table_ref[...], axis=0)
     fill = store_columns(columns_ref)
 
@@ -297,9 +297,10 @@
     write_columns(
         store, table, fields_ref, (), params_ref, stats_ref, RSTD0, 0, 2, (TOP, LIVE, BOTTOM)
     )
-    value_out = pltpu.make_async_copy(value_ref, value_hbm, sems.at[1])
+    value_out = pltpu.make_async_copy(value_ref, value_hbm, sems.at[9])
     value_out.start()
-    copy.wait()
+    for copy in copies:
+        copy.wait()
     conv(columns_ref, weight_ref, params_ref, 0, ROWS + 2, sum_ref)
     grad_ref[...] = sum_ref[...].astype(BF16).reshape(grad_ref.shape)
     value_out.wait()
@@ -315,12 +316,16 @@
                 out_ref[:, at : at + CH] = y.astype(BF16)
 
 
-def kernel_terms(columns_ref, act_ref, kt, dy):
+def kernel_terms(columns_ref, act_ref, kt):
     count = FRAMES - kt
-    start = (1 - dy) * COLS
-    columns = columns_ref[:, kt:FRAMES, start : start + ROWS * COLS, :].reshape(2 * count * CH, 3 * CH)
+    blocks = [
+        columns_ref[:, kt:FRAMES, start : start + ROWS * COLS, :].reshape(2 * count * CH, 3 * CH)
+        for start in (2 * COLS, COLS, 0)
+    ]
     at = 2 * CH * sum(FRAMES - n for n in range(kt))
-    return jnp.dot(act_ref[:, at : at + 2 * count * CH], columns, preferred_element_type=F32)
+    return jnp.dot(
+        act_ref[:, at : at + 2 * count * CH], jnp.concatenate(blocks, axis=1), preferred_element_type=F32
+    )
 
 
 def act_second_kernel(hand_ref, loss_ref, slope_ref, params_ref, stats_ref, out_ref, incoming_ref):
@@ -344,8 +349,8 @@
 
 def weight_first_kernel(
     table_ref, params_ref, stats_ref, value_hbm, bundle_hbm, other_hbm,
-    slope_ref, act_hbm, first_hbm,
-    columns_ref, act_first_ref, act_ref, first_ref, value_ref, bundle_ref, other_ref, fields_ref, sems,
+    slope_ref, act_ref, first_ref,
+    columns_ref, act_first_ref, value_ref, bundle_ref, other_ref, fields_ref, sems,
 ):
     copies = copy_in([(bundle_hbm, bundle_ref), (other_hbm, other_ref), (value_hbm, value_ref)], sems)
     table = jnp.sum(table_ref[...], axis=0)
@@ -359,8 +364,6 @@
     copies[1].wait()
     put_acts(0, bundle_ref, other_ref, params_ref, act_first_ref)
     put_acts(1, bundle_ref, other_ref, params_ref, act_ref)
-    acts_out = pltpu.make_async_copy(act_ref, act_hbm, sems.at[3])
-    acts_out.start()
     for f in range(FRAMES):
         mean, rstd = row(stats_ref, MEAN0 + f), row(stats_ref, RSTD0 + f)
         for at, count, mask in ((0, 1, OTHER_TOP), (1, ROWS, LIVE), (1 + ROWS, 1, OTHER_BOTTOM)):
@@ -384,15 +387,9 @@
         right = jnp.where(column == 0, 0.0, pltpu.roll(value, 1, 0))
         fill(f, left.astype(BF16), value.astype(BF16), right.astype(BF16))
     for kt in range(3):
-        for dy in (-1, 0, 1):
-            terms = kernel_terms(columns_ref, act_first_ref, kt, dy)
-            tap = 9 * kt + 3 * (dy + 1)
-            for dx in range(3):
-                first_ref[tap + dx] = terms[:, dx * CH : (dx + 1) * CH]
-    first_out = pltpu.make_async_copy(first_ref, first_hbm, sems.at[4])
-    first_out.start()
-    acts_out.wait()
-    first_out.wait()
+        terms = kernel_terms(columns_ref, act_first_ref, kt)
+        for n in range(9):
+            first_ref[9 * kt + n] = terms[:, n * CH : (n + 1) * CH].astype(first_ref.dtype)
 
 
 def fields_second_kernel(
@@ -421,12 +418,9 @@
 
 
 def weight_second_kernel(
-    scale, chunk, table_ref, fields_ref, params_ref, stats_ref, first_hbm, act_hbm,
-    out_hbm, own_hbm, parts_ref, columns_ref, sum_ref, act_ref, first_ref, out_ref, sems,
+    scale, chunk, table_ref, fields_ref, params_ref, stats_ref, first_ref, act_ref,
+    out_hbm, own_hbm, parts_ref, columns_ref, sum_ref, out_ref, sems,
 ):
-    arrive = copy_in(
-        [(act_hbm, act_ref)] + [(first_hbm.at[n : n + 3], first_ref.at[n : n + 3]) for n in range(0, TAPS, 3)], sems
-    )
     table = jnp.sum(table_ref[...], axis=0)
     parts_ref[...] = table[2:4] * scale
     for strip, top, bottom in ((0, TURN + TOP, TURN + BOTTOM), (1, OTHER_TURN + OTHER_TOP, OTHER_TURN + OTHER_BOTTOM)):
@@ -434,22 +428,18 @@
             store_columns(columns_ref, (strip,)), table[0:2], fields_ref, (strip,), params_ref, stats_ref,
             RSTD1, 1, 1, (top, TURN + LIVE, bottom),
         )
-    copy_own = pltpu.make_async_copy(columns_ref.at[0], own_hbm, sems.at[10])
+    copy_own = pltpu.make_async_copy(columns_ref.at[0], own_hbm, sems.at[0])
     copy_own.start()
-    arrive[0].wait()
     second = row(params_ref, CORE) > 0.5
     filler = jnp.zeros((out_ref.shape[1] - chunk, CH), F32)
     chips = out_ref.shape[0]
     done = 0
     copies = [copy_own]
     for kt in range(3):
-        for dy in (-1, 0, 1):
-            terms = kernel_terms(columns_ref, act_ref, kt, dy)
-            tap = 9 * kt + 3 * (dy + 1)
-            arrive[1 + tap // 3].wait()
-            for dx in range(3):
-                at = (tap + dx) * CH
-                sum_ref[at : at + CH] = first_ref[tap + dx] + terms[:, dx * CH : (dx + 1) * CH]
+        terms = kernel_terms(columns_ref, act_ref, kt)
+        for n in range(9 * kt, 9 * kt + 9):
+            at = (n - 9 * kt) * CH
+            sum_ref[n * CH : (n + 1) * CH] = first_ref[n].astype(F32) + terms[:, at : at + CH]
         begin = done
         while done < chips and 2 * (done + 1) * chunk <= 9 * (kt + 1) * CH:
             at = 2 * done * chunk
@@ -459,7 +449,7 @@
             out_ref[done] = mine.astype(BF16)
             done += 1
         if done > begin:
-            send = pltpu.make_async_copy(out_ref.at[begin:done], out_hbm.at[begin:done], sems.at[11 + kt])
+            send = pltpu.make_async_copy(out_ref.at[begin:done], out_hbm.at[begin:done], sems.at[1 + kt])
             send.start()
             copies.append(send)
     for copy in copies:
@@ -469,7 +459,8 @@
 def conv_second_kernel(
     params_ref, columns_hbm, first_hbm, taps_ref, out_ref, weight_ref, columns_ref, first_ref, sum_ref, sems
 ):
-    for copy in copy_in([(columns_hbm, columns_ref), (first_hbm, first_ref), (taps_ref, weight_ref)], sems):
+    pairs = [(columns_hbm, columns_ref), (first_hbm, first_ref)] + weight_copies(taps_ref, weight_ref)
+    for copy in copy_in(pairs, sems):
         copy.wait()
     conv(columns_ref, weight_ref, params_ref, 1, ROWS, sum_ref)
     out_ref[0] = first_ref[:, 1 : 1 + ROWS]
@@ -523,7 +514,7 @@
     flags = jnp.stack([x.astype(jnp.int32) for x in flags])
     pre, act = pre_norm[0], activations[0]
     cot, loss = cot_first[0], loss_grad[0]
-    taps = weight[0]
+    taps = weight[0].reshape(3, 9, CH, CH)
     edge = (FRAMES, ROWS + 2, COLS, CH)
     strip = (FRAMES, ROWS, COLS, CH)
     bundled = (FRAMES, 3 * (ROWS + 2) + 2 * ROWS, COLS, CH)
@@ -565,13 +556,13 @@
     )
     other_bundle = lax.ppermute(bundle, "dp", mates)
 
-    weights = pltpu.VMEM((TAPS * CH, CH), BF16)
+    weights = pltpu.VMEM((3, CH, 9 * CH), BF16)
     grad_first, value = call(
         conv_first_kernel, "conv_first", (table, first_fields, params, stats, taps),
         (shape(edge, BF16), in_hbm(edge, BF16)),
         scratch=[
             pltpu.VMEM(columns_of(ROWS + 4), BF16), weights, pltpu.VMEM(edge, BF16),
-            pltpu.VMEM((FRAMES, (ROWS + 2) * COLS, CH), F32), sems(2),
+            pltpu.VMEM((FRAMES, (ROWS + 2) * COLS, CH), F32), sems(10),
         ],
         specs="vkkkh", flops=20_000_000_000,
     )
@@ -582,9 +573,9 @@
     acts_dims, taps_dims = (CH, 2 * 9 * CH), (TAPS, CH, CH)
     slope, acts, weight_first = call(
         weight_first_kernel, "weight_first", (table, params, stats, value, bundle, other_bundle),
-        (kept((2,) + strip), in_hbm(acts_dims, BF16), in_hbm(taps_dims)),
-        scratch=[both, pltpu.VMEM(acts_dims, BF16), pltpu.VMEM(acts_dims, BF16), pltpu.VMEM(taps_dims, F32)]
-        + [pltpu.VMEM(edge, BF16)] + [pltpu.VMEM(bundled, BF16)] * 2 + [pltpu.VMEM((2,) + edge, F32), sems(5)],
+        (kept((2,) + strip), kept(acts_dims, BF16), kept(taps_dims, BF16)),
+        scratch=[both, pltpu.VMEM(acts_dims, BF16)]
+        + [pltpu.VMEM(edge, BF16)] + [pltpu.VMEM(bundled, BF16)] * 2 + [pltpu.VMEM((2,) + edge, F32), sems(3)],
         specs="vkkhhh",
     )
 
@@ -604,10 +595,10 @@
         (table, second_fields, params, stats, weight_first, acts),
         (in_hbm((chips, padded, CH), BF16), in_hbm(columns_of(ROWS + 2), BF16), shape((2, CH))),
         scratch=[
-            both, pltpu.VMEM((TAPS * CH, CH), F32), pltpu.VMEM(acts_dims, BF16), pltpu.VMEM(taps_dims, F32),
-            pltpu.VMEM((chips, padded, CH), BF16), sems(14),
+            both, pltpu.VMEM((TAPS * CH, CH), F32),
+            pltpu.VMEM((chips, padded, CH), BF16), sems(4),
         ],
-        specs="vkkkhh",
+        specs="vkkkkk",
     )
     sides = [[2 * i + core for i in range(chips)] for core in range(2)]
     terms = lax.all_to_all(terms, "dp", 0, 0, axis_index_groups=sides, tiled=True)
@@ -619,7 +610,7 @@
         (shape((2, FRAMES, ROWS, COLS, CH), BF16),),
         scratch=[
             weights, pltpu.VMEM(columns_of(ROWS + 2), BF16), pltpu.VMEM(edge, BF16),
-            pltpu.VMEM((FRAMES, ROWS * COLS, CH), F32), sems(3),
+            pltpu.VMEM((FRAMES, ROWS * COLS, CH), F32), sems(11),
         ],
         specs="khhh",
     )

time: 103 us -> 101 us (0.981)
  Pallas kernels: 23.2 us -> 20.1 us
  waiting for transfers between devices: 30.2 us -> 31.4 us
    pallas_call x10, Pallas kernels: 23.2 us -> 20.1 us  [call(): pl.pallas_call(kernel, out_shape=tuple(outs), in_specs=[{'v': VMEM, 'k':...]
    ppermute x1, waiting for transfers between devices: 2.14 us -> 3.4 us  [local(): lax.ppermute(grad_first, 'segment', [(i + 1, i) for i in range(count - 1)])]
  transfers between devices with their start and end apart: 9 -> 9, of which waited for: 6 -> 6; matrix products, arithmetic and copies ran while one was open for 1% -> 1% of each run, Pallas kernels for 15% -> 14%
where the time goes in v5:
time: 101 us
  starting transfers between devices  46.6 us (46%)
  waiting for transfers between devices  31.4 us (31%)
  Pallas kernels  20.1 us (20%)
  local copies, waits for them, and re-layouts  1.66 us (2%)
    all_to_all x3, starting transfers between devices, exchange(): return lax.all_to_all(table, 'dp', 0, 0, tiled=True)  30.8 us
    pallas_call x10, Pallas kernels, call(): pl.pallas_call(kernel, out_shape=tuple(outs), in_specs=[{'v': VMEM, 'k':...  20.1 us
    all_to_all x3, waiting for transfers between devices, exchange(): return lax.all_to_all(table, 'dp', 0, 0, tiled=True)  13.8 us
    all_to_all x1, waiting for transfers between devices, local(): lax.all_to_all(terms, 'dp', 0, 0, axis_index_groups=sides, tiled=True)  12.9 us
    all_to_all x1, starting transfers between devices, local(): lax.all_to_all(terms, 'dp', 0, 0, axis_index_groups=sides, tiled=True)  4.81 us
    ppermute x1, starting transfers between devices, local(): down = lax.ppermute(head, 'dp', [(i + 1, i) for i in range(dp - 1)])  3.51 us
    ppermute x1, waiting for transfers between devices, local(): lax.ppermute(grad_first, 'segment', [(i + 1, i) for i in range(count - 1)])  3.4 us
    ppermute x1, starting transfers between devices, local(): up = lax.ppermute(tail, 'dp', [(i, i + 1) for i in range(dp - 1)])  2.06 us
  transfers between devices with their start and end apart: 9, of which 6 were waited for; matrix products, arithmetic and copies ran while one was open for 1% of the time, Pallas kernels for 14%

profile of v5, /device:TPU:8, one launch (start us, length us, event | category | flops | bytes accessed | tf_op | source)
XLA Modules:
  0.0 100.6 jit_solution(13097284313542994154)
XLA Ops:
  0.6 2.0 %sums.1 = (f32[64,4,128]{2,1,0:T(4,128)}, bf16[4,6,32,128]{3,2,1,0:T(8,128)(2,1)S(1)}, bf16[4,6,32,128]{3,2,1,0:T(8,128)(2,1)S(1)}, f32[2,4,4,32,128]{4,3,2,1,0:T(8,128)S(1)}, f32[80,128]{1,0:T(8,128)S(1)}) custom-call(s32[1,2,1,4]{3,2,1,0:T(1,128)} %clip_hbm.1, bf16[2,4,4,32,128]{4,3,2,1,0:T(8,128)(2,1)} %bitcast.13, bf16[4,4,32,128]{3,2,1,0:T(8,128)(2,1)} %bitcast.17, ...), custom_call_target="tpu_custom_call" | custom-call | flops 1000000 | bytes 525344 | tf_op jit(solution)/shard_map/sums/pallas_call | solution.py:481
  2.7 17.2 %all-to-all-start = ((f32[64,4,128]{2,1,0:T(4,128)}), f32[64,4,128]{2,1,0:T(4,128)S(1)}, u32[]{:S(2)}, u32[]{:S(2)}) async-start(f32[64,4,128]{2,1,0:T(4,128)} %get-tuple-element.28), calls=%async_computation | async-start | bytes 262144 | tf_op jit(solution)/shard_map/all_to_all | solution.py:526
  19.8 2.1 %collective-permute-start = (bf16[4,6,32,128]{3,2,1,0:T(8,128)(2,1)S(1)}, bf16[4,6,32,128]{3,2,1,0:T(8,128)(2,1)S(1)}, u32[]{:S(2)}, u32[]{:S(2)}) collective-permute-start(bf16[4,6,32,128]{3,2,1,0:T(8,128)(2,1)S(1)} %get-tuple-element.25), channel_id=1, source_target_pairs={{0,1},{1,2},{2,3},{3,4},{4,5},{5,6},{6,7},{7,8},{8,9},{9,10},{10,1... | collective-permute-start | bytes 589832 | tf_op jit(solution)/shard_map/ppermute | solution.py:541
  21.9 3.5 %collective-permute-start.1 = (bf16[4,6,32,128]{3,2,1,0:T(8,128)(2,1)S(1)}, bf16[4,6,32,128]{3,2,1,0:T(8,128)(2,1)S(1)}, u32[]{:S(2)}, u32[]{:S(2)}) collective-permute-start(bf16[4,6,32,128]{3,2,1,0:T(8,128)(2,1)S(1)} %get-tuple-element.26), channel_id=1, source_target_pairs={{1,0},{2,1},{3,2},{4,3},{5,4},{6,5},{7,6},{8,7},{9,8},{10,9},{11,1... | collective-permute-start | bytes 589832 | tf_op jit(solution)/shard_map/ppermute | solution.py:540
  25.4 4.6 %all-to-all-done.table_ref = f32[64,4,128]{2,1,0:T(4,128)S(1)} async-done(((f32[64,4,128]{2,1,0:T(4,128)}), f32[64,4,128]{2,1,0:T(4,128)S(1)}, u32[]{:S(2)}, u32[]{:S(2)}) %all-to-all-start) | async-done | bytes 131104 | tf_op jit(solution)/shard_map/all_to_all | solution.py:526
  30.0 1.2 %act_first.1 = (f32[64,2,128]{2,1,0:T(2,128)}, f32[24,128]{1,0:T(8,128)S(1)}) custom-call(f32[64,4,128]{2,1,0:T(4,128)S(1)} %all-to-all-done.table_ref, f32[2,4,4,32,128]{4,3,2,1,0:T(8,128)S(1)} %get-tuple-element.29.own_ref, f32[80,128]{1,0:T(8,128)S(1)} %get-tuple-element.27.params_ref.plain_ref), custom_call_target="tpu_custom_call" | custom-call | flops 1000000 | bytes 696320 | tf_op jit(solution)/shard_map/act_first/pallas_call | solution.py:481
  31.2 7.1 %all-to-all-start.1 = ((f32[64,2,128]{2,1,0:T(2,128)}), f32[64,2,128]{2,1,0:T(2,128)S(1)}, u32[]{:S(2)}, u32[]{:S(2)}) async-start(f32[64,2,128]{2,1,0:T(2,128)} %get-tuple-element.32), calls=%async_computation.1 | async-start | bytes 131072 | tf_op jit(solution)/shard_map/all_to_all | solution.py:526
  38.3 0.1 stack.47.flag_ref
  38.4 0.0 collective-permute-done.up_ref
  38.4 0.0 collective-permute-done.1.down_ref
  38.4 2.7 %fields_first.1 = (f32[2,4,8,32,128]{4,3,2,1,0:T(8,128)S(1)}, bf16[4,26,32,128]{3,2,1,0:T(8,128)(2,1)}, bf16[4,6,32,128]{3,2,1,0:T(8,128)(2,1)S(1)}, f32[80,128]{1,0:T(8,128)S(1)}) custom-call(s32[6]{0:T(128)S(1)} %stack.47.flag_ref, bf16[4,6,32,128]{3,2,1,0:T(8,128)(2,1)S(1)} %collective-permute-done.up_ref, ...), custom_call_target="tpu_custom_call" | custom-call | flops 1000000 | bytes 1232920 | tf_op jit(solution)/shard_map/fields_first/pallas_call | solution.py:481
  41.1 2.1 %collective-permute-start.3 = (bf16[4,26,32,128]{3,2,1,0:T(8,128)(2,1)}, bf16[4,26,32,128]{3,2,1,0:T(8,128)(2,1)S(1)}, u32[]{:S(2)}, u32[]{:S(2)}) collective-permute-start(bf16[4,26,32,128]{3,2,1,0:T(8,128)(2,1)} %get-tuple-element.37.bundle_hbm), channel_id=1, source_target_pairs={{0,1},{1,0},{2,3},{3,2},{4,5},{5,4},{6,7},{7,6},{8,9},{9,8},{10,11... | collective-permute-start | bytes 2555912 | tf_op jit(solution)/shard_map/ppermute | solution.py:557
  43.2 4.0 %all-to-all-done.1.table_ref = f32[64,2,128]{2,1,0:T(2,128)S(1)} async-done(((f32[64,2,128]{2,1,0:T(2,128)}), f32[64,2,128]{2,1,0:T(2,128)S(1)}, u32[]{:S(2)}, u32[]{:S(2)}) %all-to-all-start.1) | async-done | bytes 65568 | tf_op jit(solution)/shard_map/all_to_all | solution.py:526
  47.2 2.6 %conv_first.1 = (bf16[4,6,32,128]{3,2,1,0:T(8,128)(2,1)S(1)}, bf16[4,6,32,128]{3,2,1,0:T(8,128)(2,1)}) custom-call(f32[64,2,128]{2,1,0:T(2,128)S(1)} %all-to-all-done.1.table_ref, f32[2,4,8,32,128]{4,3,2,1,0:T(8,128)S(1)} %get-tuple-element.33.fields_ref, f32[80,128]{1,0:T(8,128)S(1)} %get-tuple-element.31.params_ref, ...), custom_call_target="tpu_custom_call" | custom-call | flops 20000000000 | bytes 2052096 | tf_op jit(solution)/shard_map/conv_first/pallas_call | solution.py:481
  49.8 0.0 copy-start
  49.8 1.3 %collective-permute-start.2 = (bf16[4,6,32,128]{3,2,1,0:T(8,128)(2,1)S(1)}, bf16[4,6,32,128]{3,2,1,0:T(8,128)(2,1)S(1)}, u32[]{:S(2)}, u32[]{:S(2)}) collective-permute-start(bf16[4,6,32,128]{3,2,1,0:T(8,128)(2,1)S(1)} %get-tuple-element.34.first_hbm), channel_id=1, source_target_pairs={{64,0},{128,64},{192,128},{256,192},{320,256},{384,320},{448,384},... | collective-permute-start | bytes 589832 | tf_op jit(solution)/shard_map/ppermute | solution.py:570
  51.1 0.0 collective-permute-done.3.other_hbm
  51.1 0.0 copy-start.1
  51.1 1.0 copy-done.1
  52.1 3.1 %weight_first.1 = (f32[2,4,4,32,128]{4,3,2,1,0:T(8,128)S(1)}, bf16[128,2304]{1,0:T(8,128)(2,1)S(1)}, bf16[27,128,128]{2,1,0:T(8,128)(2,1)S(1)}) custom-call(f32[64,2,128]{2,1,0:T(2,128)S(1)} %all-to-all-done.1.table_ref, f32[80,128]{1,0:T(8,128)S(1)} %get-tuple-element.31.params_ref, f32[24,128]{1,0:T(8,128)S(1)} %get-tuple-element.30.stats_ref, ...), custom_call_target="tpu_custom_call" | custom-call | flops 1000000 | bytes 2019328 | tf_op jit(solution)/shard_map/weight_first/pallas_call | solution.py:481
  55.2 3.4 %collective-permute-done.2.hand_ref = bf16[4,6,32,128]{3,2,1,0:T(8,128)(2,1)S(1)} collective-permute-done((bf16[4,6,32,128]{3,2,1,0:T(8,128)(2,1)S(1)}, bf16[4,6,32,128]{3,2,1,0:T(8,128)(2,1)S(1)}, u32[]{:S(2)}, u32[]{:S(2)}) %collective-permute-start.2) | collective-permute-done | bytes 196640 | tf_op jit(solution)/shard_map/ppermute | solution.py:570
  58.6 0.9 act_second.1
  59.5 0.0 copy-done
  59.5 6.5 %all-to-all-start.2 = ((f32[64,4,128]{2,1,0:T(4,128)}), f32[64,4,128]{2,1,0:T(4,128)S(1)}, u32[]{:S(2)}, u32[]{:S(2)}) async-start(f32[64,4,128]{2,1,0:T(4,128)} %get-tuple-element.39), calls=%async_computation.2 | async-start | bytes 262144 | tf_op jit(solution)/shard_map/all_to_all | solution.py:526
  66.1 2.1 %collective-permute-start.4 = (bf16[4,6,32,128]{3,2,1,0:T(8,128)(2,1)S(1)}, bf16[4,6,32,128]{3,2,1,0:T(8,128)(2,1)S(1)}, u32[]{:S(2)}, u32[]{:S(2)}) collective-permute-start(bf16[4,6,32,128]{3,2,1,0:T(8,128)(2,1)S(1)} %get-tuple-element.40.incoming_ref), channel_id=1, source_target_pairs={{0,1},{1,0},{2,3},{3,2},{4,5},{5,4},{6,7},{7,6},{8,9},{9,8},{10,11... | collective-permute-start | bytes 589832 | tf_op jit(solution)/shard_map/ppermute | solution.py:587
  68.1 1.3 %collective-permute-done.4.arrived_ref = bf16[4,6,32,128]{3,2,1,0:T(8,128)(2,1)S(1)} collective-permute-done((bf16[4,6,32,128]{3,2,1,0:T(8,128)(2,1)S(1)}, bf16[4,6,32,128]{3,2,1,0:T(8,128)(2,1)S(1)}, u32[]{:S(2)}, u32[]{:S(2)}) %collective-permute-start.4) | collective-permute-done | bytes 196640 | tf_op jit(solution)/shard_map/ppermute | solution.py:587
  69.4 1.5 %fields_second.1.fields_ref = f32[2,2,4,6,32,128]{5,4,3,2,1,0:T(8,128)S(1)} custom-call(bf16[4,6,32,128]{3,2,1,0:T(8,128)(2,1)S(1)} %get-tuple-element.40.incoming_ref, bf16[4,6,32,128]{3,2,1,0:T(8,128)(2,1)S(1)} %collective-permute-done.4.arrived_ref, bf16[4,26,32,128]{3,2,1,0:T(8,128)(2,1)} %get-tuple-element.37.bundle_hbm, ...), custom_call_target="tpu_custom_call" | custom-call | flops 1000000 | bytes 2150400 | tf_op jit(solution)/shard_map/fields_second/pallas_call | solution.py:481
  70.9 5.2 %all-to-all-done.2.table_ref = f32[64,4,128]{2,1,0:T(4,128)S(1)} async-done(((f32[64,4,128]{2,1,0:T(4,128)}), f32[64,4,128]{2,1,0:T(4,128)S(1)}, u32[]{:S(2)}, u32[]{:S(2)}) %all-to-all-start.2) | async-done | bytes 131104 | tf_op jit(solution)/shard_map/all_to_all | solution.py:526
  76.1 2.3 %weight_second.1 = (bf16[32,56,128]{2,1,0:T(8,128)(2,1)}, bf16[4,192,384]{2,1,0:T(8,128)(2,1)}, f32[2,128]{1,0:T(2,128)S(1)}) custom-call(f32[64,4,128]{2,1,0:T(4,128)S(1)} %all-to-all-done.2.table_ref, f32[2,2,4,6,32,128]{5,4,3,2,1,0:T(8,128)S(1)} %fields_second.1.fields_ref, f32[80,128]{1,0:T(8,128)S(1)} %get-tuple-element.31.params_ref, ...), custom_call_target="tpu_custom_call" | custom-call | flops 1000000 | bytes 3231744 | tf_op jit(solution)/shard_map/weight_second/pallas_call | solution.py:481
  78.5 4.8 %all-to-all-start.3 = ((bf16[32,56,128]{2,1,0:T(8,128)(2,1)}), bf16[32,56,128]{2,1,0:T(8,128)(2,1)S(1)}, u32[]{:S(2)}, u32[]{:S(2)}) async-start(bf16[32,56,128]{2,1,0:T(8,128)(2,1)} %get-tuple-element.44), calls=%async_computation.3 | async-start | bytes 917504 | tf_op jit(solution)/shard_map/all_to_all | solution.py:604
  83.3 3.0 %conv_second.1 = bf16[2,4,4,32,128]{4,3,2,1,0:T(8,128)(2,1)} custom-call(f32[80,128]{1,0:T(8,128)S(1)} %get-tuple-element.31.params_ref, bf16[4,192,384]{2,1,0:T(8,128)(2,1)} %get-tuple-element.43.columns_hbm, bf16[4,6,32,128]{3,2,1,0:T(8,128)(2,1)} %copy-done, bf16[3,9,128,128]{3,2,1,0:T(8,128)(2,1)} %bitcast.16), custom_call_target="tpu_custom_call" | custom-call | flops 1000000 | bytes 1712128 | tf_op jit(solution)/shard_map/conv_second/pallas_call | solution.py:481
  86.3 0.1 constant_dynamic-slice_fusion
  86.4 0.5 fusion
  86.9 12.9 %all-to-all-done.3.terms_ref = bf16[32,56,128]{2,1,0:T(8,128)(2,1)S(1)} async-done(((bf16[32,56,128]{2,1,0:T(8,128)(2,1)}), bf16[32,56,128]{2,1,0:T(8,128)(2,1)S(1)}, u32[]{:S(2)}, u32[]{:S(2)}) %all-to-all-start.3) | async-done | bytes 458784 | tf_op jit(solution)/shard_map/all_to_all | solution.py:604
  99.8 0.7 total.1
Async XLA Ops:
  2.7 27.3 %all-to-all-start = ((f32[64,4,128]{2,1,0:T(4,128)}), f32[64,4,128]{2,1,0:T(4,128)S(1)}, u32[]{:S(2)}, u32[]{:S(2)}) async-start(f32[64,4,128]{2,1,0:T(4,128)} %get-tuple-element.28), calls=%async_computation | async-start | bytes 262144 | tf_op jit(solution)/shard_map/all_to_all | solution.py:526
  19.8 18.5 %collective-permute-start = (bf16[4,6,32,128]{3,2,1,0:T(8,128)(2,1)S(1)}, bf16[4,6,32,128]{3,2,1,0:T(8,128)(2,1)S(1)}, u32[]{:S(2)}, u32[]{:S(2)}) collective-permute-start(bf16[4,6,32,128]{3,2,1,0:T(8,128)(2,1)S(1)} %get-tuple-element.25), channel_id=1, source_target_pairs={{0,1},{1,2},{2,3},{3,4},{4,5},{5,6},{6,7},{7,8},{8,9},{9,10},{10,1... | collective-permute-start | bytes 589832 | tf_op jit(solution)/shard_map/ppermute | solution.py:541
  21.9 16.5 %collective-permute-start.1 = (bf16[4,6,32,128]{3,2,1,0:T(8,128)(2,1)S(1)}, bf16[4,6,32,128]{3,2,1,0:T(8,128)(2,1)S(1)}, u32[]{:S(2)}, u32[]{:S(2)}) collective-permute-start(bf16[4,6,32,128]{3,2,1,0:T(8,128)(2,1)S(1)} %get-tuple-element.26), channel_id=1, source_target_pairs={{1,0},{2,1},{3,2},{4,3},{5,4},{6,5},{7,6},{8,7},{9,8},{10,9},{11,1... | collective-permute-start | bytes 589832 | tf_op jit(solution)/shard_map/ppermute | solution.py:540
  31.2 16.0 %all-to-all-start.1 = ((f32[64,2,128]{2,1,0:T(2,128)}), f32[64,2,128]{2,1,0:T(2,128)S(1)}, u32[]{:S(2)}, u32[]{:S(2)}) async-start(f32[64,2,128]{2,1,0:T(2,128)} %get-tuple-element.32), calls=%async_computation.1 | async-start | bytes 131072 | tf_op jit(solution)/shard_map/all_to_all | solution.py:526
  41.1 10.0 %collective-permute-start.3 = (bf16[4,26,32,128]{3,2,1,0:T(8,128)(2,1)}, bf16[4,26,32,128]{3,2,1,0:T(8,128)(2,1)S(1)}, u32[]{:S(2)}, u32[]{:S(2)}) collective-permute-start(bf16[4,26,32,128]{3,2,1,0:T(8,128)(2,1)} %get-tuple-element.37.bundle_hbm), channel_id=1, source_target_pairs={{0,1},{1,0},{2,3},{3,2},{4,5},{5,4},{6,7},{7,6},{8,9},{9,8},{10,11... | collective-permute-start | bytes 2555912 | tf_op jit(solution)/shard_map/ppermute | solution.py:557
  49.8 9.8 %copy-start = (bf16[4,6,32,128]{3,2,1,0:T(8,128)(2,1)}, bf16[4,6,32,128]{3,2,1,0:T(8,128)(2,1)S(1)}, u32[]{:S(2)}) copy-start(bf16[4,6,32,128]{3,2,1,0:T(8,128)(2,1)S(1)} %get-tuple-element.34.first_hbm) | copy-start | bytes 589828
  49.8 8.8 %collective-permute-start.2 = (bf16[4,6,32,128]{3,2,1,0:T(8,128)(2,1)S(1)}, bf16[4,6,32,128]{3,2,1,0:T(8,128)(2,1)S(1)}, u32[]{:S(2)}, u32[]{:S(2)}) collective-permute-start(bf16[4,6,32,128]{3,2,1,0:T(8,128)(2,1)S(1)} %get-tuple-element.34.first_hbm), channel_id=1, source_target_pairs={{64,0},{128,64},{192,128},{256,192},{320,256},{384,320},{448,384},... | collective-permute-start | bytes 589832 | tf_op jit(solution)/shard_map/ppermute | solution.py:570
  51.1 1.0 copy-start.1
  59.5 16.6 %all-to-all-start.2 = ((f32[64,4,128]{2,1,0:T(4,128)}), f32[64,4,128]{2,1,0:T(4,128)S(1)}, u32[]{:S(2)}, u32[]{:S(2)}) async-start(f32[64,4,128]{2,1,0:T(4,128)} %get-tuple-element.39), calls=%async_computation.2 | async-start | bytes 262144 | tf_op jit(solution)/shard_map/all_to_all | solution.py:526
  66.1 3.3 %collective-permute-start.4 = (bf16[4,6,32,128]{3,2,1,0:T(8,128)(2,1)S(1)}, bf16[4,6,32,128]{3,2,1,0:T(8,128)(2,1)S(1)}, u32[]{:S(2)}, u32[]{:S(2)}) collective-permute-start(bf16[4,6,32,128]{3,2,1,0:T(8,128)(2,1)S(1)} %get-tuple-element.40.incoming_ref), channel_id=1, source_target_pairs={{0,1},{1,0},{2,3},{3,2},{4,5},{5,4},{6,7},{7,6},{8,9},{9,8},{10,11... | collective-permute-start | bytes 589832 | tf_op jit(solution)/shard_map/ppermute | solution.py:587
  78.5 21.4 %all-to-all-start.3 = ((bf16[32,56,128]{2,1,0:T(8,128)(2,1)}), bf16[32,56,128]{2,1,0:T(8,128)(2,1)S(1)}, u32[]{:S(2)}, u32[]{:S(2)}) async-start(bf16[32,56,128]{2,1,0:T(8,128)(2,1)} %get-tuple-element.44), calls=%async_computation.3 | async-start | bytes 917504 | tf_op jit(solution)/shard_map/all_to_all | solution.py:604

commit v6 on v5

--- a/solution.py
+++ b/solution.py
@@ -82,19 +82,19 @@
 
 
 def sums_kernel(
-    cells, clip_hbm, pre_ref, cot_ref, loss_ref, gain_ref, shift_ref,
-    out_ref, head_ref, tail_ref, own_ref, params_ref, clip_ref, held_ref, held_cot, sems,
+    cells, odd_ref, clip_hbm, pre_ref, cot_ref, loss_ref, gain_ref, shift_ref,
+    out_ref, inner_ref, outer_ref, own_ref, params_ref, clip_ref, held_ref, held_cot, sems,
 ):
     pairs = [
         (clip_hbm, clip_ref), (pre_ref, held_ref), (cot_ref, held_cot),
         (gain_ref, params_ref.at[GAIN : GAIN + 1]), (shift_ref, params_ref.at[SHIFT : SHIFT + 1]),
     ]
-    for ref, two, one in ((head_ref, 0, 0), (tail_ref, ROWS - 2, ROWS - 1)):
+    odd = odd_ref[0]
+    for ref, side in ((inner_ref, 1 - odd), (outer_ref, odd)):
+        two, one = pl.ds(side * (ROWS - 2), 2), pl.ds(side * (ROWS - 1), 1)
         pairs += [
-            (pre_ref.at[0, :, two : two + 2], ref.at[:, 0:2]),
-            (cot_ref.at[:, two : two + 2], ref.at[:, 2:4]),
-            (pre_ref.at[1, :, one : one + 1], ref.at[:, 4:5]),
-            (loss_ref.at[:, one : one + 1], ref.at[:, 5:6]),
+            (pre_ref.at[0, :, two], ref.at[:, 0:2]), (cot_ref.at[:, two], ref.at[:, 2:4]),
+            (pre_ref.at[1, :, one], ref.at[:, 4:5]), (loss_ref.at[:, one], ref.at[:, 5:6]),
         ]
     copies = copy_in(pairs, sems)
     params_ref[SHIFT + 1 :] = jnp.zeros((PARAM_ROWS - SHIFT - 1, CH), F32)
@@ -182,8 +182,8 @@
 
 
 def fields_first_kernel(
-    flag_ref, up_ref, down_ref, plain_ref, stats_ref, pre_ref, cot_ref, loss_ref, act_ref,
-    out_ref, bundle_hbm, loss_out_ref, params_ref, bundle_ref, held_loss, sems,
+    flag_ref, inner_ref, outer_ref, plain_ref, stats_ref, pre_ref, cot_ref, loss_ref, act_ref,
+    out_ref, bundle_hbm, loss_out_ref, params_ref, bundle_ref, held_loss, up_ref, down_ref, sems,
 ):
     copies = copy_in(
         [
@@ -194,6 +194,17 @@
         ],
         sems,
     )
+
+    @pl.when(flag_ref[4] == 0)
+    def even():
+        up_ref[...] = outer_ref[...]
+        down_ref[...] = inner_ref[...]
+
+    @pl.when(flag_ref[4] != 0)
+    def odd():
+        up_ref[...] = inner_ref[...]
+        down_ref[...] = outer_ref[...]
+
     params_ref[...] = plain_ref[...]
     flag = [flag_ref[n].astype(F32) for n in range(6)]
     for at, n in ((CORE, 4), (LAST, 5)):
@@ -283,10 +294,10 @@
 
 
 def conv_first_kernel(
-    table_ref, fields_ref, params_ref, stats_ref, taps_ref, grad_ref, value_hbm,
-    columns_ref, weight_ref, value_ref, sum_ref, sems,
+    table_ref, fields_ref, params_ref, stats_ref, taps_hbm, grad_ref, value_hbm,
+    columns_ref, taps_ref, weight_ref, value_ref, sum_ref, sems,
 ):
-    copies = copy_in(weight_copies(taps_ref, weight_ref), sems)
+    (copy,) = copy_in([(taps_hbm, taps_ref)], sems)
     table = jnp.sum(table_ref[...], axis=0)
     fill = store_columns(columns_ref)
 
@@ -297,10 +308,12 @@
     write_columns(
         store, table, fields_ref, (), params_ref, stats_ref, RSTD0, 0, 2, (TOP, LIVE, BOTTOM)
     )
-    value_out = pltpu.make_async_copy(value_ref, value_hbm, sems.at[9])
+    value_out = pltpu.make_async_copy(value_ref, value_hbm, sems.at[1])
     value_out.start()
-    for copy in copies:
-        copy.wait()
+    copy.wait()
+    for kt in range(3):
+        for n in range(9):
+            weight_ref[kt, :, n * CH : (n + 1) * CH] = taps_ref[kt, n]
     conv(columns_ref, weight_ref, params_ref, 0, ROWS + 2, sum_ref)
     grad_ref[...] = sum_ref[...].astype(BF16).reshape(grad_ref.shape)
     value_out.wait()
@@ -525,8 +538,8 @@
     def exchange(table):
         return lax.all_to_all(table, "dp", 0, 0, tiled=True)
 
-    table, head, tail, own, plain = call(
-        functools.partial(sums_kernel, cells), "sums", (frame_clip, pre, cot, loss, norm_gain, norm_shift),
+    table, inner, outer, own, plain = call(
+        functools.partial(sums_kernel, cells), "sums", ((me & 1).reshape(1), frame_clip, pre, cot, loss, norm_gain, norm_shift),
         (
             shape((dp, 4, CH)), shape(edge, BF16), shape(edge, BF16),
             kept((2,) + strip), kept((PARAM_ROWS, CH)),
@@ -534,11 +547,12 @@
         scratch=[
             pltpu.SMEM((1, 2, 1, FRAMES), jnp.int32), pltpu.VMEM((2,) + strip, BF16), pltpu.VMEM(strip, BF16), sems(13)
         ],
-        specs="hhhhhh",
+        specs="shhhhhh",
     )
     table = exchange(table)
-    down = lax.ppermute(head, "dp", [(i + 1, i) for i in range(dp - 1)])
-    up = lax.ppermute(tail, "dp", [(i, i + 1) for i in range(dp - 1)])
+    inner = lax.ppermute(inner, "dp", mates)
+    sides = [(i, i + 1) for i in range(1, dp - 1, 2)]
+    outer = lax.ppermute(outer, "dp", sides + [(j, i) for i, j in sides])
 
     table, stats = call(
         act_first_kernel, "act_first", (table, own, plain), (shape((dp, 2, CH)), kept((STAT_ROWS, CH))), specs="vkk"
@@ -546,12 +560,12 @@
     table = exchange(table)
 
     first_fields, bundle, loss_rows, params = call(
-        fields_first_kernel, "fields_first", (flags, up, down, plain, stats, pre, cot, loss, act),
+        fields_first_kernel, "fields_first", (flags, inner, outer, plain, stats, pre, cot, loss, act),
         (
             kept((2, FRAMES, ROWS + 4, COLS, CH)), in_hbm(bundled, BF16),
             kept(edge, BF16), kept((PARAM_ROWS, CH)),
         ),
-        scratch=[pltpu.VMEM(bundled, BF16), pltpu.VMEM(strip, BF16), sems(7)],
+        scratch=[pltpu.VMEM(bundled, BF16), pltpu.VMEM(strip, BF16)] + [pltpu.VMEM(edge, BF16)] * 2 + [sems(7)],
         specs="svvkkhhhh",
     )
     other_bundle = lax.ppermute(bundle, "dp", mates)
@@ -561,8 +575,8 @@
         conv_first_kernel, "conv_first", (table, first_fields, params, stats, taps),
         (shape(edge, BF16), in_hbm(edge, BF16)),
         scratch=[
-            pltpu.VMEM(columns_of(ROWS + 4), BF16), weights, pltpu.VMEM(edge, BF16),
-            pltpu.VMEM((FRAMES, (ROWS + 2) * COLS, CH), F32), sems(10),
+            pltpu.VMEM(columns_of(ROWS + 4), BF16), pltpu.VMEM((3, 9, CH, CH), BF16), weights, pltpu.VMEM(edge, BF16),
+            pltpu.VMEM((FRAMES, (ROWS + 2) * COLS, CH), F32), sems(2),
         ],
         specs="vkkkh", flops=20_000_000_000,
     )

time: 101 us -> 99.2 us (0.982)
  starting transfers between devices: 46.6 us -> 43.5 us
  waiting for transfers between devices: 31.4 us -> 32.6 us
    all_to_all x3, starting transfers between devices: 30.8 us -> 28.8 us  [exchange(): return lax.all_to_all(table, 'dp', 0, 0, tiled=True)]
    all_to_all x3, waiting for transfers between devices: 13.8 us -> 15 us  [exchange(): return lax.all_to_all(table, 'dp', 0, 0, tiled=True)]
    ppermute x2, starting transfers between devices: 5.56 us -> 4.49 us  [the longest x1 2.43 us: local(): outer = lax.ppermute(outer, 'dp', sides + [(j, i) for i, j in sides])]
where the time goes in v6:
time: 99.2 us; the launch traced here: 98.6 us
  starting transfers between devices  43.5 us (44%)
  waiting for transfers between devices  32.6 us (33%)
  Pallas kernels  20 us (20%)
  local copies, waits for them, and re-layouts  1.66 us (2%)
    all_to_all x3, starting transfers between devices, exchange(): return lax.all_to_all(table, 'dp', 0, 0, tiled=True)  28.8 us
    pallas_call x10, Pallas kernels, call(): pl.pallas_call(kernel, out_shape=tuple(outs), in_specs=[{'v': VMEM, 'k':...  20 us
    all_to_all x3, waiting for transfers between devices, exchange(): return lax.all_to_all(table, 'dp', 0, 0, tiled=True)  15 us
    all_to_all x1, waiting for transfers between devices, local(): lax.all_to_all(terms, 'dp', 0, 0, axis_index_groups=sides, tiled=True)  12.9 us
    all_to_all x1, starting transfers between devices, local(): lax.all_to_all(terms, 'dp', 0, 0, axis_index_groups=sides, tiled=True)  4.82 us
    ppermute x1, waiting for transfers between devices, local(): lax.ppermute(grad_first, 'segment', [(i + 1, i) for i in range(count - 1)])  3.4 us
    ppermute x1, starting transfers between devices, local(): outer = lax.ppermute(outer, 'dp', sides + [(j, i) for i, j in sides])  2.43 us
    ppermute x1, starting transfers between devices, local(): inner = lax.ppermute(inner, 'dp', mates)  2.06 us
  transfers between devices with their start and end apart: 9, of which 6 were waited for; matrix products, arithmetic and copies ran while one was open for 1% of the time, Pallas kernels for 14%

profile of v6, /device:TPU:8, one launch (start us, length us, event | category | flops | bytes accessed | tf_op | source)
XLA Modules:
  0.0 98.6 jit_solution(6179667054667150562)
XLA Ops:
  0.6 2.0 %sums.1 = (f32[64,4,128]{2,1,0:T(4,128)}, bf16[4,6,32,128]{3,2,1,0:T(8,128)(2,1)S(1)}, bf16[4,6,32,128]{3,2,1,0:T(8,128)(2,1)S(1)}, f32[2,4,4,32,128]{4,3,2,1,0:T(8,128)S(1)}, f32[80,128]{1,0:T(8,128)S(1)}) custom-call(s32[1]{0:T(128)} %bitcast.4.odd_ref, s32[1,2,1,4]{3,2,1,0:T(1,128)} %clip_hbm.1, bf16[2,4,4,32,128]{4,3,2,1,0:T(8,128)(2,1)} %bitcast.13, ...), custom_call_target="tpu_custom_call" | custom-call | flops 1000000 | bytes 525348 | tf_op jit(solution)/shard_map/sums/pallas_call | solution.py:494
  2.7 17.2 %all-to-all-start = ((f32[64,4,128]{2,1,0:T(4,128)}), f32[64,4,128]{2,1,0:T(4,128)S(1)}, u32[]{:S(2)}, u32[]{:S(2)}) async-start(f32[64,4,128]{2,1,0:T(4,128)} %get-tuple-element.28), calls=%async_computation | async-start | bytes 262144 | tf_op jit(solution)/shard_map/all_to_all | solution.py:539
  19.8 2.1 %collective-permute-start = (bf16[4,6,32,128]{3,2,1,0:T(8,128)(2,1)S(1)}, bf16[4,6,32,128]{3,2,1,0:T(8,128)(2,1)S(1)}, u32[]{:S(2)}, u32[]{:S(2)}) collective-permute-start(bf16[4,6,32,128]{3,2,1,0:T(8,128)(2,1)S(1)} %get-tuple-element.25), channel_id=1, source_target_pairs={{0,1},{1,0},{2,3},{3,2},{4,5},{5,4},{6,7},{7,6},{8,9},{9,8},{10,11... | collective-permute-start | bytes 589832 | tf_op jit(solution)/shard_map/ppermute | solution.py:553
  21.9 2.4 %collective-permute-start.1 = (bf16[4,6,32,128]{3,2,1,0:T(8,128)(2,1)S(1)}, bf16[4,6,32,128]{3,2,1,0:T(8,128)(2,1)S(1)}, u32[]{:S(2)}, u32[]{:S(2)}) collective-permute-start(bf16[4,6,32,128]{3,2,1,0:T(8,128)(2,1)S(1)} %get-tuple-element.26), channel_id=1, source_target_pairs={{1,2},{3,4},{5,6},{7,8},{9,10},{11,12},{13,14},{15,16},{17,18},{19... | collective-permute-start | bytes 589832 | tf_op jit(solution)/shard_map/ppermute | solution.py:555
  24.4 5.7 %all-to-all-done.table_ref = f32[64,4,128]{2,1,0:T(4,128)S(1)} async-done(((f32[64,4,128]{2,1,0:T(4,128)}), f32[64,4,128]{2,1,0:T(4,128)S(1)}, u32[]{:S(2)}, u32[]{:S(2)}) %all-to-all-start) | async-done | bytes 131104 | tf_op jit(solution)/shard_map/all_to_all | solution.py:539
  30.1 1.2 %act_first.1 = (f32[64,2,128]{2,1,0:T(2,128)}, f32[24,128]{1,0:T(8,128)S(1)}) custom-call(f32[64,4,128]{2,1,0:T(4,128)S(1)} %all-to-all-done.table_ref, f32[2,4,4,32,128]{4,3,2,1,0:T(8,128)S(1)} %get-tuple-element.29.own_ref, f32[80,128]{1,0:T(8,128)S(1)} %get-tuple-element.27.params_ref.plain_ref), custom_call_target="tpu_custom_call" | custom-call | flops 1000000 | bytes 696320 | tf_op jit(solution)/shard_map/act_first/pallas_call | solution.py:494
  31.3 5.1 %all-to-all-start.1 = ((f32[64,2,128]{2,1,0:T(2,128)}), f32[64,2,128]{2,1,0:T(2,128)S(1)}, u32[]{:S(2)}, u32[]{:S(2)}) async-start(f32[64,2,128]{2,1,0:T(2,128)} %get-tuple-element.32), calls=%async_computation.1 | async-start | bytes 131072 | tf_op jit(solution)/shard_map/all_to_all | solution.py:539
  36.4 0.1 stack.47.flag_ref
  36.5 0.0 collective-permute-done.inner_ref
  36.5 0.0 collective-permute-done.1.outer_ref
  36.5 2.7 %fields_first.1 = (f32[2,4,8,32,128]{4,3,2,1,0:T(8,128)S(1)}, bf16[4,26,32,128]{3,2,1,0:T(8,128)(2,1)}, bf16[4,6,32,128]{3,2,1,0:T(8,128)(2,1)S(1)}, f32[80,128]{1,0:T(8,128)S(1)}) custom-call(s32[6]{0:T(128)S(1)} %stack.47.flag_ref, bf16[4,6,32,128]{3,2,1,0:T(8,128)(2,1)S(1)} %collective-permute-done.inner_ref, ...), custom_call_target="tpu_custom_call" | custom-call | flops 1000000 | bytes 1232920 | tf_op jit(solution)/shard_map/fields_first/pallas_call | solution.py:494
  39.2 2.1 %collective-permute-start.3 = (bf16[4,26,32,128]{3,2,1,0:T(8,128)(2,1)}, bf16[4,26,32,128]{3,2,1,0:T(8,128)(2,1)S(1)}, u32[]{:S(2)}, u32[]{:S(2)}) collective-permute-start(bf16[4,26,32,128]{3,2,1,0:T(8,128)(2,1)} %get-tuple-element.37.bundle_hbm), channel_id=1, source_target_pairs={{0,1},{1,0},{2,3},{3,2},{4,5},{5,4},{6,7},{7,6},{8,9},{9,8},{10,11... | collective-permute-start | bytes 2555912 | tf_op jit(solution)/shard_map/ppermute | solution.py:571
  41.3 4.0 %all-to-all-done.1.table_ref = f32[64,2,128]{2,1,0:T(2,128)S(1)} async-done(((f32[64,2,128]{2,1,0:T(2,128)}), f32[64,2,128]{2,1,0:T(2,128)S(1)}, u32[]{:S(2)}, u32[]{:S(2)}) %all-to-all-start.1) | async-done | bytes 65568 | tf_op jit(solution)/shard_map/all_to_all | solution.py:539
  45.3 2.5 %conv_first.1 = (bf16[4,6,32,128]{3,2,1,0:T(8,128)(2,1)S(1)}, bf16[4,6,32,128]{3,2,1,0:T(8,128)(2,1)}) custom-call(f32[64,2,128]{2,1,0:T(2,128)S(1)} %all-to-all-done.1.table_ref, f32[2,4,8,32,128]{4,3,2,1,0:T(8,128)S(1)} %get-tuple-element.33.fields_ref, f32[80,128]{1,0:T(8,128)S(1)} %get-tuple-element.31.params_ref, ...), custom_call_target="tpu_custom_call" | custom-call | flops 20000000000 | bytes 2052096 | tf_op jit(solution)/shard_map/conv_first/pallas_call | solution.py:494
  47.8 0.0 copy-start
  47.8 1.3 %collective-permute-start.2 = (bf16[4,6,32,128]{3,2,1,0:T(8,128)(2,1)S(1)}, bf16[4,6,32,128]{3,2,1,0:T(8,128)(2,1)S(1)}, u32[]{:S(2)}, u32[]{:S(2)}) collective-permute-start(bf16[4,6,32,128]{3,2,1,0:T(8,128)(2,1)S(1)} %get-tuple-element.34.first_hbm), channel_id=1, source_target_pairs={{64,0},{128,64},{192,128},{256,192},{320,256},{384,320},{448,384},... | collective-permute-start | bytes 589832 | tf_op jit(solution)/shard_map/ppermute | solution.py:584
  49.1 0.0 collective-permute-done.3.other_hbm
  49.1 0.0 copy-start.1
  49.2 1.0 copy-done.1
  50.1 3.1 %weight_first.1 = (f32[2,4,4,32,128]{4,3,2,1,0:T(8,128)S(1)}, bf16[128,2304]{1,0:T(8,128)(2,1)S(1)}, bf16[27,128,128]{2,1,0:T(8,128)(2,1)S(1)}) custom-call(f32[64,2,128]{2,1,0:T(2,128)S(1)} %all-to-all-done.1.table_ref, f32[80,128]{1,0:T(8,128)S(1)} %get-tuple-element.31.params_ref, f32[24,128]{1,0:T(8,128)S(1)} %get-tuple-element.30.stats_ref, ...), custom_call_target="tpu_custom_call" | custom-call | flops 1000000 | bytes 2019328 | tf_op jit(solution)/shard_map/weight_first/pallas_call | solution.py:494
  53.2 3.4 %collective-permute-done.2.hand_ref = bf16[4,6,32,128]{3,2,1,0:T(8,128)(2,1)S(1)} collective-permute-done((bf16[4,6,32,128]{3,2,1,0:T(8,128)(2,1)S(1)}, bf16[4,6,32,128]{3,2,1,0:T(8,128)(2,1)S(1)}, u32[]{:S(2)}, u32[]{:S(2)}) %collective-permute-start.2) | collective-permute-done | bytes 196640 | tf_op jit(solution)/shard_map/ppermute | solution.py:584
  56.6 0.9 act_second.1
  57.6 0.0 copy-done
  57.6 6.5 %all-to-all-start.2 = ((f32[64,4,128]{2,1,0:T(4,128)}), f32[64,4,128]{2,1,0:T(4,128)S(1)}, u32[]{:S(2)}, u32[]{:S(2)}) async-start(f32[64,4,128]{2,1,0:T(4,128)} %get-tuple-element.39), calls=%async_computation.2 | async-start | bytes 262144 | tf_op jit(solution)/shard_map/all_to_all | solution.py:539
  64.1 2.1 %collective-permute-start.4 = (bf16[4,6,32,128]{3,2,1,0:T(8,128)(2,1)S(1)}, bf16[4,6,32,128]{3,2,1,0:T(8,128)(2,1)S(1)}, u32[]{:S(2)}, u32[]{:S(2)}) collective-permute-start(bf16[4,6,32,128]{3,2,1,0:T(8,128)(2,1)S(1)} %get-tuple-element.40.incoming_ref), channel_id=1, source_target_pairs={{0,1},{1,0},{2,3},{3,2},{4,5},{5,4},{6,7},{7,6},{8,9},{9,8},{10,11... | collective-permute-start | bytes 589832 | tf_op jit(solution)/shard_map/ppermute | solution.py:601
  66.2 1.3 %collective-permute-done.4.arrived_ref = bf16[4,6,32,128]{3,2,1,0:T(8,128)(2,1)S(1)} collective-permute-done((bf16[4,6,32,128]{3,2,1,0:T(8,128)(2,1)S(1)}, bf16[4,6,32,128]{3,2,1,0:T(8,128)(2,1)S(1)}, u32[]{:S(2)}, u32[]{:S(2)}) %collective-permute-start.4) | collective-permute-done | bytes 196640 | tf_op jit(solution)/shard_map/ppermute | solution.py:601
  67.5 1.5 %fields_second.1.fields_ref = f32[2,2,4,6,32,128]{5,4,3,2,1,0:T(8,128)S(1)} custom-call(bf16[4,6,32,128]{3,2,1,0:T(8,128)(2,1)S(1)} %get-tuple-element.40.incoming_ref, bf16[4,6,32,128]{3,2,1,0:T(8,128)(2,1)S(1)} %collective-permute-done.4.arrived_ref, bf16[4,26,32,128]{3,2,1,0:T(8,128)(2,1)} %get-tuple-element.37.bundle_hbm, ...), custom_call_target="tpu_custom_call" | custom-call | flops 1000000 | bytes 2150400 | tf_op jit(solution)/shard_map/fields_second/pallas_call | solution.py:494
  68.9 5.2 %all-to-all-done.2.table_ref = f32[64,4,128]{2,1,0:T(4,128)S(1)} async-done(((f32[64,4,128]{2,1,0:T(4,128)}), f32[64,4,128]{2,1,0:T(4,128)S(1)}, u32[]{:S(2)}, u32[]{:S(2)}) %all-to-all-start.2) | async-done | bytes 131104 | tf_op jit(solution)/shard_map/all_to_all | solution.py:539
  74.2 2.3 %weight_second.1 = (bf16[32,56,128]{2,1,0:T(8,128)(2,1)}, bf16[4,192,384]{2,1,0:T(8,128)(2,1)}, f32[2,128]{1,0:T(2,128)S(1)}) custom-call(f32[64,4,128]{2,1,0:T(4,128)S(1)} %all-to-all-done.2.table_ref, f32[2,2,4,6,32,128]{5,4,3,2,1,0:T(8,128)S(1)} %fields_second.1.fields_ref, f32[80,128]{1,0:T(8,128)S(1)} %get-tuple-element.31.params_ref, ...), custom_call_target="tpu_custom_call" | custom-call | flops 1000000 | bytes 3231744 | tf_op jit(solution)/shard_map/weight_second/pallas_call | solution.py:494
  76.5 4.8 %all-to-all-start.3 = ((bf16[32,56,128]{2,1,0:T(8,128)(2,1)}), bf16[32,56,128]{2,1,0:T(8,128)(2,1)S(1)}, u32[]{:S(2)}, u32[]{:S(2)}) async-start(bf16[32,56,128]{2,1,0:T(8,128)(2,1)} %get-tuple-element.44), calls=%async_computation.3 | async-start | bytes 917504 | tf_op jit(solution)/shard_map/all_to_all | solution.py:618
  81.3 3.0 %conv_second.1 = bf16[2,4,4,32,128]{4,3,2,1,0:T(8,128)(2,1)} custom-call(f32[80,128]{1,0:T(8,128)S(1)} %get-tuple-element.31.params_ref, bf16[4,192,384]{2,1,0:T(8,128)(2,1)} %get-tuple-element.43.columns_hbm, bf16[4,6,32,128]{3,2,1,0:T(8,128)(2,1)} %copy-done, bf16[3,9,128,128]{3,2,1,0:T(8,128)(2,1)} %bitcast.16), custom_call_target="tpu_custom_call" | custom-call | flops 1000000 | bytes 1712128 | tf_op jit(solution)/shard_map/conv_second/pallas_call | solution.py:494
  84.4 0.1 constant_dynamic-slice_fusion
  84.5 0.5 fusion
  85.0 12.9 %all-to-all-done.3.terms_ref = bf16[32,56,128]{2,1,0:T(8,128)(2,1)S(1)} async-done(((bf16[32,56,128]{2,1,0:T(8,128)(2,1)}), bf16[32,56,128]{2,1,0:T(8,128)(2,1)S(1)}, u32[]{:S(2)}, u32[]{:S(2)}) %all-to-all-start.3) | async-done | bytes 458784 | tf_op jit(solution)/shard_map/all_to_all | solution.py:618
  97.9 0.7 total.1
Async XLA Ops:
  2.7 27.4 %all-to-all-start = ((f32[64,4,128]{2,1,0:T(4,128)}), f32[64,4,128]{2,1,0:T(4,128)S(1)}, u32[]{:S(2)}, u32[]{:S(2)}) async-start(f32[64,4,128]{2,1,0:T(4,128)} %get-tuple-element.28), calls=%async_computation | async-start | bytes 262144 | tf_op jit(solution)/shard_map/all_to_all | solution.py:539
  19.8 16.6 %collective-permute-start = (bf16[4,6,32,128]{3,2,1,0:T(8,128)(2,1)S(1)}, bf16[4,6,32,128]{3,2,1,0:T(8,128)(2,1)S(1)}, u32[]{:S(2)}, u32[]{:S(2)}) collective-permute-start(bf16[4,6,32,128]{3,2,1,0:T(8,128)(2,1)S(1)} %get-tuple-element.25), channel_id=1, source_target_pairs={{0,1},{1,0},{2,3},{3,2},{4,5},{5,4},{6,7},{7,6},{8,9},{9,8},{10,11... | collective-permute-start | bytes 589832 | tf_op jit(solution)/shard_map/ppermute | solution.py:553
  21.9 14.6 %collective-permute-start.1 = (bf16[4,6,32,128]{3,2,1,0:T(8,128)(2,1)S(1)}, bf16[4,6,32,128]{3,2,1,0:T(8,128)(2,1)S(1)}, u32[]{:S(2)}, u32[]{:S(2)}) collective-permute-start(bf16[4,6,32,128]{3,2,1,0:T(8,128)(2,1)S(1)} %get-tuple-element.26), channel_id=1, source_target_pairs={{1,2},{3,4},{5,6},{7,8},{9,10},{11,12},{13,14},{15,16},{17,18},{19... | collective-permute-start | bytes 589832 | tf_op jit(solution)/shard_map/ppermute | solution.py:555
  31.3 14.1 %all-to-all-start.1 = ((f32[64,2,128]{2,1,0:T(2,128)}), f32[64,2,128]{2,1,0:T(2,128)S(1)}, u32[]{:S(2)}, u32[]{:S(2)}) async-start(f32[64,2,128]{2,1,0:T(2,128)} %get-tuple-element.32), calls=%async_computation.1 | async-start | bytes 131072 | tf_op jit(solution)/shard_map/all_to_all | solution.py:539
  39.2 9.9 %collective-permute-start.3 = (bf16[4,26,32,128]{3,2,1,0:T(8,128)(2,1)}, bf16[4,26,32,128]{3,2,1,0:T(8,128)(2,1)S(1)}, u32[]{:S(2)}, u32[]{:S(2)}) collective-permute-start(bf16[4,26,32,128]{3,2,1,0:T(8,128)(2,1)} %get-tuple-element.37.bundle_hbm), channel_id=1, source_target_pairs={{0,1},{1,0},{2,3},{3,2},{4,5},{5,4},{6,7},{7,6},{8,9},{9,8},{10,11... | collective-permute-start | bytes 2555912 | tf_op jit(solution)/shard_map/ppermute | solution.py:571
  47.8 9.8 %copy-start = (bf16[4,6,32,128]{3,2,1,0:T(8,128)(2,1)}, bf16[4,6,32,128]{3,2,1,0:T(8,128)(2,1)S(1)}, u32[]{:S(2)}) copy-start(bf16[4,6,32,128]{3,2,1,0:T(8,128)(2,1)S(1)} %get-tuple-element.34.first_hbm) | copy-start | bytes 589828
  47.8 8.8 %collective-permute-start.2 = (bf16[4,6,32,128]{3,2,1,0:T(8,128)(2,1)S(1)}, bf16[4,6,32,128]{3,2,1,0:T(8,128)(2,1)S(1)}, u32[]{:S(2)}, u32[]{:S(2)}) collective-permute-start(bf16[4,6,32,128]{3,2,1,0:T(8,128)(2,1)S(1)} %get-tuple-element.34.first_hbm), channel_id=1, source_target_pairs={{64,0},{128,64},{192,128},{256,192},{320,256},{384,320},{448,384},... | collective-permute-start | bytes 589832 | tf_op jit(solution)/shard_map/ppermute | solution.py:584
  49.1 1.0 copy-start.1
  57.6 16.6 %all-to-all-start.2 = ((f32[64,4,128]{2,1,0:T(4,128)}), f32[64,4,128]{2,1,0:T(4,128)S(1)}, u32[]{:S(2)}, u32[]{:S(2)}) async-start(f32[64,4,128]{2,1,0:T(4,128)} %get-tuple-element.39), calls=%async_computation.2 | async-start | bytes 262144 | tf_op jit(solution)/shard_map/all_to_all | solution.py:539
  64.1 3.3 %collective-permute-start.4 = (bf16[4,6,32,128]{3,2,1,0:T(8,128)(2,1)S(1)}, bf16[4,6,32,128]{3,2,1,0:T(8,128)(2,1)S(1)}, u32[]{:S(2)}, u32[]{:S(2)}) collective-permute-start(bf16[4,6,32,128]{3,2,1,0:T(8,128)(2,1)S(1)} %get-tuple-element.40.incoming_ref), channel_id=1, source_target_pairs={{0,1},{1,0},{2,3},{3,2},{4,5},{5,4},{6,7},{7,6},{8,9},{9,8},{10,11... | collective-permute-start | bytes 589832 | tf_op jit(solution)/shard_map/ppermute | solution.py:601
  76.5 21.4 %all-to-all-start.3 = ((bf16[32,56,128]{2,1,0:T(8,128)(2,1)}), bf16[32,56,128]{2,1,0:T(8,128)(2,1)S(1)}, u32[]{:S(2)}, u32[]{:S(2)}) async-start(bf16[32,56,128]{2,1,0:T(8,128)(2,1)} %get-tuple-element.44), calls=%async_computation.3 | async-start | bytes 917504 | tf_op jit(solution)/shard_map/all_to_all | solution.py:618

commit v7 on v6

--- a/solution.py
+++ b/solution.py
@@ -226,9 +226,8 @@
     bundle_out.start()
     gain, shift = row(params_ref, GAIN), row(params_ref, SHIFT)
     last = row(params_ref, LAST).reshape(1, 1, 1, CH)
-    loss_out_ref[:, 0:1] = (up_ref[:, 5:6].astype(F32) * last).astype(BF16)
-    loss_out_ref[:, 1 : 1 + ROWS] = (held_loss[...].astype(F32) * last).astype(BF16)
-    loss_out_ref[:, 1 + ROWS : 2 + ROWS] = (down_ref[:, 5:6].astype(F32) * last).astype(BF16)
+    loss_out_ref[:, 0:ROWS] = (held_loss[...].astype(F32) * last).astype(BF16)
+    loss_out_ref[:, ROWS : ROWS + 1] = (outer_ref[:, 5:6].astype(F32) * last).astype(BF16)
     for f in range(FRAMES):
         mean, rstd = row(stats_ref, MEAN0 + f), row(stats_ref, RSTD0 + f)
         for at, count, pre, cot, mask in (
@@ -273,13 +272,15 @@
     size = rows * COLS
     for kt in range(3):
         count = FRAMES - kt
-        blocks = [
-            columns_ref[kt:FRAMES, start : start + size, :].reshape(count * size, 3 * CH)
-            for start in (2 * COLS, COLS, 0)
-        ]
-        part = lax.dot_general(
-            jnp.concatenate(blocks, axis=1), weight_ref[kt], (((1,), (1,)), ((), ())), preferred_element_type=F32
-        )
+        part = None
+        for dy in range(3):
+            start = (2 - dy) * COLS
+            term = lax.dot_general(
+                columns_ref[kt:FRAMES, start : start + size, :].reshape(count * size, 3 * CH),
+                weight_ref[kt, :, 3 * dy * CH : 3 * (dy + 1) * CH], (((1,), (1,)), ((), ())),
+                preferred_element_type=F32,
+            )
+            part = term if part is None else part + term
         for f in range(count):
             mine = part[f * size : (f + 1) * size]
             if kt:
@@ -315,7 +316,11 @@
         for n in range(9):
             weight_ref[kt, :, n * CH : (n + 1) * CH] = taps_ref[kt, n]
     conv(columns_ref, weight_ref, params_ref, 0, ROWS + 2, sum_ref)
-    grad_ref[...] = sum_ref[...].astype(BF16).reshape(grad_ref.shape)
+    second = row(params_ref, CORE) > 0.5
+    for f in range(FRAMES):
+        grad_ref[f, 0:ROWS] = sum_ref[f, COLS : COLS * (ROWS + 1)].astype(BF16).reshape(ROWS, COLS, CH)
+        outer = jnp.where(second, sum_ref[f, COLS * (ROWS + 1) : COLS * (ROWS + 2)], sum_ref[f, 0:COLS])
+        grad_ref[f, ROWS : ROWS + 1] = outer.astype(BF16).reshape(1, COLS, CH)
     value_out.wait()
 
 
@@ -349,7 +354,7 @@
     for f in range(FRAMES):
         incoming = hand_ref[f].astype(F32) + loss_ref[f].astype(F32)
         incoming_ref[f] = incoming.astype(BF16)
-        grad_act = flat(incoming[1 : 1 + ROWS]) * flat(slope_ref[0, f])
+        grad_act = flat(incoming[0:ROWS]) * flat(slope_ref[0, f])
         live = row(params_ref, TURN + LIVE + f)
         plain = colsum(grad_act) * live
         times = colsum(grad_act * flat(slope_ref[1, f])) * live
@@ -415,16 +420,27 @@
     for copy in copies:
         copy.wait()
     gain, shift = row(params_ref, GAIN), row(params_ref, SHIFT)
+    second = (row(params_ref, CORE) > 0.5).reshape(1, 1, CH)
     for f in range(FRAMES):
         mean, rstd = row(stats_ref, MEAN1 + f), row(stats_ref, RSTD1 + f)
-        for strip, pre_ref, come_ref, top, bottom in (
-            (0, bundle_ref, incoming_ref, TURN + TOP, TURN + BOTTOM),
-            (1, other_ref, arrived_ref, OTHER_TURN + OTHER_TOP, OTHER_TURN + OTHER_BOTTOM),
+        mine, others = incoming_ref[f].astype(F32), arrived_ref[f].astype(F32)
+        far, near = slice(ROWS, ROWS + 1), slice(0, 1)
+        end = slice(ROWS - 1, ROWS)
+        for strip, pre_ref, top, own, bottom, top_mask, bottom_mask in (
+            (
+                0, bundle_ref, jnp.where(second, others[end], mine[far]), mine[0:ROWS],
+                jnp.where(second, mine[far], others[near]), TURN + TOP, TURN + BOTTOM,
+            ),
+            (
+                1, other_ref, jnp.where(second, others[far], mine[end]), others[0:ROWS],
+                jnp.where(second, mine[near], others[far]), OTHER_TURN + OTHER_TOP, OTHER_TURN + OTHER_BOTTOM,
+            ),
         ):
-            for at, count, mask in ((0, 1, top), (1, ROWS, TURN + LIVE), (1 + ROWS, 1, bottom)):
+            for at, count, come, mask in (
+                (0, 1, top, top_mask), (1, ROWS, own, TURN + LIVE), (1 + ROWS, 1, bottom, bottom_mask)
+            ):
                 pair = fields(
-                    pre_ref[f, at : at + count], come_ref[f, at : at + count], mean, rstd, gain, shift,
-                    row(params_ref, mask + f),
+                    pre_ref[f, at : at + count], come, mean, rstd, gain, shift, row(params_ref, mask + f)
                 )
                 for n in range(2):
                     out_ref[strip, n, f, at : at + count] = pair[n].reshape(count, COLS, CH)
@@ -476,8 +492,8 @@
     for copy in copy_in(pairs, sems):
         copy.wait()
     conv(columns_ref, weight_ref, params_ref, 1, ROWS, sum_ref)
-    out_ref[0] = first_ref[:, 1 : 1 + ROWS]
-    out_ref[1] = sum_ref[...].astype(BF16).reshape(first_ref[:, 1 : 1 + ROWS].shape)
+    out_ref[0] = first_ref[:, 0:ROWS]
+    out_ref[1] = sum_ref[...].astype(BF16).reshape(first_ref[:, 0:ROWS].shape)
 
 
 def total_kernel(scale, terms_ref, out_ref):
@@ -529,6 +545,7 @@
     cot, loss = cot_first[0], loss_grad[0]
     taps = weight[0].reshape(3, 9, CH, CH)
     edge = (FRAMES, ROWS + 2, COLS, CH)
+    handed = (FRAMES, ROWS + 1, COLS, CH)
     strip = (FRAMES, ROWS, COLS, CH)
     bundled = (FRAMES, 3 * (ROWS + 2) + 2 * ROWS, COLS, CH)
     mates = [(i, i ^ 1) for i in range(dp)]
@@ -563,7 +580,7 @@
         fields_first_kernel, "fields_first", (flags, inner, outer, plain, stats, pre, cot, loss, act),
         (
             kept((2, FRAMES, ROWS + 4, COLS, CH)), in_hbm(bundled, BF16),
-            kept(edge, BF16), kept((PARAM_ROWS, CH)),
+            kept(handed, BF16), kept((PARAM_ROWS, CH)),
         ),
         scratch=[pltpu.VMEM(bundled, BF16), pltpu.VMEM(strip, BF16)] + [pltpu.VMEM(edge, BF16)] * 2 + [sems(7)],
         specs="svvkkhhhh",
@@ -573,7 +590,7 @@
     weights = pltpu.VMEM((3, CH, 9 * CH), BF16)
     grad_first, value = call(
         conv_first_kernel, "conv_first", (table, first_fields, params, stats, taps),
-        (shape(edge, BF16), in_hbm(edge, BF16)),
+        (shape(handed, BF16), in_hbm(edge, BF16)),
         scratch=[
             pltpu.VMEM(columns_of(ROWS + 4), BF16), pltpu.VMEM((3, 9, CH, CH), BF16), weights, pltpu.VMEM(edge, BF16),
             pltpu.VMEM((FRAMES, (ROWS + 2) * COLS, CH), F32), sems(2),
@@ -595,7 +612,7 @@
 
     table, incoming = call(
         act_second_kernel, "act_second", (hand, loss_rows, slope, params, stats),
-        (shape((dp, 4, CH)), shape(edge, BF16)), specs="vkkkk",
+        (shape((dp, 4, CH)), shape(handed, BF16)), specs="vkkkk",
     )
     table = exchange(table)
     arrived = lax.ppermute(incoming, "dp", mates)
@@ -623,7 +640,7 @@
         conv_second_kernel, "conv_second", (params, columns, grad_first, taps),
         (shape((2, FRAMES, ROWS, COLS, CH), BF16),),
         scratch=[
-            weights, pltpu.VMEM(columns_of(ROWS + 2), BF16), pltpu.VMEM(edge, BF16),
+            weights, pltpu.VMEM(columns_of(ROWS + 2), BF16), pltpu.VMEM(handed, BF16),
             pltpu.VMEM((FRAMES, ROWS * COLS, CH), F32), sems(11),
         ],
         specs="khhh",

time: 99.2 us -> 98.5 us (level)
  no operation moved by 1% of the time
where the time goes in v7:
time: 98.5 us; the launch traced here: 97.9 us
  starting transfers between devices  43.5 us (44%)
  waiting for transfers between devices  31.9 us (32%)
  Pallas kernels  20 us (20%)
  local copies, waits for them, and re-layouts  1.66 us (2%)
    all_to_all x3, starting transfers between devices, exchange(): return lax.all_to_all(table, 'dp', 0, 0, tiled=True)  28.8 us
    pallas_call x10, Pallas kernels, call(): pl.pallas_call(kernel, out_shape=tuple(outs), in_specs=[{'v': VMEM, 'k':...  20 us
    all_to_all x3, waiting for transfers between devices, exchange(): return lax.all_to_all(table, 'dp', 0, 0, tiled=True)  15 us
    all_to_all x1, waiting for transfers between devices, local(): lax.all_to_all(terms, 'dp', 0, 0, axis_index_groups=sides, tiled=True)  12.9 us
    all_to_all x1, starting transfers between devices, local(): lax.all_to_all(terms, 'dp', 0, 0, axis_index_groups=sides, tiled=True)  4.81 us
    ppermute x1, waiting for transfers between devices, local(): lax.ppermute(grad_first, 'segment', [(i + 1, i) for i in range(count - 1)])  2.7 us
    ppermute x1, starting transfers between devices, local(): outer = lax.ppermute(outer, 'dp', sides + [(j, i) for i, j in sides])  2.43 us
    ppermute x1, starting transfers between devices, local(): inner = lax.ppermute(inner, 'dp', mates)  2.06 us
  transfers between devices with their start and end apart: 9, of which 6 were waited for; matrix products, arithmetic and copies ran while one was open for 1% of the time, Pallas kernels for 14%

profile of v7, /device:TPU:8, one launch (start us, length us, event | category | flops | bytes accessed | tf_op | source)
XLA Modules:
  0.0 97.9 jit_solution(7562657129231017737)
XLA Ops:
  0.6 2.0 %sums.1 = (f32[64,4,128]{2,1,0:T(4,128)}, bf16[4,6,32,128]{3,2,1,0:T(8,128)(2,1)S(1)}, bf16[4,6,32,128]{3,2,1,0:T(8,128)(2,1)S(1)}, f32[2,4,4,32,128]{4,3,2,1,0:T(8,128)S(1)}, f32[80,128]{1,0:T(8,128)S(1)}) custom-call(s32[1]{0:T(128)} %bitcast.4.odd_ref, s32[1,2,1,4]{3,2,1,0:T(1,128)} %clip_hbm.1, bf16[2,4,4,32,128]{4,3,2,1,0:T(8,128)(2,1)} %bitcast.13, ...), custom_call_target="tpu_custom_call" | custom-call | flops 1000000 | bytes 525348 | tf_op jit(solution)/shard_map/sums/pallas_call | solution.py:510
  2.7 17.2 %all-to-all-start = ((f32[64,4,128]{2,1,0:T(4,128)}), f32[64,4,128]{2,1,0:T(4,128)S(1)}, u32[]{:S(2)}, u32[]{:S(2)}) async-start(f32[64,4,128]{2,1,0:T(4,128)} %get-tuple-element.28), calls=%async_computation | async-start | bytes 262144 | tf_op jit(solution)/shard_map/all_to_all | solution.py:556
  19.8 2.1 %collective-permute-start = (bf16[4,6,32,128]{3,2,1,0:T(8,128)(2,1)S(1)}, bf16[4,6,32,128]{3,2,1,0:T(8,128)(2,1)S(1)}, u32[]{:S(2)}, u32[]{:S(2)}) collective-permute-start(bf16[4,6,32,128]{3,2,1,0:T(8,128)(2,1)S(1)} %get-tuple-element.25), channel_id=1, source_target_pairs={{0,1},{1,0},{2,3},{3,2},{4,5},{5,4},{6,7},{7,6},{8,9},{9,8},{10,11... | collective-permute-start | bytes 589832 | tf_op jit(solution)/shard_map/ppermute | solution.py:570
  21.9 2.4 %collective-permute-start.1 = (bf16[4,6,32,128]{3,2,1,0:T(8,128)(2,1)S(1)}, bf16[4,6,32,128]{3,2,1,0:T(8,128)(2,1)S(1)}, u32[]{:S(2)}, u32[]{:S(2)}) collective-permute-start(bf16[4,6,32,128]{3,2,1,0:T(8,128)(2,1)S(1)} %get-tuple-element.26), channel_id=1, source_target_pairs={{1,2},{3,4},{5,6},{7,8},{9,10},{11,12},{13,14},{15,16},{17,18},{19... | collective-permute-start | bytes 589832 | tf_op jit(solution)/shard_map/ppermute | solution.py:572
  24.4 5.7 %all-to-all-done.table_ref = f32[64,4,128]{2,1,0:T(4,128)S(1)} async-done(((f32[64,4,128]{2,1,0:T(4,128)}), f32[64,4,128]{2,1,0:T(4,128)S(1)}, u32[]{:S(2)}, u32[]{:S(2)}) %all-to-all-start) | async-done | bytes 131104 | tf_op jit(solution)/shard_map/all_to_all | solution.py:556
  30.1 1.2 %act_first.1 = (f32[64,2,128]{2,1,0:T(2,128)}, f32[24,128]{1,0:T(8,128)S(1)}) custom-call(f32[64,4,128]{2,1,0:T(4,128)S(1)} %all-to-all-done.table_ref, f32[2,4,4,32,128]{4,3,2,1,0:T(8,128)S(1)} %get-tuple-element.29.own_ref, f32[80,128]{1,0:T(8,128)S(1)} %get-tuple-element.27.params_ref.plain_ref), custom_call_target="tpu_custom_call" | custom-call | flops 1000000 | bytes 696320 | tf_op jit(solution)/shard_map/act_first/pallas_call | solution.py:510
  31.3 5.1 %all-to-all-start.1 = ((f32[64,2,128]{2,1,0:T(2,128)}), f32[64,2,128]{2,1,0:T(2,128)S(1)}, u32[]{:S(2)}, u32[]{:S(2)}) async-start(f32[64,2,128]{2,1,0:T(2,128)} %get-tuple-element.32), calls=%async_computation.1 | async-start | bytes 131072 | tf_op jit(solution)/shard_map/all_to_all | solution.py:556
  36.4 0.1 stack.47.flag_ref
  36.5 0.0 collective-permute-done.inner_ref
  36.5 0.0 collective-permute-done.1.outer_ref
  36.5 2.7 %fields_first.1 = (f32[2,4,8,32,128]{4,3,2,1,0:T(8,128)S(1)}, bf16[4,26,32,128]{3,2,1,0:T(8,128)(2,1)}, bf16[4,5,32,128]{3,2,1,0:T(8,128)(2,1)S(1)}, f32[80,128]{1,0:T(8,128)S(1)}) custom-call(s32[6]{0:T(128)S(1)} %stack.47.flag_ref, bf16[4,6,32,128]{3,2,1,0:T(8,128)(2,1)S(1)} %collective-permute-done.inner_ref, ...), custom_call_target="tpu_custom_call" | custom-call | flops 1000000 | bytes 1232920 | tf_op jit(solution)/shard_map/fields_first/pallas_call | solution.py:510
  39.2 2.1 %collective-permute-start.3 = (bf16[4,26,32,128]{3,2,1,0:T(8,128)(2,1)}, bf16[4,26,32,128]{3,2,1,0:T(8,128)(2,1)S(1)}, u32[]{:S(2)}, u32[]{:S(2)}) collective-permute-start(bf16[4,26,32,128]{3,2,1,0:T(8,128)(2,1)} %get-tuple-element.37.bundle_hbm), channel_id=1, source_target_pairs={{0,1},{1,0},{2,3},{3,2},{4,5},{5,4},{6,7},{7,6},{8,9},{9,8},{10,11... | collective-permute-start | bytes 2555912 | tf_op jit(solution)/shard_map/ppermute | solution.py:588
  41.3 4.0 %all-to-all-done.1.table_ref = f32[64,2,128]{2,1,0:T(2,128)S(1)} async-done(((f32[64,2,128]{2,1,0:T(2,128)}), f32[64,2,128]{2,1,0:T(2,128)S(1)}, u32[]{:S(2)}, u32[]{:S(2)}) %all-to-all-start.1) | async-done | bytes 65568 | tf_op jit(solution)/shard_map/all_to_all | solution.py:556
  45.3 2.5 %conv_first.1 = (bf16[4,5,32,128]{3,2,1,0:T(8,128)(2,1)S(1)}, bf16[4,6,32,128]{3,2,1,0:T(8,128)(2,1)}) custom-call(f32[64,2,128]{2,1,0:T(2,128)S(1)} %all-to-all-done.1.table_ref, f32[2,4,8,32,128]{4,3,2,1,0:T(8,128)S(1)} %get-tuple-element.33.fields_ref, f32[80,128]{1,0:T(8,128)S(1)} %get-tuple-element.31.params_ref, ...), custom_call_target="tpu_custom_call" | custom-call | flops 20000000000 | bytes 2052096 | tf_op jit(solution)/shard_map/conv_first/pallas_call | solution.py:510
  47.8 0.0 copy-start
  47.8 1.3 %collective-permute-start.2 = (bf16[4,5,32,128]{3,2,1,0:T(8,128)(2,1)S(1)}, bf16[4,5,32,128]{3,2,1,0:T(8,128)(2,1)S(1)}, u32[]{:S(2)}, u32[]{:S(2)}) collective-permute-start(bf16[4,5,32,128]{3,2,1,0:T(8,128)(2,1)S(1)} %get-tuple-element.34.first_hbm), channel_id=1, source_target_pairs={{64,0},{128,64},{192,128},{256,192},{320,256},{384,320},{448,384},... | collective-permute-start | bytes 491528 | tf_op jit(solution)/shard_map/ppermute | solution.py:601
  49.1 0.0 collective-permute-done.3.other_hbm
  49.2 0.0 copy-start.1
  49.2 1.0 copy-done.1
  50.1 3.1 %weight_first.1 = (f32[2,4,4,32,128]{4,3,2,1,0:T(8,128)S(1)}, bf16[128,2304]{1,0:T(8,128)(2,1)S(1)}, bf16[27,128,128]{2,1,0:T(8,128)(2,1)S(1)}) custom-call(f32[64,2,128]{2,1,0:T(2,128)S(1)} %all-to-all-done.1.table_ref, f32[80,128]{1,0:T(8,128)S(1)} %get-tuple-element.31.params_ref, f32[24,128]{1,0:T(8,128)S(1)} %get-tuple-element.30.stats_ref, ...), custom_call_target="tpu_custom_call" | custom-call | flops 1000000 | bytes 2019328 | tf_op jit(solution)/shard_map/weight_first/pallas_call | solution.py:510
  53.3 2.7 %collective-permute-done.2.hand_ref = bf16[4,5,32,128]{3,2,1,0:T(8,128)(2,1)S(1)} collective-permute-done((bf16[4,5,32,128]{3,2,1,0:T(8,128)(2,1)S(1)}, bf16[4,5,32,128]{3,2,1,0:T(8,128)(2,1)S(1)}, u32[]{:S(2)}, u32[]{:S(2)}) %collective-permute-start.2) | collective-permute-done | bytes 163872 | tf_op jit(solution)/shard_map/ppermute | solution.py:601
  56.0 0.9 act_second.1
  56.9 0.0 copy-done
  56.9 6.5 %all-to-all-start.2 = ((f32[64,4,128]{2,1,0:T(4,128)}), f32[64,4,128]{2,1,0:T(4,128)S(1)}, u32[]{:S(2)}, u32[]{:S(2)}) async-start(f32[64,4,128]{2,1,0:T(4,128)} %get-tuple-element.39), calls=%async_computation.2 | async-start | bytes 262144 | tf_op jit(solution)/shard_map/all_to_all | solution.py:556
  63.4 2.1 %collective-permute-start.4 = (bf16[4,5,32,128]{3,2,1,0:T(8,128)(2,1)S(1)}, bf16[4,5,32,128]{3,2,1,0:T(8,128)(2,1)S(1)}, u32[]{:S(2)}, u32[]{:S(2)}) collective-permute-start(bf16[4,5,32,128]{3,2,1,0:T(8,128)(2,1)S(1)} %get-tuple-element.40.incoming_ref), channel_id=1, source_target_pairs={{0,1},{1,0},{2,3},{3,2},{4,5},{5,4},{6,7},{7,6},{8,9},{9,8},{10,11... | collective-permute-start | bytes 491528 | tf_op jit(solution)/shard_map/ppermute | solution.py:618
  65.5 1.2 %collective-permute-done.4.arrived_ref = bf16[4,5,32,128]{3,2,1,0:T(8,128)(2,1)S(1)} collective-permute-done((bf16[4,5,32,128]{3,2,1,0:T(8,128)(2,1)S(1)}, bf16[4,5,32,128]{3,2,1,0:T(8,128)(2,1)S(1)}, u32[]{:S(2)}, u32[]{:S(2)}) %collective-permute-start.4) | collective-permute-done | bytes 163872 | tf_op jit(solution)/shard_map/ppermute | solution.py:618
  66.7 1.5 %fields_second.1.fields_ref = f32[2,2,4,6,32,128]{5,4,3,2,1,0:T(8,128)S(1)} custom-call(bf16[4,5,32,128]{3,2,1,0:T(8,128)(2,1)S(1)} %get-tuple-element.40.incoming_ref, bf16[4,5,32,128]{3,2,1,0:T(8,128)(2,1)S(1)} %collective-permute-done.4.arrived_ref, bf16[4,26,32,128]{3,2,1,0:T(8,128)(2,1)} %get-tuple-element.37.bundle_hbm, ...), custom_call_target="tpu_custom_call" | custom-call | flops 1000000 | bytes 2084864 | tf_op jit(solution)/shard_map/fields_second/pallas_call | solution.py:510
  68.2 5.3 %all-to-all-done.2.table_ref = f32[64,4,128]{2,1,0:T(4,128)S(1)} async-done(((f32[64,4,128]{2,1,0:T(4,128)}), f32[64,4,128]{2,1,0:T(4,128)S(1)}, u32[]{:S(2)}, u32[]{:S(2)}) %all-to-all-start.2) | async-done | bytes 131104 | tf_op jit(solution)/shard_map/all_to_all | solution.py:556
  73.5 2.3 %weight_second.1 = (bf16[32,56,128]{2,1,0:T(8,128)(2,1)}, bf16[4,192,384]{2,1,0:T(8,128)(2,1)}, f32[2,128]{1,0:T(2,128)S(1)}) custom-call(f32[64,4,128]{2,1,0:T(4,128)S(1)} %all-to-all-done.2.table_ref, f32[2,2,4,6,32,128]{5,4,3,2,1,0:T(8,128)S(1)} %fields_second.1.fields_ref, f32[80,128]{1,0:T(8,128)S(1)} %get-tuple-element.31.params_ref, ...), custom_call_target="tpu_custom_call" | custom-call | flops 1000000 | bytes 3231744 | tf_op jit(solution)/shard_map/weight_second/pallas_call | solution.py:510
  75.8 4.8 %all-to-all-start.3 = ((bf16[32,56,128]{2,1,0:T(8,128)(2,1)}), bf16[32,56,128]{2,1,0:T(8,128)(2,1)S(1)}, u32[]{:S(2)}, u32[]{:S(2)}) async-start(bf16[32,56,128]{2,1,0:T(8,128)(2,1)} %get-tuple-element.44), calls=%async_computation.3 | async-start | bytes 917504 | tf_op jit(solution)/shard_map/all_to_all | solution.py:635
  80.6 3.0 %conv_second.1 = bf16[2,4,4,32,128]{4,3,2,1,0:T(8,128)(2,1)} custom-call(f32[80,128]{1,0:T(8,128)S(1)} %get-tuple-element.31.params_ref, bf16[4,192,384]{2,1,0:T(8,128)(2,1)} %get-tuple-element.43.columns_hbm, bf16[4,5,32,128]{3,2,1,0:T(8,128)(2,1)} %copy-done, bf16[3,9,128,128]{3,2,1,0:T(8,128)(2,1)} %bitcast.16), custom_call_target="tpu_custom_call" | custom-call | flops 1000000 | bytes 1679360 | tf_op jit(solution)/shard_map/conv_second/pallas_call | solution.py:510
  83.7 0.1 constant_dynamic-slice_fusion
  83.8 0.5 fusion
  84.3 12.9 %all-to-all-done.3.terms_ref = bf16[32,56,128]{2,1,0:T(8,128)(2,1)S(1)} async-done(((bf16[32,56,128]{2,1,0:T(8,128)(2,1)}), bf16[32,56,128]{2,1,0:T(8,128)(2,1)S(1)}, u32[]{:S(2)}, u32[]{:S(2)}) %all-to-all-start.3) | async-done | bytes 458784 | tf_op jit(solution)/shard_map/all_to_all | solution.py:635
  97.2 0.7 total.1
Async XLA Ops:
  2.7 27.4 %all-to-all-start = ((f32[64,4,128]{2,1,0:T(4,128)}), f32[64,4,128]{2,1,0:T(4,128)S(1)}, u32[]{:S(2)}, u32[]{:S(2)}) async-start(f32[64,4,128]{2,1,0:T(4,128)} %get-tuple-element.28), calls=%async_computation | async-start | bytes 262144 | tf_op jit(solution)/shard_map/all_to_all | solution.py:556
  19.8 16.6 %collective-permute-start = (bf16[4,6,32,128]{3,2,1,0:T(8,128)(2,1)S(1)}, bf16[4,6,32,128]{3,2,1,0:T(8,128)(2,1)S(1)}, u32[]{:S(2)}, u32[]{:S(2)}) collective-permute-start(bf16[4,6,32,128]{3,2,1,0:T(8,128)(2,1)S(1)} %get-tuple-element.25), channel_id=1, source_target_pairs={{0,1},{1,0},{2,3},{3,2},{4,5},{5,4},{6,7},{7,6},{8,9},{9,8},{10,11... | collective-permute-start | bytes 589832 | tf_op jit(solution)/shard_map/ppermute | solution.py:570
  21.9 14.6 %collective-permute-start.1 = (bf16[4,6,32,128]{3,2,1,0:T(8,128)(2,1)S(1)}, bf16[4,6,32,128]{3,2,1,0:T(8,128)(2,1)S(1)}, u32[]{:S(2)}, u32[]{:S(2)}) collective-permute-start(bf16[4,6,32,128]{3,2,1,0:T(8,128)(2,1)S(1)} %get-tuple-element.26), channel_id=1, source_target_pairs={{1,2},{3,4},{5,6},{7,8},{9,10},{11,12},{13,14},{15,16},{17,18},{19... | collective-permute-start | bytes 589832 | tf_op jit(solution)/shard_map/ppermute | solution.py:572
  31.3 14.1 %all-to-all-start.1 = ((f32[64,2,128]{2,1,0:T(2,128)}), f32[64,2,128]{2,1,0:T(2,128)S(1)}, u32[]{:S(2)}, u32[]{:S(2)}) async-start(f32[64,2,128]{2,1,0:T(2,128)} %get-tuple-element.32), calls=%async_computation.1 | async-start | bytes 131072 | tf_op jit(solution)/shard_map/all_to_all | solution.py:556
  39.2 9.9 %collective-permute-start.3 = (bf16[4,26,32,128]{3,2,1,0:T(8,128)(2,1)}, bf16[4,26,32,128]{3,2,1,0:T(8,128)(2,1)S(1)}, u32[]{:S(2)}, u32[]{:S(2)}) collective-permute-start(bf16[4,26,32,128]{3,2,1,0:T(8,128)(2,1)} %get-tuple-element.37.bundle_hbm), channel_id=1, source_target_pairs={{0,1},{1,0},{2,3},{3,2},{4,5},{5,4},{6,7},{7,6},{8,9},{9,8},{10,11... | collective-permute-start | bytes 2555912 | tf_op jit(solution)/shard_map/ppermute | solution.py:588
  47.8 9.1 %copy-start = (bf16[4,5,32,128]{3,2,1,0:T(8,128)(2,1)}, bf16[4,5,32,128]{3,2,1,0:T(8,128)(2,1)S(1)}, u32[]{:S(2)}) copy-start(bf16[4,5,32,128]{3,2,1,0:T(8,128)(2,1)S(1)} %get-tuple-element.34.first_hbm) | copy-start | bytes 491524
  47.8 8.1 %collective-permute-start.2 = (bf16[4,5,32,128]{3,2,1,0:T(8,128)(2,1)S(1)}, bf16[4,5,32,128]{3,2,1,0:T(8,128)(2,1)S(1)}, u32[]{:S(2)}, u32[]{:S(2)}) collective-permute-start(bf16[4,5,32,128]{3,2,1,0:T(8,128)(2,1)S(1)} %get-tuple-element.34.first_hbm), channel_id=1, source_target_pairs={{64,0},{128,64},{192,128},{256,192},{320,256},{384,320},{448,384},... | collective-permute-start | bytes 491528 | tf_op jit(solution)/shard_map/ppermute | solution.py:601
  49.2 1.0 %copy-start.1 = (bf16[4,26,32,128]{3,2,1,0:T(8,128)(2,1)}, bf16[4,26,32,128]{3,2,1,0:T(8,128)(2,1)S(1)}, u32[]{:S(2)}) copy-start(bf16[4,26,32,128]{3,2,1,0:T(8,128)(2,1)S(1)} %collective-permute-done.3.other_hbm) | copy-start | bytes 2555908
  56.9 16.6 %all-to-all-start.2 = ((f32[64,4,128]{2,1,0:T(4,128)}), f32[64,4,128]{2,1,0:T(4,128)S(1)}, u32[]{:S(2)}, u32[]{:S(2)}) async-start(f32[64,4,128]{2,1,0:T(4,128)} %get-tuple-element.39), calls=%async_computation.2 | async-start | bytes 262144 | tf_op jit(solution)/shard_map/all_to_all | solution.py:556
  63.4 3.3 %collective-permute-start.4 = (bf16[4,5,32,128]{3,2,1,0:T(8,128)(2,1)S(1)}, bf16[4,5,32,128]{3,2,1,0:T(8,128)(2,1)S(1)}, u32[]{:S(2)}, u32[]{:S(2)}) collective-permute-start(bf16[4,5,32,128]{3,2,1,0:T(8,128)(2,1)S(1)} %get-tuple-element.40.incoming_ref), channel_id=1, source_target_pairs={{0,1},{1,0},{2,3},{3,2},{4,5},{5,4},{6,7},{7,6},{8,9},{9,8},{10,11... | collective-permute-start | bytes 491528 | tf_op jit(solution)/shard_map/ppermute | solution.py:618
  75.8 21.3 %all-to-all-start.3 = ((bf16[32,56,128]{2,1,0:T(8,128)(2,1)}), bf16[32,56,128]{2,1,0:T(8,128)(2,1)S(1)}, u32[]{:S(2)}, u32[]{:S(2)}) async-start(bf16[32,56,128]{2,1,0:T(8,128)(2,1)} %get-tuple-element.44), calls=%async_computation.3 | async-start | bytes 917504 | tf_op jit(solution)/shard_map/all_to_all | solution.py:635

commit v8 on v7

--- a/solution.py
+++ b/solution.py
@@ -460,8 +460,9 @@
     copy_own = pltpu.make_async_copy(columns_ref.at[0], own_hbm, sems.at[0])
     copy_own.start()
     second = row(params_ref, CORE) > 0.5
-    filler = jnp.zeros((out_ref.shape[1] - chunk, CH), F32)
-    chips = out_ref.shape[0]
+    chips = TAPS * CH // (2 * chunk)
+    padded = out_ref.shape[0] // chips
+    filler = [jnp.zeros((padded - chunk, CH), F32)] if padded > chunk else []
     done = 0
     copies = [copy_own]
     for kt in range(3):
@@ -470,15 +471,16 @@
             at = (n - 9 * kt) * CH
             sum_ref[n * CH : (n + 1) * CH] = first_ref[n].astype(F32) + terms[:, at : at + CH]
         begin = done
-        while done < chips and 2 * (done + 1) * chunk <= 9 * (kt + 1) * CH:
-            at = 2 * done * chunk
-            mine = jnp.where(second, sum_ref[at + chunk : at + 2 * chunk], sum_ref[at : at + chunk])
-            if filler.shape[0]:
-                mine = jnp.concatenate([mine, filler], axis=0)
-            out_ref[done] = mine.astype(BF16)
-            done += 1
+        while done < chips and 2 * (done + 2) * chunk <= 9 * (kt + 1) * CH:
+            pieces = []
+            for at in (2 * done * chunk, 2 * (done + 1) * chunk):
+                pieces.append(jnp.where(second, sum_ref[at + chunk : at + 2 * chunk], sum_ref[at : at + chunk]))
+                pieces += filler
+            out_ref[done * padded : (done + 2) * padded] = jnp.concatenate(pieces, axis=0).astype(BF16)
+            done += 2
         if done > begin:
-            send = pltpu.make_async_copy(out_ref.at[begin:done], out_hbm.at[begin:done], sems.at[1 + kt])
+            rows = slice(begin * padded, done * padded)
+            send = pltpu.make_async_copy(out_ref.at[rows], out_hbm.at[rows], sems.at[1 + kt])
             send.start()
             copies.append(send)
     for copy in copies:
@@ -624,14 +626,15 @@
     terms, columns, parts = call(
         functools.partial(weight_second_kernel, 1.0 / dp, chunk), "weight_second",
         (table, second_fields, params, stats, weight_first, acts),
-        (in_hbm((chips, padded, CH), BF16), in_hbm(columns_of(ROWS + 2), BF16), shape((2, CH))),
+        (in_hbm((chips * padded, CH), BF16), in_hbm(columns_of(ROWS + 2), BF16), shape((2, CH))),
         scratch=[
             both, pltpu.VMEM((TAPS * CH, CH), F32),
-            pltpu.VMEM((chips, padded, CH), BF16), sems(4),
+            pltpu.VMEM((chips * padded, CH), BF16), sems(4),
         ],
         specs="vkkkkk",
     )
     sides = [[2 * i + core for i in range(chips)] for core in range(2)]
+    terms = terms.reshape(chips, padded, CH)
     terms = lax.all_to_all(terms, "dp", 0, 0, axis_index_groups=sides, tiled=True)
     (grad_weight,) = call(
         functools.partial(total_kernel, 1.0 / dp), "total", (terms,), (shape((chunk, 1, CH)),)

time: 98.5 us -> 98.5 us (level)
  no operation moved by 1% of the time
where the time goes in v8:
time: 98.5 us; the launch traced here: 97.9 us
  starting transfers between devices  43.5 us (44%)
  waiting for transfers between devices  31.9 us (32%)
  Pallas kernels  20 us (20%)
  local copies, waits for them, and re-layouts  1.66 us (2%)
    all_to_all x3, starting transfers between devices, exchange(): return lax.all_to_all(table, 'dp', 0, 0, tiled=True)  28.8 us
    pallas_call x10, Pallas kernels, call(): pl.pallas_call(kernel, out_shape=tuple(outs), in_specs=[{'v': VMEM, 'k':...  20 us
    all_to_all x3, waiting for transfers between devices, exchange(): return lax.all_to_all(table, 'dp', 0, 0, tiled=True)  15 us
    all_to_all x1, waiting for transfers between devices, local(): lax.all_to_all(terms, 'dp', 0, 0, axis_index_groups=sides, tiled=True)  12.9 us
    all_to_all x1, starting transfers between devices, local(): lax.all_to_all(terms, 'dp', 0, 0, axis_index_groups=sides, tiled=True)  4.81 us
    ppermute x1, waiting for transfers between devices, local(): lax.ppermute(grad_first, 'segment', [(i + 1, i) for i in range(count - 1)])  2.7 us
    ppermute x1, starting transfers between devices, local(): outer = lax.ppermute(outer, 'dp', sides + [(j, i) for i, j in sides])  2.43 us
    ppermute x1, starting transfers between devices, local(): inner = lax.ppermute(inner, 'dp', mates)  2.06 us
  transfers between devices with their start and end apart: 9, of which 6 were waited for; matrix products, arithmetic and copies ran while one was open for 1% of the time, Pallas kernels for 14%

profile of v8, /device:TPU:8, one launch (start us, length us, event | category | flops | bytes accessed | tf_op | source)
XLA Modules:
  0.0 97.9 jit_solution(6978317698593800500)
XLA Ops:
  0.6 2.0 %sums.1 = (f32[64,4,128]{2,1,0:T(4,128)}, bf16[4,6,32,128]{3,2,1,0:T(8,128)(2,1)S(1)}, bf16[4,6,32,128]{3,2,1,0:T(8,128)(2,1)S(1)}, f32[2,4,4,32,128]{4,3,2,1,0:T(8,128)S(1)}, f32[80,128]{1,0:T(8,128)S(1)}) custom-call(s32[1]{0:T(128)} %bitcast.4.odd_ref, s32[1,2,1,4]{3,2,1,0:T(1,128)} %clip_hbm.1, bf16[2,4,4,32,128]{4,3,2,1,0:T(8,128)(2,1)} %bitcast.14, ...), custom_call_target="tpu_custom_call" | custom-call | flops 1000000 | bytes 525348 | tf_op jit(solution)/shard_map/sums/pallas_call | solution.py:512
  2.7 17.2 %all-to-all-start = ((f32[64,4,128]{2,1,0:T(4,128)}), f32[64,4,128]{2,1,0:T(4,128)S(1)}, u32[]{:S(2)}, u32[]{:S(2)}) async-start(f32[64,4,128]{2,1,0:T(4,128)} %get-tuple-element.28), calls=%async_computation | async-start | bytes 262144 | tf_op jit(solution)/shard_map/all_to_all | solution.py:558
  19.8 2.1 %collective-permute-start = (bf16[4,6,32,128]{3,2,1,0:T(8,128)(2,1)S(1)}, bf16[4,6,32,128]{3,2,1,0:T(8,128)(2,1)S(1)}, u32[]{:S(2)}, u32[]{:S(2)}) collective-permute-start(bf16[4,6,32,128]{3,2,1,0:T(8,128)(2,1)S(1)} %get-tuple-element.25), channel_id=1, source_target_pairs={{0,1},{1,0},{2,3},{3,2},{4,5},{5,4},{6,7},{7,6},{8,9},{9,8},{10,11... | collective-permute-start | bytes 589832 | tf_op jit(solution)/shard_map/ppermute | solution.py:572
  21.9 2.4 %collective-permute-start.1 = (bf16[4,6,32,128]{3,2,1,0:T(8,128)(2,1)S(1)}, bf16[4,6,32,128]{3,2,1,0:T(8,128)(2,1)S(1)}, u32[]{:S(2)}, u32[]{:S(2)}) collective-permute-start(bf16[4,6,32,128]{3,2,1,0:T(8,128)(2,1)S(1)} %get-tuple-element.26), channel_id=1, source_target_pairs={{1,2},{3,4},{5,6},{7,8},{9,10},{11,12},{13,14},{15,16},{17,18},{19... | collective-permute-start | bytes 589832 | tf_op jit(solution)/shard_map/ppermute | solution.py:574
  24.4 5.7 %all-to-all-done.table_ref = f32[64,4,128]{2,1,0:T(4,128)S(1)} async-done(((f32[64,4,128]{2,1,0:T(4,128)}), f32[64,4,128]{2,1,0:T(4,128)S(1)}, u32[]{:S(2)}, u32[]{:S(2)}) %all-to-all-start) | async-done | bytes 131104 | tf_op jit(solution)/shard_map/all_to_all | solution.py:558
  30.1 1.2 %act_first.1 = (f32[64,2,128]{2,1,0:T(2,128)}, f32[24,128]{1,0:T(8,128)S(1)}) custom-call(f32[64,4,128]{2,1,0:T(4,128)S(1)} %all-to-all-done.table_ref, f32[2,4,4,32,128]{4,3,2,1,0:T(8,128)S(1)} %get-tuple-element.29.own_ref, f32[80,128]{1,0:T(8,128)S(1)} %get-tuple-element.27.params_ref.plain_ref), custom_call_target="tpu_custom_call" | custom-call | flops 1000000 | bytes 696320 | tf_op jit(solution)/shard_map/act_first/pallas_call | solution.py:512
  31.3 5.1 %all-to-all-start.1 = ((f32[64,2,128]{2,1,0:T(2,128)}), f32[64,2,128]{2,1,0:T(2,128)S(1)}, u32[]{:S(2)}, u32[]{:S(2)}) async-start(f32[64,2,128]{2,1,0:T(2,128)} %get-tuple-element.32), calls=%async_computation.1 | async-start | bytes 131072 | tf_op jit(solution)/shard_map/all_to_all | solution.py:558
  36.4 0.1 stack.47.flag_ref
  36.5 0.0 collective-permute-done.inner_ref
  36.5 0.0 collective-permute-done.1.outer_ref
  36.5 2.7 %fields_first.1 = (f32[2,4,8,32,128]{4,3,2,1,0:T(8,128)S(1)}, bf16[4,26,32,128]{3,2,1,0:T(8,128)(2,1)}, bf16[4,5,32,128]{3,2,1,0:T(8,128)(2,1)S(1)}, f32[80,128]{1,0:T(8,128)S(1)}) custom-call(s32[6]{0:T(128)S(1)} %stack.47.flag_ref, bf16[4,6,32,128]{3,2,1,0:T(8,128)(2,1)S(1)} %collective-permute-done.inner_ref, ...), custom_call_target="tpu_custom_call" | custom-call | flops 1000000 | bytes 1232920 | tf_op jit(solution)/shard_map/fields_first/pallas_call | solution.py:512
  39.2 2.1 %collective-permute-start.3 = (bf16[4,26,32,128]{3,2,1,0:T(8,128)(2,1)}, bf16[4,26,32,128]{3,2,1,0:T(8,128)(2,1)S(1)}, u32[]{:S(2)}, u32[]{:S(2)}) collective-permute-start(bf16[4,26,32,128]{3,2,1,0:T(8,128)(2,1)} %get-tuple-element.37.bundle_hbm), channel_id=1, source_target_pairs={{0,1},{1,0},{2,3},{3,2},{4,5},{5,4},{6,7},{7,6},{8,9},{9,8},{10,11... | collective-permute-start | bytes 2555912 | tf_op jit(solution)/shard_map/ppermute | solution.py:590
  41.3 4.0 %all-to-all-done.1.table_ref = f32[64,2,128]{2,1,0:T(2,128)S(1)} async-done(((f32[64,2,128]{2,1,0:T(2,128)}), f32[64,2,128]{2,1,0:T(2,128)S(1)}, u32[]{:S(2)}, u32[]{:S(2)}) %all-to-all-start.1) | async-done | bytes 65568 | tf_op jit(solution)/shard_map/all_to_all | solution.py:558
  45.3 2.5 %conv_first.1 = (bf16[4,5,32,128]{3,2,1,0:T(8,128)(2,1)S(1)}, bf16[4,6,32,128]{3,2,1,0:T(8,128)(2,1)}) custom-call(f32[64,2,128]{2,1,0:T(2,128)S(1)} %all-to-all-done.1.table_ref, f32[2,4,8,32,128]{4,3,2,1,0:T(8,128)S(1)} %get-tuple-element.33.fields_ref, f32[80,128]{1,0:T(8,128)S(1)} %get-tuple-element.31.params_ref, ...), custom_call_target="tpu_custom_call" | custom-call | flops 20000000000 | bytes 2052096 | tf_op jit(solution)/shard_map/conv_first/pallas_call | solution.py:512
  47.8 0.0 copy-start
  47.8 1.3 %collective-permute-start.2 = (bf16[4,5,32,128]{3,2,1,0:T(8,128)(2,1)S(1)}, bf16[4,5,32,128]{3,2,1,0:T(8,128)(2,1)S(1)}, u32[]{:S(2)}, u32[]{:S(2)}) collective-permute-start(bf16[4,5,32,128]{3,2,1,0:T(8,128)(2,1)S(1)} %get-tuple-element.34.first_hbm), channel_id=1, source_target_pairs={{64,0},{128,64},{192,128},{256,192},{320,256},{384,320},{448,384},... | collective-permute-start | bytes 491528 | tf_op jit(solution)/shard_map/ppermute | solution.py:603
  49.1 0.0 collective-permute-done.3.other_hbm
  49.2 0.0 copy-start.1
  49.2 1.0 copy-done.1
  50.1 3.1 %weight_first.1 = (f32[2,4,4,32,128]{4,3,2,1,0:T(8,128)S(1)}, bf16[128,2304]{1,0:T(8,128)(2,1)S(1)}, bf16[27,128,128]{2,1,0:T(8,128)(2,1)S(1)}) custom-call(f32[64,2,128]{2,1,0:T(2,128)S(1)} %all-to-all-done.1.table_ref, f32[80,128]{1,0:T(8,128)S(1)} %get-tuple-element.31.params_ref, f32[24,128]{1,0:T(8,128)S(1)} %get-tuple-element.30.stats_ref, ...), custom_call_target="tpu_custom_call" | custom-call | flops 1000000 | bytes 2019328 | tf_op jit(solution)/shard_map/weight_first/pallas_call | solution.py:512
  53.3 2.7 %collective-permute-done.2.hand_ref = bf16[4,5,32,128]{3,2,1,0:T(8,128)(2,1)S(1)} collective-permute-done((bf16[4,5,32,128]{3,2,1,0:T(8,128)(2,1)S(1)}, bf16[4,5,32,128]{3,2,1,0:T(8,128)(2,1)S(1)}, u32[]{:S(2)}, u32[]{:S(2)}) %collective-permute-start.2) | collective-permute-done | bytes 163872 | tf_op jit(solution)/shard_map/ppermute | solution.py:603
  56.0 0.9 act_second.1
  56.9 0.0 copy-done
  56.9 6.5 %all-to-all-start.2 = ((f32[64,4,128]{2,1,0:T(4,128)}), f32[64,4,128]{2,1,0:T(4,128)S(1)}, u32[]{:S(2)}, u32[]{:S(2)}) async-start(f32[64,4,128]{2,1,0:T(4,128)} %get-tuple-element.39), calls=%async_computation.2 | async-start | bytes 262144 | tf_op jit(solution)/shard_map/all_to_all | solution.py:558
  63.4 2.1 %collective-permute-start.4 = (bf16[4,5,32,128]{3,2,1,0:T(8,128)(2,1)S(1)}, bf16[4,5,32,128]{3,2,1,0:T(8,128)(2,1)S(1)}, u32[]{:S(2)}, u32[]{:S(2)}) collective-permute-start(bf16[4,5,32,128]{3,2,1,0:T(8,128)(2,1)S(1)} %get-tuple-element.40.incoming_ref), channel_id=1, source_target_pairs={{0,1},{1,0},{2,3},{3,2},{4,5},{5,4},{6,7},{7,6},{8,9},{9,8},{10,11... | collective-permute-start | bytes 491528 | tf_op jit(solution)/shard_map/ppermute | solution.py:620
  65.5 1.2 %collective-permute-done.4.arrived_ref = bf16[4,5,32,128]{3,2,1,0:T(8,128)(2,1)S(1)} collective-permute-done((bf16[4,5,32,128]{3,2,1,0:T(8,128)(2,1)S(1)}, bf16[4,5,32,128]{3,2,1,0:T(8,128)(2,1)S(1)}, u32[]{:S(2)}, u32[]{:S(2)}) %collective-permute-start.4) | collective-permute-done | bytes 163872 | tf_op jit(solution)/shard_map/ppermute | solution.py:620
  66.7 1.5 %fields_second.1.fields_ref = f32[2,2,4,6,32,128]{5,4,3,2,1,0:T(8,128)S(1)} custom-call(bf16[4,5,32,128]{3,2,1,0:T(8,128)(2,1)S(1)} %get-tuple-element.40.incoming_ref, bf16[4,5,32,128]{3,2,1,0:T(8,128)(2,1)S(1)} %collective-permute-done.4.arrived_ref, bf16[4,26,32,128]{3,2,1,0:T(8,128)(2,1)} %get-tuple-element.37.bundle_hbm, ...), custom_call_target="tpu_custom_call" | custom-call | flops 1000000 | bytes 2084864 | tf_op jit(solution)/shard_map/fields_second/pallas_call | solution.py:512
  68.2 5.3 %all-to-all-done.2.table_ref = f32[64,4,128]{2,1,0:T(4,128)S(1)} async-done(((f32[64,4,128]{2,1,0:T(4,128)}), f32[64,4,128]{2,1,0:T(4,128)S(1)}, u32[]{:S(2)}, u32[]{:S(2)}) %all-to-all-start.2) | async-done | bytes 131104 | tf_op jit(solution)/shard_map/all_to_all | solution.py:558
  73.5 2.3 %weight_second.1 = (bf16[1792,128]{1,0:T(8,128)(2,1)}, bf16[4,192,384]{2,1,0:T(8,128)(2,1)}, f32[2,128]{1,0:T(2,128)S(1)}) custom-call(f32[64,4,128]{2,1,0:T(4,128)S(1)} %all-to-all-done.2.table_ref, f32[2,2,4,6,32,128]{5,4,3,2,1,0:T(8,128)S(1)} %fields_second.1.fields_ref, f32[80,128]{1,0:T(8,128)S(1)} %get-tuple-element.31.params_ref, ...), custom_call_target="tpu_custom_call" | custom-call | flops 1000000 | bytes 3231744 | tf_op jit(solution)/shard_map/weight_second/pallas_call | solution.py:512
  75.8 4.8 %all-to-all-start.3 = ((bf16[32,56,128]{2,1,0:T(8,128)(2,1)}), bf16[32,56,128]{2,1,0:T(8,128)(2,1)S(1)}, u32[]{:S(2)}, u32[]{:S(2)}) async-start(bf16[32,56,128]{2,1,0:T(8,128)(2,1)} %bitcast.22), calls=%async_computation.3 | async-start | bytes 917504 | tf_op jit(solution)/shard_map/all_to_all | solution.py:638
  80.6 3.0 %conv_second.1 = bf16[2,4,4,32,128]{4,3,2,1,0:T(8,128)(2,1)} custom-call(f32[80,128]{1,0:T(8,128)S(1)} %get-tuple-element.31.params_ref, bf16[4,192,384]{2,1,0:T(8,128)(2,1)} %get-tuple-element.43.columns_hbm, bf16[4,5,32,128]{3,2,1,0:T(8,128)(2,1)} %copy-done, bf16[3,9,128,128]{3,2,1,0:T(8,128)(2,1)} %bitcast.17), custom_call_target="tpu_custom_call" | custom-call | flops 1000000 | bytes 1679360 | tf_op jit(solution)/shard_map/conv_second/pallas_call | solution.py:512
  83.7 0.1 constant_dynamic-slice_fusion
  83.8 0.5 fusion
  84.3 12.9 %all-to-all-done.3.terms_ref = bf16[32,56,128]{2,1,0:T(8,128)(2,1)S(1)} async-done(((bf16[32,56,128]{2,1,0:T(8,128)(2,1)}), bf16[32,56,128]{2,1,0:T(8,128)(2,1)S(1)}, u32[]{:S(2)}, u32[]{:S(2)}) %all-to-all-start.3) | async-done | bytes 458784 | tf_op jit(solution)/shard_map/all_to_all | solution.py:638
  97.2 0.7 total.1
Async XLA Ops:
  2.7 27.4 %all-to-all-start = ((f32[64,4,128]{2,1,0:T(4,128)}), f32[64,4,128]{2,1,0:T(4,128)S(1)}, u32[]{:S(2)}, u32[]{:S(2)}) async-start(f32[64,4,128]{2,1,0:T(4,128)} %get-tuple-element.28), calls=%async_computation | async-start | bytes 262144 | tf_op jit(solution)/shard_map/all_to_all | solution.py:558
  19.8 16.6 %collective-permute-start = (bf16[4,6,32,128]{3,2,1,0:T(8,128)(2,1)S(1)}, bf16[4,6,32,128]{3,2,1,0:T(8,128)(2,1)S(1)}, u32[]{:S(2)}, u32[]{:S(2)}) collective-permute-start(bf16[4,6,32,128]{3,2,1,0:T(8,128)(2,1)S(1)} %get-tuple-element.25), channel_id=1, source_target_pairs={{0,1},{1,0},{2,3},{3,2},{4,5},{5,4},{6,7},{7,6},{8,9},{9,8},{10,11... | collective-permute-start | bytes 589832 | tf_op jit(solution)/shard_map/ppermute | solution.py:572
  21.9 14.6 %collective-permute-start.1 = (bf16[4,6,32,128]{3,2,1,0:T(8,128)(2,1)S(1)}, bf16[4,6,32,128]{3,2,1,0:T(8,128)(2,1)S(1)}, u32[]{:S(2)}, u32[]{:S(2)}) collective-permute-start(bf16[4,6,32,128]{3,2,1,0:T(8,128)(2,1)S(1)} %get-tuple-element.26), channel_id=1, source_target_pairs={{1,2},{3,4},{5,6},{7,8},{9,10},{11,12},{13,14},{15,16},{17,18},{19... | collective-permute-start | bytes 589832 | tf_op jit(solution)/shard_map/ppermute | solution.py:574
  31.3 14.1 %all-to-all-start.1 = ((f32[64,2,128]{2,1,0:T(2,128)}), f32[64,2,128]{2,1,0:T(2,128)S(1)}, u32[]{:S(2)}, u32[]{:S(2)}) async-start(f32[64,2,128]{2,1,0:T(2,128)} %get-tuple-element.32), calls=%async_computation.1 | async-start | bytes 131072 | tf_op jit(solution)/shard_map/all_to_all | solution.py:558
  39.2 9.9 %collective-permute-start.3 = (bf16[4,26,32,128]{3,2,1,0:T(8,128)(2,1)}, bf16[4,26,32,128]{3,2,1,0:T(8,128)(2,1)S(1)}, u32[]{:S(2)}, u32[]{:S(2)}) collective-permute-start(bf16[4,26,32,128]{3,2,1,0:T(8,128)(2,1)} %get-tuple-element.37.bundle_hbm), channel_id=1, source_target_pairs={{0,1},{1,0},{2,3},{3,2},{4,5},{5,4},{6,7},{7,6},{8,9},{9,8},{10,11... | collective-permute-start | bytes 2555912 | tf_op jit(solution)/shard_map/ppermute | solution.py:590
  47.8 9.1 %copy-start = (bf16[4,5,32,128]{3,2,1,0:T(8,128)(2,1)}, bf16[4,5,32,128]{3,2,1,0:T(8,128)(2,1)S(1)}, u32[]{:S(2)}) copy-start(bf16[4,5,32,128]{3,2,1,0:T(8,128)(2,1)S(1)} %get-tuple-element.34.first_hbm) | copy-start | bytes 491524
  47.8 8.1 %collective-permute-start.2 = (bf16[4,5,32,128]{3,2,1,0:T(8,128)(2,1)S(1)}, bf16[4,5,32,128]{3,2,1,0:T(8,128)(2,1)S(1)}, u32[]{:S(2)}, u32[]{:S(2)}) collective-permute-start(bf16[4,5,32,128]{3,2,1,0:T(8,128)(2,1)S(1)} %get-tuple-element.34.first_hbm), channel_id=1, source_target_pairs={{64,0},{128,64},{192,128},{256,192},{320,256},{384,320},{448,384},... | collective-permute-start | bytes 491528 | tf_op jit(solution)/shard_map/ppermute | solution.py:603
  49.2 1.0 %copy-start.1 = (bf16[4,26,32,128]{3,2,1,0:T(8,128)(2,1)}, bf16[4,26,32,128]{3,2,1,0:T(8,128)(2,1)S(1)}, u32[]{:S(2)}) copy-start(bf16[4,26,32,128]{3,2,1,0:T(8,128)(2,1)S(1)} %collective-permute-done.3.other_hbm) | copy-start | bytes 2555908
  56.9 16.6 %all-to-all-start.2 = ((f32[64,4,128]{2,1,0:T(4,128)}), f32[64,4,128]{2,1,0:T(4,128)S(1)}, u32[]{:S(2)}, u32[]{:S(2)}) async-start(f32[64,4,128]{2,1,0:T(4,128)} %get-tuple-element.39), calls=%async_computation.2 | async-start | bytes 262144 | tf_op jit(solution)/shard_map/all_to_all | solution.py:558
  63.4 3.3 %collective-permute-start.4 = (bf16[4,5,32,128]{3,2,1,0:T(8,128)(2,1)S(1)}, bf16[4,5,32,128]{3,2,1,0:T(8,128)(2,1)S(1)}, u32[]{:S(2)}, u32[]{:S(2)}) collective-permute-start(bf16[4,5,32,128]{3,2,1,0:T(8,128)(2,1)S(1)} %get-tuple-element.40.incoming_ref), channel_id=1, source_target_pairs={{0,1},{1,0},{2,3},{3,2},{4,5},{5,4},{6,7},{7,6},{8,9},{9,8},{10,11... | collective-permute-start | bytes 491528 | tf_op jit(solution)/shard_map/ppermute | solution.py:620
  75.8 21.3 %all-to-all-start.3 = ((bf16[32,56,128]{2,1,0:T(8,128)(2,1)}), bf16[32,56,128]{2,1,0:T(8,128)(2,1)S(1)}, u32[]{:S(2)}, u32[]{:S(2)}) async-start(bf16[32,56,128]{2,1,0:T(8,128)(2,1)} %bitcast.22), calls=%async_computation.3 | async-start | bytes 917504 | tf_op jit(solution)/shard_map/all_to_all | solution.py:638
